TPU v7x, 32 devices: a whole 2x2x4 slice. The times are simulated.
32 devices in a mesh: grp: 2 (over y), gx: 8 (over z, x), gy: 2 (over core).
Axes of the slice: x: 2, y: 2, z: 4, core: 2. Of those that a mesh axis runs over, the one named last changes fastest.
Arguments:
- misfit: float32 [2, 256, 1536], P(None, ('grp', 'gx'), 'gy'), parts along dimension 1
- velocity: float32 [2, 256, 1536], P(None, ('grp', 'gx'), 'gy'), parts along dimension 1
- viscosity: float32 [256, 1536], P(('grp', 'gx'), 'gy'), parts along dimension 0, may hold values from 0.2 to 2
- friction: float32 [256, 1536], P(('grp', 'gx'), 'gy'), parts along dimension 0, may hold values from 0.2 to 4
- ice: int32 [256, 1536], P(('grp', 'gx'), 'gy'), parts along dimension 0, may hold values 0 or 1
- grounded: int32 [256, 1536], P(('grp', 'gx'), 'gy'), parts along dimension 0, may hold values 0 or 1
- bounds: float32 [8], P('grp'), parts along dimension 0, may hold values from 2.1 to 32, as said below
Outputs:
- multiplier: float32 [2, 256, 1536], P(None, ('grp', 'gx'), 'gy'), parts along dimension 1
- scaled_gradient: float32 [256, 1536], P(('grp', 'gx'), 'gy'), parts along dimension 0
- residual_norm: float32 [2], P('grp'), parts along dimension 0
There are 2 independent parts, one for each index of `grp`. A program takes and returns all parts, laid end to end along the dimension named above; each array names one. Nothing has to cross between parts.
Inputs may be any that keep to these rules, and one draw needn't show every extreme that they name: bounds holds a lower and an upper bound for the fine grid, then for the coarse grid; each lower bound is under its upper bound.
All inputs are finite; a program needn't handle non-finite values. No bound on the sum of `ice` or of `grounded` on one device may be relied on, other than what follows from the above.
Results may differ from a plain program's by a relative error of at most 0.0003.
Values sent between devices are 32-bit elements; how exact they have to be, the bound alone decides.
No kernel may reach another device: no remote copies, remote signals or barrier semaphores. Data moves between devices by JAX's collectives and lax.ppermute only.
A program may use at most 64 MiB of HBM per device.

v0:
```python
import jax
import jax.numpy as jnp
from jax import lax
from jax.sharding import PartitionSpec as P

DEG = 4


def extended(array, sides, width):
    for axis, dim in sides:
        size, length = (lax.axis_size(axis), array.shape[dim])
        up = [(i, (i + 1) % size) for i in range(size - 1)]
        down = [(j, i) for i, j in up]
        last = lax.slice_in_dim(array, length - width, length, axis=dim)
        first = lax.slice_in_dim(array, 0, width, axis=dim)
        before = lax.ppermute(last, axis, up)
        after = lax.ppermute(first, axis, down)
        array = jnp.concatenate([before, array, after], axis=dim)
    return array


def apply_stencil(bordered, border_visc, beta):
    stiffness = 0.25 * (
        border_visc[:-1, :-1] + border_visc[1:, :-1] + border_visc[:-1, 1:] + border_visc[1:, 1:]
    )
    low_low = bordered[:, :-1, :-1]
    high_low = bordered[:, 1:, :-1]
    low_high = bordered[:, :-1, 1:]
    high_high = bordered[:, 1:, 1:]
    along_x = 0.5 * (high_low + high_high - low_low - low_high)
    along_y = 0.5 * (low_high + high_high - low_low - high_low)
    normal_x = stiffness * (4.0 * along_x[0] + 2.0 * along_y[1])
    normal_y = stiffness * (4.0 * along_y[1] + 2.0 * along_x[0])
    shear_term = stiffness * (along_y[0] + along_x[1])
    force_x = jnp.stack([normal_x, shear_term])
    force_y = jnp.stack([shear_term, normal_y])
    corner_a = -0.5 * (force_x + force_y)
    corner_b = 0.5 * (force_x - force_y)
    corner_c = 0.5 * (force_y - force_x)
    corner_d = 0.5 * (force_x + force_y)
    centre = bordered[:, 1:-1, 1:-1]
    total = (
        corner_a[:, 1:, 1:] + corner_b[:, :-1, 1:] + corner_c[:, 1:, :-1] + corner_d[:, :-1, :-1]
    )
    return total + beta * centre


def chebyshev(source, operator, lower, upper, inside, final):
    middle = 0.5 * (upper + lower)
    half_width = 0.5 * (upper - lower)
    spread = middle / half_width
    factor = 1.0 / spread
    update = source / middle * inside
    iterate = update
    for step in range(DEG - 1):
        remaining = source - operator(iterate)
        factor_next = 1.0 / (2.0 * spread - factor)
        update = (
            factor_next * factor * update + 2.0 * factor_next / half_width * remaining
        ) * inside
        iterate = iterate + update
        factor = factor_next
    if final:
        return (iterate, source - operator(iterate))
    return (iterate, iterate)


def fine_border(field):
    return extended(field, (("gx", 1), ("gy", 2)), 1)


def coarse_border(field):
    return extended(field, (("gx", 1), ("gy", 2)), 1)


def cached_apply(border_fn, visc, beta):
    cached = {}

    def apply_now(iterate):
        if "visc" in cached:
            bordered = border_fn(iterate)
        else:
            joined = border_fn(jnp.concatenate([iterate, visc[None]], axis=0))
            cached["visc"] = joined[2]
            bordered = joined[:2]
        return apply_stencil(bordered, cached["visc"], beta)

    return apply_now


def body(misfit, velocity, viscosity, friction, ice, grounded, bounds):
    tile_rows, tile_cols = viscosity.shape
    visc_eff = viscosity * ice.astype(jnp.float32)
    beta_eff = friction * grounded.astype(jnp.float32)
    fine_apply = cached_apply(fine_border, visc_eff, beta_eff)
    fine_x, residual = chebyshev(misfit, fine_apply, bounds[0], bounds[1], 1.0, True)
    half_rows = tile_rows // 2
    half_cols = tile_cols // 2
    residual_part = jnp.sum(residual * residual)
    residual_total = lax.psum(residual_part, ("gx", "gy"))
    coarse_source = residual.reshape(2, half_rows, 2, half_cols, 2).sum(axis=(2, 4))
    coarse_visc = 0.25 * visc_eff.reshape(half_rows, 2, half_cols, 2).sum(axis=(1, 3))
    coarse_beta = beta_eff.reshape(half_rows, 2, half_cols, 2).sum(axis=(1, 3))
    coarse_apply = cached_apply(coarse_border, coarse_visc, coarse_beta)
    correction, unused = chebyshev(coarse_source, coarse_apply, bounds[2], bounds[3], 1.0, False)
    multiplier = fine_x + jnp.repeat(jnp.repeat(correction, 2, axis=1), 2, axis=2)
    gradient = -beta_eff * jnp.sum(velocity * multiplier, axis=0)
    gradient_part = jnp.sum(gradient * gradient)
    gradient_total = lax.psum(gradient_part, ("gx", "gy"))
    node_count = tile_rows * tile_cols * lax.axis_size("gx") * lax.axis_size("gy")
    grad_scale = jnp.sqrt(gradient_total / node_count + 1e-06)
    norm_value = jnp.sqrt(residual_total / (2 * node_count)).reshape(1)
    return (multiplier, gradient / grad_scale, norm_value)


def solution(mesh):
    placed = (
        P(None, ("grp", "gx"), "gy"),
        P(None, ("grp", "gx"), "gy"),
        P(("grp", "gx"), "gy"),
        P(("grp", "gx"), "gy"),
        P(("grp", "gx"), "gy"),
        P(("grp", "gx"), "gy"),
        P("grp"),
    )
    return jax.shard_map(
        body,
        mesh=mesh,
        in_specs=placed,
        out_specs=(P(None, ("grp", "gx"), "gy"), P(("grp", "gx"), "gy"), P("grp")),
        check_vma=False,
    )
```

profile of v0, /device:TPU:0, one launch (start us, length us, event | category | flops | bytes accessed | tf_op | source)
XLA Modules:
  0.0 179.1 jit_solution(18010656218009652186)
XLA Ops:
  5.1 4.8 %collective-permute-start = (f32[3,1,768]{2,1,0:T(1,128)S(1)}, f32[3,1,768]{2,1,0:T(1,128)S(1)}, u32[]{:S(2)}, u32[]{:S(2)}) collective-permute-start(f32[3,1,768]{2,1,0:T(1,128)S(1)} %get-tuple-element.69), channel_id=1, source_target_pairs={{0,2},{2,4},{4,6},{6,8},{8,10},{10,12},{12,14},{1,3},{3,5},{5,7},{... | collective-permute-start | bytes 27656 | tf_op jit(solution)/shard_map/ppermute | solution.py:16
  13.7 1.8 %collective-permute-done.1 = f32[3,1,768]{2,1,0:T(1,128)S(1)} collective-permute-done((f32[3,1,768]{2,1,0:T(1,128)S(1)}, f32[3,1,768]{2,1,0:T(1,128)S(1)}, u32[]{:S(2)}, u32[]{:S(2)}) %collective-permute-start.1) | collective-permute-done | bytes 9248 | tf_op jit(solution)/shard_map/ppermute | solution.py:17
  20.8 4.4 %collective-permute-start.4 = (f32[2,1,768]{2,0,1:T(2,128)S(1)}, f32[2,1,768]{2,0,1:T(2,128)S(1)}, u32[]{:S(2)}, u32[]{:S(2)}) collective-permute-start(f32[2,1,768]{2,0,1:T(2,128)S(1)} %copy.206), channel_id=1, source_target_pairs={{0,2},{2,4},{4,6},{6,8},{8,10},{10,12},{12,14},{1,3},{3,5},{5,7},{... | collective-permute-start | bytes 18440 | tf_op jit(solution)/shard_map/ppermute | solution.py:16
  26.7 4.1 %collective-permute-done.5 = f32[2,1,768]{2,0,1:T(2,128)S(1)} collective-permute-done((f32[2,1,768]{2,0,1:T(2,128)S(1)}, f32[2,1,768]{2,0,1:T(2,128)S(1)}, u32[]{:S(2)}, u32[]{:S(2)}) %collective-permute-start.5) | collective-permute-done | bytes 6176 | tf_op jit(solution)/shard_map/ppermute | solution.py:17
  32.2 3.0 %collective-permute-start.6 = (f32[2,18,1]{2,0,1:T(2,128)S(1)}, f32[2,18,1]{2,0,1:T(2,128)S(1)}, u32[]{:S(2)}, u32[]{:S(2)}) collective-permute-start(f32[2,18,1]{2,0,1:T(2,128)S(1)} %get-tuple-element.98), channel_id=1, source_target_pairs={{0,1},{2,3},{4,5},{6,7},{8,9},{10,11},{12,13},{14,15},{16,17},{18,... | collective-permute-start | bytes 440 | tf_op jit(solution)/shard_map/ppermute | solution.py:16
  38.0 4.3 %collective-permute-start.8 = (f32[2,1,768]{2,0,1:T(2,128)S(1)}, f32[2,1,768]{2,0,1:T(2,128)}, u32[]{:S(2)}, u32[]{:S(2)}) collective-permute-start(f32[2,1,768]{2,0,1:T(2,128)S(1)} %copy.213), channel_id=1, source_target_pairs={{0,2},{2,4},{4,6},{6,8},{8,10},{10,12},{12,14},{1,3},{3,5},{5,7},{... | collective-permute-start | bytes 18440 | tf_op jit(solution)/shard_map/ppermute | solution.py:16
  42.3 4.0 %reshape.125 = f32[8,2,384,2]{3,2,1,0:T(8,128)S(1)} reshape(f32[16,768]{1,0:T(8,128)} %copy-done.4) | data formatting | bytes 98304 | tf_op jit(solution)/shard_map/reshape | solution.py:102
  49.3 2.5 %collective-permute-done.9 = f32[2,1,768]{2,0,1:T(2,128)S(1)} collective-permute-done((f32[2,1,768]{2,0,1:T(2,128)S(1)}, f32[2,1,768]{2,0,1:T(2,128)S(1)}, u32[]{:S(2)}, u32[]{:S(2)}) %collective-permute-start.9) | collective-permute-done | bytes 6176 | tf_op jit(solution)/shard_map/ppermute | solution.py:17
  53.2 1.9 %collective-permute-start.10 = (f32[2,18,1]{2,0,1:T(2,128)}, f32[2,18,1]{2,0,1:T(2,128)}, u32[]{:S(2)}, u32[]{:S(2)}) collective-permute-start(f32[2,18,1]{2,0,1:T(2,128)} %get-tuple-element.93), channel_id=1, source_target_pairs={{0,1},{2,3},{4,5},{6,7},{8,9},{10,11},{12,13},{14,15},{16,17},{18,... | collective-permute-start | bytes 440 | tf_op jit(solution)/shard_map/ppermute | solution.py:16
  62.2 3.5 %collective-permute-start.12 = (f32[2,1,768]{2,0,1:T(2,128)S(1)}, f32[2,1,768]{2,0,1:T(2,128)S(1)}, u32[]{:S(2)}, u32[]{:S(2)}) collective-permute-start(f32[2,1,768]{2,0,1:T(2,128)S(1)} %copy.220), channel_id=1, source_target_pairs={{0,2},{2,4},{4,6},{6,8},{8,10},{10,12},{12,14},{1,3},{3,5},{5,7},{... | collective-permute-start | bytes 18440 | tf_op jit(solution)/shard_map/ppermute | solution.py:16
  68.4 4.1 %collective-permute-done.13 = f32[2,1,768]{2,0,1:T(2,128)S(1)} collective-permute-done((f32[2,1,768]{2,0,1:T(2,128)S(1)}, f32[2,1,768]{2,0,1:T(2,128)S(1)}, u32[]{:S(2)}, u32[]{:S(2)}) %collective-permute-start.13) | collective-permute-done | bytes 6176 | tf_op jit(solution)/shard_map/ppermute | solution.py:17
  73.9 3.0 %collective-permute-start.14 = (f32[2,18,1]{2,0,1:T(2,128)S(1)}, f32[2,18,1]{2,0,1:T(2,128)S(1)}, u32[]{:S(2)}, u32[]{:S(2)}) collective-permute-start(f32[2,18,1]{2,0,1:T(2,128)S(1)} %get-tuple-element.90), channel_id=1, source_target_pairs={{0,1},{2,3},{4,5},{6,7},{8,9},{10,11},{12,13},{14,15},{16,17},{18,... | collective-permute-start | bytes 440 | tf_op jit(solution)/shard_map/ppermute | solution.py:16
  79.1 8.0 %reshape.124 = f32[2,8,2,384,2]{4,3,2,1,0:T(8,128)} reshape(f32[2,16,768]{2,1,0:T(8,128)S(1)} %get-tuple-element.21) | data formatting | bytes 196608 | tf_op jit(solution)/shard_map/reshape | solution.py:101
  87.1 3.7 %reduce_sum.54 = f32[2,8,384]{2,1,0:T(8,128)S(1)} reduce(f32[2,8,2,384,2]{4,3,2,1,0:T(8,128)} %reshape.124, f32[]{:T(128)} %constant.6.clone.1), dimensions={2,4}, to_apply=%region_0.0 | reduce | flops 18432 | bytes 122884 | tf_op jit(solution)/shard_map/reduce_sum | solution.py:101
  92.0 4.2 %collective-permute-start.16 = (f32[3,1,384]{2,1,0:T(1,128)}, f32[3,1,384]{2,1,0:T(1,128)}, u32[]{:S(2)}, u32[]{:S(2)}) collective-permute-start(f32[3,1,384]{2,1,0:T(1,128)} %get-tuple-element.109), channel_id=1, source_target_pairs={{0,2},{2,4},{4,6},{6,8},{8,10},{10,12},{12,14},{1,3},{3,5},{5,7},{... | collective-permute-start | bytes 13832 | tf_op jit(solution)/shard_map/ppermute | solution.py:16
  98.9 4.0 %reshape.126 = f32[8,2,384,2]{3,2,1,0:T(8,128)S(1)} reshape(f32[16,768]{1,0:T(8,128)} %copy-done.5) | data formatting | bytes 98304 | tf_op jit(solution)/shard_map/reshape | solution.py:103
  104.4 2.6 %collective-permute-start.18 = (f32[3,10,1]{2,1,0:T(8,128)}, f32[3,10,1]{2,1,0:T(8,128)}, u32[]{:S(2)}, u32[]{:S(2)}) collective-permute-start(f32[3,10,1]{2,1,0:T(8,128)} %get-tuple-element.107), channel_id=1, source_target_pairs={{0,1},{2,3},{4,5},{6,7},{8,9},{10,11},{12,13},{14,15},{16,17},{18,... | collective-permute-start | bytes 368 | tf_op jit(solution)/shard_map/ppermute | solution.py:16
  113.2 4.3 %collective-permute-start.20 = (f32[2,1,384]{2,1,0:T(1,128)S(1)}, f32[2,1,384]{2,1,0:T(1,128)S(1)}, u32[]{:S(2)}, u32[]{:S(2)}) collective-permute-start(f32[2,1,384]{2,1,0:T(1,128)S(1)} %get-tuple-element.121), channel_id=1, source_target_pairs={{0,2},{2,4},{4,6},{6,8},{8,10},{10,12},{12,14},{1,3},{3,5},{5,7},{... | collective-permute-start | bytes 9224 | tf_op jit(solution)/shard_map/ppermute | solution.py:16
  118.9 4.1 %collective-permute-done.21 = f32[2,1,384]{2,1,0:T(1,128)S(1)} collective-permute-done((f32[2,1,384]{2,1,0:T(1,128)S(1)}, f32[2,1,384]{2,1,0:T(1,128)S(1)}, u32[]{:S(2)}, u32[]{:S(2)}) %collective-permute-start.21) | collective-permute-done | bytes 3104 | tf_op jit(solution)/shard_map/ppermute | solution.py:17
  125.7 1.8 collective-permute-done.23
  128.5 4.4 %collective-permute-start.24 = (f32[2,1,384]{2,1,0:T(1,128)S(1)}, f32[2,1,384]{2,1,0:T(1,128)S(1)}, u32[]{:S(2)}, u32[]{:S(2)}) collective-permute-start(f32[2,1,384]{2,1,0:T(1,128)S(1)} %get-tuple-element.119), channel_id=1, source_target_pairs={{0,2},{2,4},{4,6},{6,8},{8,10},{10,12},{12,14},{1,3},{3,5},{5,7},{... | collective-permute-start | bytes 9224 | tf_op jit(solution)/shard_map/ppermute | solution.py:16
  134.3 4.1 %collective-permute-done.25 = f32[2,1,384]{2,1,0:T(1,128)S(1)} collective-permute-done((f32[2,1,384]{2,1,0:T(1,128)S(1)}, f32[2,1,384]{2,1,0:T(1,128)S(1)}, u32[]{:S(2)}, u32[]{:S(2)}) %collective-permute-start.25) | collective-permute-done | bytes 3104 | tf_op jit(solution)/shard_map/ppermute | solution.py:17
  141.1 1.8 collective-permute-done.27
  145.5 30.3 %all-reduce = (f32[]{:T(128)}, f32[]{:T(128)}) all-reduce(f32[]{:T(128)} %multiply_reduce_fusion, f32[]{:T(128)} %get-tuple-element.20), channel_id=1, replica_groups=mesh['grp'=2,'gx'=8,'gy'=2] {'gx','gy'}, use_global_device_ids=true, to_apply=%region_5.0 | all-reduce | flops 2 | bytes 16 | tf_op jit(solution)/shard_map/psum | solution.py:109
  (161 shorter events, 54.6 us)
Async XLA Ops:
  5.1 8.6 %collective-permute-start = (f32[3,1,768]{2,1,0:T(1,128)S(1)}, f32[3,1,768]{2,1,0:T(1,128)S(1)}, u32[]{:S(2)}, u32[]{:S(2)}) collective-permute-start(f32[3,1,768]{2,1,0:T(1,128)S(1)} %get-tuple-element.69), channel_id=1, source_target_pairs={{0,2},{2,4},{4,6},{6,8},{8,10},{10,12},{12,14},{1,3},{3,5},{5,7},{... | collective-permute-start | bytes 27656 | tf_op jit(solution)/shard_map/ppermute | solution.py:16
  10.0 5.6 %collective-permute-start.1 = (f32[3,1,768]{2,1,0:T(1,128)S(1)}, f32[3,1,768]{2,1,0:T(1,128)S(1)}, u32[]{:S(2)}, u32[]{:S(2)}) collective-permute-start(f32[3,1,768]{2,1,0:T(1,128)S(1)} %get-tuple-element.70), channel_id=1, source_target_pairs={{2,0},{4,2},{6,4},{8,6},{10,8},{12,10},{14,12},{3,1},{5,3},{7,5},{... | collective-permute-start | bytes 27656 | tf_op jit(solution)/shard_map/ppermute | solution.py:17
  15.6 3.8 %collective-permute-start.2 = (f32[3,18,1]{2,1,0:T(8,128)S(1)}, f32[3,18,1]{2,1,0:T(8,128)S(1)}, u32[]{:S(2)}, u32[]{:S(2)}) collective-permute-start(f32[3,18,1]{2,1,0:T(8,128)S(1)} %get-tuple-element.59), channel_id=1, source_target_pairs={{0,1},{2,3},{4,5},{6,7},{8,9},{10,11},{12,13},{14,15},{16,17},{18,... | collective-permute-start | bytes 656 | tf_op jit(solution)/shard_map/ppermute | solution.py:16
  16.9 3.1 %collective-permute-start.3 = (f32[3,18,1]{2,1,0:T(8,128)S(1)}, f32[3,18,1]{2,1,0:T(8,128)S(1)}, u32[]{:S(2)}, u32[]{:S(2)}) collective-permute-start(f32[3,18,1]{2,1,0:T(8,128)S(1)} %get-tuple-element.60), channel_id=1, source_target_pairs={{1,0},{3,2},{5,4},{7,6},{9,8},{11,10},{13,12},{15,14},{17,16},{19,... | collective-permute-start | bytes 656 | tf_op jit(solution)/shard_map/ppermute | solution.py:17
  20.8 5.7 %collective-permute-start.4 = (f32[2,1,768]{2,0,1:T(2,128)S(1)}, f32[2,1,768]{2,0,1:T(2,128)S(1)}, u32[]{:S(2)}, u32[]{:S(2)}) collective-permute-start(f32[2,1,768]{2,0,1:T(2,128)S(1)} %copy.206), channel_id=1, source_target_pairs={{0,2},{2,4},{4,6},{6,8},{8,10},{10,12},{12,14},{1,3},{3,5},{5,7},{... | collective-permute-start | bytes 18440 | tf_op jit(solution)/shard_map/ppermute | solution.py:16
  25.2 5.5 %collective-permute-start.5 = (f32[2,1,768]{2,0,1:T(2,128)S(1)}, f32[2,1,768]{2,0,1:T(2,128)S(1)}, u32[]{:S(2)}, u32[]{:S(2)}) collective-permute-start(f32[2,1,768]{2,0,1:T(2,128)S(1)} %copy.207), channel_id=1, source_target_pairs={{2,0},{4,2},{6,4},{8,6},{10,8},{12,10},{14,12},{3,1},{5,3},{7,5},{... | collective-permute-start | bytes 18440 | tf_op jit(solution)/shard_map/ppermute | solution.py:17
  30.9 4.4 %collective-permute-start.7 = (f32[2,18,1]{2,0,1:T(2,128)S(1)}, f32[2,18,1]{2,0,1:T(2,128)S(1)}, u32[]{:S(2)}, u32[]{:S(2)}) collective-permute-start(f32[2,18,1]{2,0,1:T(2,128)S(1)} %get-tuple-element.97), channel_id=1, source_target_pairs={{1,0},{3,2},{5,4},{7,6},{9,8},{11,10},{13,12},{15,14},{17,16},{19,... | collective-permute-start | bytes 440 | tf_op jit(solution)/shard_map/ppermute | solution.py:17
  32.2 3.9 %collective-permute-start.6 = (f32[2,18,1]{2,0,1:T(2,128)S(1)}, f32[2,18,1]{2,0,1:T(2,128)S(1)}, u32[]{:S(2)}, u32[]{:S(2)}) collective-permute-start(f32[2,18,1]{2,0,1:T(2,128)S(1)} %get-tuple-element.98), channel_id=1, source_target_pairs={{0,1},{2,3},{4,5},{6,7},{8,9},{10,11},{12,13},{14,15},{16,17},{18,... | collective-permute-start | bytes 440 | tf_op jit(solution)/shard_map/ppermute | solution.py:16
  38.0 9.6 %collective-permute-start.8 = (f32[2,1,768]{2,0,1:T(2,128)S(1)}, f32[2,1,768]{2,0,1:T(2,128)}, u32[]{:S(2)}, u32[]{:S(2)}) collective-permute-start(f32[2,1,768]{2,0,1:T(2,128)S(1)} %copy.213), channel_id=1, source_target_pairs={{0,2},{2,4},{4,6},{6,8},{8,10},{10,12},{12,14},{1,3},{3,5},{5,7},{... | collective-permute-start | bytes 18440 | tf_op jit(solution)/shard_map/ppermute | solution.py:16
  46.3 5.5 %collective-permute-start.9 = (f32[2,1,768]{2,0,1:T(2,128)S(1)}, f32[2,1,768]{2,0,1:T(2,128)S(1)}, u32[]{:S(2)}, u32[]{:S(2)}) collective-permute-start(f32[2,1,768]{2,0,1:T(2,128)S(1)} %copy.214), channel_id=1, source_target_pairs={{2,0},{4,2},{6,4},{8,6},{10,8},{12,10},{14,12},{3,1},{5,3},{7,5},{... | collective-permute-start | bytes 18440 | tf_op jit(solution)/shard_map/ppermute | solution.py:17
  53.2 4.3 %collective-permute-start.10 = (f32[2,18,1]{2,0,1:T(2,128)}, f32[2,18,1]{2,0,1:T(2,128)}, u32[]{:S(2)}, u32[]{:S(2)}) collective-permute-start(f32[2,18,1]{2,0,1:T(2,128)} %get-tuple-element.93), channel_id=1, source_target_pairs={{0,1},{2,3},{4,5},{6,7},{8,9},{10,11},{12,13},{14,15},{16,17},{18,... | collective-permute-start | bytes 440 | tf_op jit(solution)/shard_map/ppermute | solution.py:16
  55.0 3.4 %collective-permute-start.11 = (f32[2,18,1]{2,0,1:T(2,128)}, f32[2,18,1]{2,0,1:T(2,128)}, u32[]{:S(2)}, u32[]{:S(2)}) collective-permute-start(f32[2,18,1]{2,0,1:T(2,128)} %get-tuple-element.94), channel_id=1, source_target_pairs={{1,0},{3,2},{5,4},{7,6},{9,8},{11,10},{13,12},{15,14},{17,16},{19,... | collective-permute-start | bytes 440 | tf_op jit(solution)/shard_map/ppermute | solution.py:17
  62.2 6.1 %collective-permute-start.12 = (f32[2,1,768]{2,0,1:T(2,128)S(1)}, f32[2,1,768]{2,0,1:T(2,128)S(1)}, u32[]{:S(2)}, u32[]{:S(2)}) collective-permute-start(f32[2,1,768]{2,0,1:T(2,128)S(1)} %copy.220), channel_id=1, source_target_pairs={{0,2},{2,4},{4,6},{6,8},{8,10},{10,12},{12,14},{1,3},{3,5},{5,7},{... | collective-permute-start | bytes 18440 | tf_op jit(solution)/shard_map/ppermute | solution.py:16
  67.0 5.5 %collective-permute-start.13 = (f32[2,1,768]{2,0,1:T(2,128)S(1)}, f32[2,1,768]{2,0,1:T(2,128)S(1)}, u32[]{:S(2)}, u32[]{:S(2)}) collective-permute-start(f32[2,1,768]{2,0,1:T(2,128)S(1)} %copy.221), channel_id=1, source_target_pairs={{2,0},{4,2},{6,4},{8,6},{10,8},{12,10},{14,12},{3,1},{5,3},{7,5},{... | collective-permute-start | bytes 18440 | tf_op jit(solution)/shard_map/ppermute | solution.py:17
  72.6 4.3 %collective-permute-start.15 = (f32[2,18,1]{2,0,1:T(2,128)S(1)}, f32[2,18,1]{2,0,1:T(2,128)S(1)}, u32[]{:S(2)}, u32[]{:S(2)}) collective-permute-start(f32[2,18,1]{2,0,1:T(2,128)S(1)} %get-tuple-element.89), channel_id=1, source_target_pairs={{1,0},{3,2},{5,4},{7,6},{9,8},{11,10},{13,12},{15,14},{17,16},{19,... | collective-permute-start | bytes 440 | tf_op jit(solution)/shard_map/ppermute | solution.py:17
  73.9 3.9 %collective-permute-start.14 = (f32[2,18,1]{2,0,1:T(2,128)S(1)}, f32[2,18,1]{2,0,1:T(2,128)S(1)}, u32[]{:S(2)}, u32[]{:S(2)}) collective-permute-start(f32[2,18,1]{2,0,1:T(2,128)S(1)} %get-tuple-element.90), channel_id=1, source_target_pairs={{0,1},{2,3},{4,5},{6,7},{8,9},{10,11},{12,13},{14,15},{16,17},{18,... | collective-permute-start | bytes 440 | tf_op jit(solution)/shard_map/ppermute | solution.py:16
  92.0 11.0 %collective-permute-start.16 = (f32[3,1,384]{2,1,0:T(1,128)}, f32[3,1,384]{2,1,0:T(1,128)}, u32[]{:S(2)}, u32[]{:S(2)}) collective-permute-start(f32[3,1,384]{2,1,0:T(1,128)} %get-tuple-element.109), channel_id=1, source_target_pairs={{0,2},{2,4},{4,6},{6,8},{8,10},{10,12},{12,14},{1,3},{3,5},{5,7},{... | collective-permute-start | bytes 13832 | tf_op jit(solution)/shard_map/ppermute | solution.py:16
  96.2 6.7 %collective-permute-start.17 = (f32[3,1,384]{2,1,0:T(1,128)}, f32[3,1,384]{2,1,0:T(1,128)}, u32[]{:S(2)}, u32[]{:S(2)}) collective-permute-start(f32[3,1,384]{2,1,0:T(1,128)} %get-tuple-element.110), channel_id=1, source_target_pairs={{2,0},{4,2},{6,4},{8,6},{10,8},{12,10},{14,12},{3,1},{5,3},{7,5},{... | collective-permute-start | bytes 13832 | tf_op jit(solution)/shard_map/ppermute | solution.py:17
  104.4 5.1 %collective-permute-start.18 = (f32[3,10,1]{2,1,0:T(8,128)}, f32[3,10,1]{2,1,0:T(8,128)}, u32[]{:S(2)}, u32[]{:S(2)}) collective-permute-start(f32[3,10,1]{2,1,0:T(8,128)} %get-tuple-element.107), channel_id=1, source_target_pairs={{0,1},{2,3},{4,5},{6,7},{8,9},{10,11},{12,13},{14,15},{16,17},{18,... | collective-permute-start | bytes 368 | tf_op jit(solution)/shard_map/ppermute | solution.py:16
  107.0 3.4 %collective-permute-start.19 = (f32[3,10,1]{2,1,0:T(8,128)}, f32[3,10,1]{2,1,0:T(8,128)}, u32[]{:S(2)}, u32[]{:S(2)}) collective-permute-start(f32[3,10,1]{2,1,0:T(8,128)} %get-tuple-element.108), channel_id=1, source_target_pairs={{1,0},{3,2},{5,4},{7,6},{9,8},{11,10},{13,12},{15,14},{17,16},{19,... | collective-permute-start | bytes 368 | tf_op jit(solution)/shard_map/ppermute | solution.py:17
  113.2 5.7 %collective-permute-start.20 = (f32[2,1,384]{2,1,0:T(1,128)S(1)}, f32[2,1,384]{2,1,0:T(1,128)S(1)}, u32[]{:S(2)}, u32[]{:S(2)}) collective-permute-start(f32[2,1,384]{2,1,0:T(1,128)S(1)} %get-tuple-element.121), channel_id=1, source_target_pairs={{0,2},{2,4},{4,6},{6,8},{8,10},{10,12},{12,14},{1,3},{3,5},{5,7},{... | collective-permute-start | bytes 9224 | tf_op jit(solution)/shard_map/ppermute | solution.py:16
  117.5 5.5 %collective-permute-start.21 = (f32[2,1,384]{2,1,0:T(1,128)S(1)}, f32[2,1,384]{2,1,0:T(1,128)S(1)}, u32[]{:S(2)}, u32[]{:S(2)}) collective-permute-start(f32[2,1,384]{2,1,0:T(1,128)S(1)} %get-tuple-element.122), channel_id=1, source_target_pairs={{2,0},{4,2},{6,4},{8,6},{10,8},{12,10},{14,12},{3,1},{5,3},{7,5},{... | collective-permute-start | bytes 9224 | tf_op jit(solution)/shard_map/ppermute | solution.py:17
  128.5 5.8 %collective-permute-start.24 = (f32[2,1,384]{2,1,0:T(1,128)S(1)}, f32[2,1,384]{2,1,0:T(1,128)S(1)}, u32[]{:S(2)}, u32[]{:S(2)}) collective-permute-start(f32[2,1,384]{2,1,0:T(1,128)S(1)} %get-tuple-element.119), channel_id=1, source_target_pairs={{0,2},{2,4},{4,6},{6,8},{8,10},{10,12},{12,14},{1,3},{3,5},{5,7},{... | collective-permute-start | bytes 9224 | tf_op jit(solution)/shard_map/ppermute | solution.py:16
  132.9 5.5 %collective-permute-start.25 = (f32[2,1,384]{2,1,0:T(1,128)S(1)}, f32[2,1,384]{2,1,0:T(1,128)S(1)}, u32[]{:S(2)}, u32[]{:S(2)}) collective-permute-start(f32[2,1,384]{2,1,0:T(1,128)S(1)} %get-tuple-element.120), channel_id=1, source_target_pairs={{2,0},{4,2},{6,4},{8,6},{10,8},{12,10},{14,12},{3,1},{5,3},{7,5},{... | collective-permute-start | bytes 9224 | tf_op jit(solution)/shard_map/ppermute | solution.py:17
  (21 other events, 301.7 us)
where the time goes:
time: 181 us; the launch traced here: 179 us
  starting transfers between devices  62.5 us (35%)
  blocking collectives  30.3 us (17%)
  waiting for transfers between devices  28.4 us (16%)
  local copies, waits for them, and re-layouts  24.9 us (14%)
  other arithmetic  23.1 us (13%)
  between operations  9.88 us (5%)
    ppermute x14, starting transfers between devices, extended(): before = lax.ppermute(last, axis, up)  44.2 us
    psum x1, blocking collectives, body(): gradient_total = lax.psum(gradient_part, ('gx', 'gy'))  30.3 us
    ppermute x14, waiting for transfers between devices, extended(): after = lax.ppermute(first, axis, down)  26.8 us
    ppermute x14, starting transfers between devices, extended(): after = lax.ppermute(first, axis, down)  18.2 us
    reshape x1, local copies, waits for them, and re-layouts, body(): residual.reshape(2, half_rows, 2, half_cols, 2).sum(axis=(2, 4))  8.03 us
    unnamed x43, local copies, waits for them, and re-layouts  5.65 us
    reshape x1, local copies, waits for them, and re-layouts, body(): coarse_beta = beta_eff.reshape(half_rows, 2, half_cols, 2).sum(axis=(1, 3))  3.96 us
    reshape x1, local copies, waits for them, and re-layouts, body(): visc_eff.reshape(half_rows, 2, half_cols, 2).sum(axis=(1, 3))  3.96 us
  transfers between devices with their start and end apart: 28, of which 13 were waited for; matrix products, arithmetic and copies ran while one was open for 8% of the time, Pallas kernels for 0%

commit v1 on v0

v1 whole, which is shorter than its diff:
```python
import functools

import jax
import jax.numpy as jnp
from jax import lax
from jax.experimental import pallas as pl
from jax.experimental.pallas import tpu as pltpu
from jax.sharding import PartitionSpec as P

DEG = 4
LANES = 128
SEGS = 8
RIM = 10
EDGE = 16
F32 = jnp.float32
AXES = ("gx", "gy")


def lane_ids():
    return lax.broadcasted_iota(jnp.int32, (8, LANES), 1)


def pack_kernel(misfit, visc, friction, ice, grounded, kb, down_send, up_send, side_send):
    rows, cols = visc.shape
    left = lax.axis_index("gy") == 0
    kb[0] = visc[...] * ice[...].astype(F32)
    kb[1] = friction[...] * grounded[...].astype(F32)
    fields = (misfit.at[0], misfit.at[1], kb.at[0], kb.at[1])
    for n, field in enumerate(fields):
        down_send[8 * n : 8 * n + 8, :] = field[rows - 8 :, :]
        down_send[32 + 2 * n : 34 + 2 * n, :] = field[rows - 10 : rows - 8, :]
        up_send[8 * n : 8 * n + 8, :] = field[:8, :]
        up_send[32 + 2 * n : 34 + 2 * n, :] = field[8:10, :]
        side_send[rows * n : rows * n + rows, :] = jnp.where(
            left, field[:, cols - LANES :], field[:, :LANES]
        )


def spread_rows(blocks, store):
    lanes = lax.broadcasted_iota(jnp.int32, blocks[1].shape, 1)
    for s in range(SEGS):
        start = 96 * s - EDGE
        first = start // LANES
        offset = start - LANES * first
        merged = jnp.where(lanes >= offset, blocks[first + 1], blocks[first + 2])
        store(s, pltpu.roll(merged, LANES - offset, 1))


def main_kernel(
    bounds, misfit, kb, velocity, from_up, from_down, side, side_up, side_down,
    multiplier, gradient, sums,
    fu, fv, kk, bb, cell, xu, xv, du, dv, ru, rv, cfu, cfv, ckk, cbb, ccell, cxu, cxv, cdu, cdv, mu, mv,
):
    rows, cols = gradient.shape
    total = rows + 2 * RIM
    column_blocks = cols // LANES
    gx_at, gx_size = lax.axis_index("gx"), lax.axis_size("gx")
    left = lax.axis_index("gy") == 0

    def spread(ref, base, height, side_block, target, first_row):
        blocks = [ref[base : base + height, LANES * j : LANES * j + LANES] for j in range(column_blocks)]
        zero = jnp.zeros_like(side_block)
        blocks = [jnp.where(left, zero, side_block)] + blocks + [jnp.where(left, side_block, zero)]

        def store(s, value):
            target[pl.ds(first_row * 8 + s, height, stride=8), :] = value

        spread_rows(blocks, store)

    targets = (fu, fv, kk, bb)
    own = (misfit.at[0], misfit.at[1], kb.at[0], kb.at[1])
    for n in range(4):
        for h in range(0, rows, 8):
            spread(own[n], h, 8, side[rows * n + h : rows * n + h + 8, :], targets[n], RIM + h)
    for received, partner, near, far in (
        (from_up, side_up, RIM - 8, 0),
        (from_down, side_down, RIM + rows, RIM + rows + 8),
    ):
        edge = jnp.where(left, partner[:, :LANES], partner[:, cols - LANES :])
        for n in range(4):
            spread(received, 8 * n, 8, edge[8 * n : 8 * n + 8], targets[n], near)
            spread(received, 32 + 2 * n, 2, edge[32 + 2 * n : 34 + 2 * n], targets[n], far)

    lanes = lane_ids()
    column = 96 * lax.broadcasted_iota(jnp.int32, (8, LANES), 0) + lanes - EDGE
    inside = jnp.where(left, (column >= 0).astype(F32), (column < cols).astype(F32))
    above = inside * jnp.where(gx_at > 0, 1.0, 0.0)
    below = inside * jnp.where(gx_at < gx_size - 1, 1.0, 0.0)
    mine = ((lanes >= EDGE) & (lanes < LANES - EDGE)).astype(F32)
    even = lanes % 2 == 0

    def at(ref, row):
        return ref[8 * row : 8 * row + 8, :]

    def put(ref, row, value):
        ref[8 * row : 8 * row + 8, :] = value

    def stiffness(visc, target, count, shift):
        paired = None
        for row in range(count):
            k = at(visc, row)
            now = k + pltpu.roll(k, LANES - shift, 1)
            if row:
                put(target, row - 1, 0.125 * (paired + now))
            paired = now

    def residual(x_u, x_v, f_u, f_v, beta, stiff, low, high, shift, use):
        def gradients(row):
            u, v = at(x_u, row), at(x_v, row)
            ru_, rv_ = pltpu.roll(u, LANES - shift, 1), pltpu.roll(v, LANES - shift, 1)
            return u, v, u + ru_, v + rv_, ru_ - u, rv_ - v

        def forces(row, one, two):
            a, b = two[2] - one[2], two[5] + one[5]
            c, d = two[4] + one[4], two[3] - one[3]
            s = at(stiff, row)
            both = a + b
            return s * (both + a), s * (both + b), (0.5 * s) * (c + d)

        before = gradients(low - 1)
        here = gradients(low)
        cell_before = forces(low - 1, before, here)
        for row in range(low, high):
            after = gradients(row + 1)
            cell_here = forces(row, here, after)
            shear = cell_before[2] + cell_here[2]
            shear_step = cell_before[2] - cell_here[2]
            px, qy = cell_before[0] - cell_here[0], cell_before[1] + cell_here[1]
            au = (px - shear) + pltpu.roll(px + shear, shift, 1)
            av = (shear_step - qy) + pltpu.roll(shear_step + qy, shift, 1)
            u, v = here[0], here[1]
            b = at(beta, row)
            use(row, u, v, at(f_u, row) - au - b * u, at(f_v, row) - av - b * v)
            here, cell_before = after, cell_here

    def sweep(x_u, x_v, d_u, d_v, f_u, f_v, beta, stiff, lower, upper, count, rim, shift):
        lower, upper = jnp.full((8, LANES), lower), jnp.full((8, LANES), upper)
        middle = 0.5 * (upper + lower)
        half = 0.5 * (upper - lower)
        spread_ = middle / half
        factor = 1.0 / spread_
        inverse = 1.0 / middle
        for row in range(count):
            put(x_u, row, at(f_u, row) * inverse)
            put(x_v, row, at(f_v, row) * inverse)
        for step in range(DEG - 1):
            factor_next = 1.0 / (2.0 * spread_ - factor)
            keep = factor_next * factor
            gain = 2.0 * factor_next / half
            gains = (gain * above, gain * inside, gain * below)
            first = step == 0

            def use(row, u, v, gu, gv):
                part = gains[0 if row < rim else 2 if row >= count - rim else 1]
                old_u = u if first else at(d_u, row)
                old_v = v if first else at(d_v, row)
                new_u = keep * old_u + part * gu
                new_v = keep * old_v + part * gv
                put(d_u, row, new_u)
                put(d_v, row, new_v)
                put(x_u, row, u + new_u)
                put(x_v, row, v + new_v)

            residual(x_u, x_v, f_u, f_v, beta, stiff, step + 1, count - step - 1, shift, use)
            factor = factor_next

    stiffness(kk, cell, total, 1)
    sweep(xu, xv, du, dv, fu, fv, bb, cell, bounds[0], bounds[1], total, RIM, 1)

    squares = [jnp.zeros((8, LANES), F32)]

    def keep_residual(row, u, v, gu, gv):
        part = above if row < RIM else below if row >= RIM + rows else inside
        gu, gv = gu * part, gv * part
        put(ru, row, gu)
        put(rv, row, gv)
        if RIM <= row < RIM + rows:
            squares[0] = squares[0] + (gu * gu + gv * gv)

    residual(xu, xv, fu, fv, bb, cell, DEG, total - DEG, 1, keep_residual)

    coarse_rim = (RIM - DEG) // 2
    coarse_rows = rows // 2 + 2 * coarse_rim
    for i in range(coarse_rows):
        row = DEG + 2 * i
        for source, target, scale in ((ru, cfu, None), (rv, cfv, None), (kk, ckk, 0.25), (bb, cbb, None)):
            pair = at(source, row) + at(source, row + 1)
            pair = pair + pltpu.roll(pair, LANES - 1, 1)
            put(target, i, pair if scale is None else scale * pair)
    stiffness(ckk, ccell, coarse_rows, 2)
    sweep(cxu, cxv, cdu, cdv, cfu, cfv, cbb, ccell, bounds[2], bounds[3], coarse_rows, coarse_rim, 2)

    for i in range(rows // 2):
        for fine, coarse, target in ((xu, cxu, mu), (xv, cxv, mv)):
            correction = at(coarse, coarse_rim + i)
            correction = jnp.where(even, correction, pltpu.roll(correction, 1, 1))
            for row in (2 * i, 2 * i + 1):
                put(target, row, at(fine, RIM + row) + correction)

    gradient_squares = jnp.zeros((8, LANES), F32)
    for h in range(0, rows, 8):
        for j in range(column_blocks):
            s = (LANES * j) // 96
            shift = LANES * j - 96 * s + EDGE
            border = 96 * (s + 1) - LANES * j
            columns = slice(LANES * j, LANES * j + LANES)
            product = None
            for n, source in enumerate((mu, mv)):
                one = source[pl.ds(8 * h + s, 8, stride=8), :]
                two = source[pl.ds(8 * h + s + 1, 8, stride=8), :]
                value = jnp.where(
                    lanes < border, pltpu.roll(one, LANES - shift, 1), pltpu.roll(two, (96 - shift) % LANES, 1)
                )
                multiplier[n, h : h + 8, columns] = value
                term = velocity[n, h : h + 8, columns] * value
                product = term if product is None else product + term
            value = -kb[1, h : h + 8, columns] * product
            gradient[h : h + 8, columns] = value
            gradient_squares = gradient_squares + value * value
    residual_squares = jnp.sum(squares[0] * mine, axis=0, keepdims=True)
    gradient_squares = jnp.sum(gradient_squares, axis=0, keepdims=True)
    pair = jnp.concatenate([residual_squares, gradient_squares], axis=1)
    sums[...] = jnp.broadcast_to(pair, sums.shape)


def scale_kernel(nodes, gathered, gradient, scaled, norm):
    residual_total = jnp.sum(gathered[:, :LANES], keepdims=True)
    gradient_total = jnp.sum(gathered[:, LANES:], keepdims=True)
    scaled[...] = gradient[...] / jnp.sqrt(gradient_total / nodes + 1e-06)
    norm[...] = jnp.sqrt(residual_total / (2 * nodes))


def body(misfit, velocity, viscosity, friction, ice, grounded, bounds):
    rows, cols = viscosity.shape
    gx_size, gy_size = lax.axis_size("gx"), lax.axis_size("gy")
    assert gy_size == 2 and cols == 96 * SEGS and rows == 16
    peers = gx_size * gy_size
    nodes = rows * cols * peers
    total = rows + 2 * RIM
    shaped = jax.ShapeDtypeStruct
    whole = pl.BlockSpec(memory_space=pltpu.VMEM)
    params = pltpu.CompilerParams(vmem_limit_bytes=32 * 1024 * 1024)

    kb, down_send, up_send, side_send = pl.pallas_call(
        pack_kernel,
        out_shape=(
            shaped((2, rows, cols), F32),
            shaped((4 * RIM, cols), F32),
            shaped((4 * RIM, cols), F32),
            shaped((4 * rows, LANES), F32),
        ),
        in_specs=[whole] * 5,
        out_specs=[whole] * 4,
        compiler_params=params,
        name="pack",
    )(misfit, viscosity, friction, ice, grounded)

    down = [(i, i + 1) for i in range(gx_size - 1)]
    up = [(j, i) for i, j in down]
    swap = [(0, 1), (1, 0)]
    from_up = lax.ppermute(down_send, "gx", down)
    from_down = lax.ppermute(up_send, "gx", up)
    side = lax.ppermute(side_send, "gy", swap)
    side_up = lax.ppermute(from_up, "gy", swap)
    side_down = lax.ppermute(from_down, "gy", swap)

    fine = pltpu.VMEM((8 * total, LANES), F32)
    coarse = pltpu.VMEM((4 * total, LANES), F32)
    owned = pltpu.VMEM((8 * rows, LANES), F32)
    multiplier, gradient, sums = pl.pallas_call(
        main_kernel,
        out_shape=(
            shaped((2, rows, cols), F32),
            shaped((rows, cols), F32),
            shaped((peers, 2 * LANES), F32),
        ),
        in_specs=[pl.BlockSpec(memory_space=pltpu.SMEM)] + [whole] * 8,
        out_specs=[whole] * 3,
        scratch_shapes=[fine] * 11 + [coarse] * 9 + [owned] * 2,
        compiler_params=params,
        name="leg",
    )(bounds, misfit, kb, velocity, from_up, from_down, side, side_up, side_down)

    gathered = lax.all_to_all(sums, AXES, 0, 0, tiled=True)
    scaled, norm = pl.pallas_call(
        functools.partial(scale_kernel, nodes),
        out_shape=(shaped((rows, cols), F32), shaped((1, 1), F32)),
        in_specs=[whole] * 2,
        out_specs=[whole] * 2,
        compiler_params=params,
        name="scale",
    )(gathered, gradient)
    return multiplier, scaled, norm.reshape(1)


def solution(mesh):
    tile = P(("grp", "gx"), "gy")
    pair = P(None, ("grp", "gx"), "gy")
    return jax.shard_map(
        body,
        mesh=mesh,
        in_specs=(pair, pair, tile, tile, tile, tile, P("grp")),
        out_specs=(pair, tile, P("grp")),
        check_vma=False,
    )
```

time: 181 us -> 36.8 us (0.20)
  starting transfers between devices: 62.5 us -> 6.65 us
  other arithmetic: 23.1 us -> 0 us
  waiting for transfers between devices: 28.4 us -> 6.35 us
  local copies, waits for them, and re-layouts: 24.9 us -> 4.1 us
  blocking collectives: 30.3 us -> 12.1 us
  between operations: 9.88 us -> 0.69 us
  Pallas kernels: 0 us -> 6.36 us
    ppermute x28 -> x5, starting transfers between devices: 62.5 us -> 6.65 us  [the longest x1 4.85 us: body(): from_up = lax.ppermute(down_send, 'gx', down)]
    psum x1 -> x0, blocking collectives: 30.3 us -> none  [body(): gradient_total = lax.psum(gradient_part, ('gx', 'gy'))]
    ppermute x28 -> x5, waiting for transfers between devices: 28.4 us -> 6.35 us  [the longest x1 4.21 us: body(): from_down = lax.ppermute(up_send, 'gx', up)]
    reshape x5 -> x0, local copies, waits for them, and re-layouts: 16.4 us -> none  [the longest x1 8.03 us: body(): residual.reshape(2, half_rows, 2, half_cols, 2).sum(axis=(2, 4))]
    all_to_all x0 -> x1, blocking collectives: none -> 12.1 us  [body(): gathered = lax.all_to_all(sums, AXES, 0, 0, tiled=True)]
    reduce_sum x6 -> x0, other arithmetic: 8.02 us -> none  [the longest x1 3.67 us: body(): residual.reshape(2, half_rows, 2, half_cols, 2).sum(axis=(2, 4))]
    pallas_call x0 -> x3, Pallas kernels: none -> 6.36 us  [the longest x1 5.56 us: body(): pl.pallas_call(main_kernel, out_shape=(shaped((2, rows, cols), F32), shap...]
    add x13 -> x0, other arithmetic: 4.05 us -> none  [the longest x6 3.93 us: chebyshev(): iterate = iterate + update]
  transfers between devices with their start and end apart: 28 -> 5, of which waited for: 13 -> 3; matrix products, arithmetic and copies ran while one was open for 8% -> 0% of each run, Pallas kernels for 0% -> 0%
where the time goes in v1:
time: 36.8 us; the launch traced here: 36.3 us
  blocking collectives  12.1 us (33%)
  starting transfers between devices  6.65 us (18%)
  Pallas kernels  6.36 us (17%)
  waiting for transfers between devices  6.35 us (17%)
  local copies, waits for them, and re-layouts  4.1 us (11%)
  between operations  0.69 us (2%)
    all_to_all x1, blocking collectives, body(): gathered = lax.all_to_all(sums, AXES, 0, 0, tiled=True)  12.1 us
    pallas_call x1, Pallas kernels, body(): pl.pallas_call(main_kernel, out_shape=(shaped((2, rows, cols), F32), shap...  5.56 us
    ppermute x1, starting transfers between devices, body(): from_up = lax.ppermute(down_send, 'gx', down)  4.85 us
    ppermute x1, waiting for transfers between devices, body(): from_down = lax.ppermute(up_send, 'gx', up)  4.21 us
    unnamed x15, local copies, waits for them, and re-layouts  4.09 us
    ppermute x1, starting transfers between devices, body(): from_down = lax.ppermute(up_send, 'gx', up)  1.29 us
    ppermute x1, waiting for transfers between devices, body(): from_up = lax.ppermute(down_send, 'gx', down)  1.26 us
    ppermute x1, waiting for transfers between devices, body(): side = lax.ppermute(side_send, 'gy', swap)  0.87 us
  transfers between devices with their start and end apart: 5, of which 3 were waited for; matrix products, arithmetic and copies ran while one was open for 0% of the time, Pallas kernels for 0%

profile of v1, /device:TPU:0, one launch (start us, length us, event | category | flops | bytes accessed | tf_op | source)
XLA Modules:
  0.0 36.3 jit_solution(6466978455333314883)
XLA Ops:
  0.6 0.0 copy-start
  0.6 0.9 %copy-done = f32[2,16,768]{2,1,0:T(8,128)S(1)} copy-done((f32[2,16,768]{2,1,0:T(8,128)S(1)}, f32[2,16,768]{2,1,0:T(8,128)}, u32[]{:S(2)}) %copy-start) | copy-done | bytes 98328
  1.5 0.0 copy-start.2
  1.5 0.8 %copy-done.2 = f32[16,768]{1,0:T(8,128)S(1)} copy-done((f32[16,768]{1,0:T(8,128)S(1)}, f32[16,768]{1,0:T(8,128)}, u32[]{:S(2)}) %copy-start.2) | copy-done | bytes 49176
  2.3 0.0 copy-start.3
  2.3 0.8 %copy-done.3 = f32[16,768]{1,0:T(8,128)S(1)} copy-done((f32[16,768]{1,0:T(8,128)S(1)}, f32[16,768]{1,0:T(8,128)}, u32[]{:S(2)}) %copy-start.3) | copy-done | bytes 49176
  3.1 0.8 %copy-done.4 = s32[16,768]{1,0:T(8,128)S(1)} copy-done((s32[16,768]{1,0:T(8,128)S(1)}, s32[16,768]{1,0:T(8,128)}, u32[]{:S(2)}) %copy-start.4) | copy-done | bytes 49176
  3.9 0.0 copy-start.5
  3.9 0.8 %copy-done.5 = s32[16,768]{1,0:T(8,128)S(1)} copy-done((s32[16,768]{1,0:T(8,128)S(1)}, s32[16,768]{1,0:T(8,128)}, u32[]{:S(2)}) %copy-start.5) | copy-done | bytes 49176
  4.8 4.8 %collective-permute-start = (f32[40,768]{1,0:T(8,128)S(1)}, f32[40,768]{1,0:T(8,128)S(1)}, u32[]{:S(2)}, u32[]{:S(2)}) collective-permute-start(f32[40,768]{1,0:T(8,128)S(1)} %get-tuple-element.13), channel_id=1, source_target_pairs={{0,2},{2,4},{4,6},{6,8},{8,10},{10,12},{12,14},{1,3},{3,5},{5,7},{... | collective-permute-start | bytes 368648 | tf_op jit(solution)/shard_map/ppermute | solution.py:261
  9.6 1.3 %collective-permute-start.1 = (f32[40,768]{1,0:T(8,128)S(1)}, f32[40,768]{1,0:T(8,128)S(1)}, u32[]{:S(2)}, u32[]{:S(2)}) collective-permute-start(f32[40,768]{1,0:T(8,128)S(1)} %get-tuple-element.14), channel_id=1, source_target_pairs={{2,0},{4,2},{6,4},{8,6},{10,8},{12,10},{14,12},{3,1},{5,3},{7,5},{... | collective-permute-start | bytes 368648 | tf_op jit(solution)/shard_map/ppermute | solution.py:262
  10.9 1.3 %collective-permute-done.from_up = f32[40,768]{1,0:T(8,128)S(1)} collective-permute-done((f32[40,768]{1,0:T(8,128)S(1)}, f32[40,768]{1,0:T(8,128)S(1)}, u32[]{:S(2)}, u32[]{:S(2)}) %collective-permute-start) | collective-permute-done | bytes 122912 | tf_op jit(solution)/shard_map/ppermute | solution.py:261
  12.2 0.0 collective-permute-start.3
  12.2 4.2 %collective-permute-done.1.from_down = f32[40,768]{1,0:T(8,128)S(1)} collective-permute-done((f32[40,768]{1,0:T(8,128)S(1)}, f32[40,768]{1,0:T(8,128)S(1)}, u32[]{:S(2)}, u32[]{:S(2)}) %collective-permute-start.1) | collective-permute-done | bytes 122912 | tf_op jit(solution)/shard_map/ppermute | solution.py:262
  16.4 0.0 collective-permute-start.4
  16.4 0.5 %collective-permute-start.2 = (f32[64,128]{1,0:T(8,128)S(1)}, f32[64,128]{1,0:T(8,128)S(1)}, u32[]{:S(2)}, u32[]{:S(2)}) collective-permute-start(f32[64,128]{1,0:T(8,128)S(1)} %get-tuple-element.15), channel_id=1, source_target_pairs={{0,1},{1,0},{2,3},{3,2},{4,5},{5,4},{6,7},{7,6},{8,9},{9,8},{10,11... | collective-permute-start | bytes 98312 | tf_op jit(solution)/shard_map/ppermute | solution.py:263
  16.9 0.9 %collective-permute-done.2.side = f32[64,128]{1,0:T(8,128)S(1)} collective-permute-done((f32[64,128]{1,0:T(8,128)S(1)}, f32[64,128]{1,0:T(8,128)S(1)}, u32[]{:S(2)}, u32[]{:S(2)}) %collective-permute-start.2) | collective-permute-done | bytes 32800 | tf_op jit(solution)/shard_map/ppermute | solution.py:263
  17.8 0.0 collective-permute-done.3.side_up
  17.8 0.0 collective-permute-done.4.side_down
  17.8 0.0 copy-done.1
  17.8 0.0 copy-done.6
  17.8 5.6 %leg.1 = (f32[2,16,768]{2,1,0:T(8,128)}, f32[16,768]{1,0:T(8,128)S(1)}, f32[16,256]{1,0:T(8,128)S(1)}) custom-call(f32[4]{0:T(128)S(1)} %copy-done.6, f32[2,16,768]{2,1,0:T(8,128)S(1)} %copy-done, f32[2,16,768]{2,1,0:T(8,128)S(1)} %get-tuple-element.12.kb, f32[2,16,768]{2,1,0:T(8,128)S(1)} %copy-done.1, f32[40,768]{1,0:T(8,128)S(1)} %collective-permute-done.from_up, ...), custom_call_target="tpu_custom_call" | custom-call | tf_op jit(solution)/shard_map/leg/pallas_call | solution.py:270
  23.4 12.1 %all_to_all.11 = f32[16,1,256]{2,1,0:T(1,128)S(1)} all-to-all(f32[16,1,256]{2,1,0:T(1,128)S(1)} %copy.10), channel_id=1, replica_groups=mesh['grp'=2,'gx'=8,'gy'=2] {'gx','gy'}, dimensions={0} | all-to-all | bytes 32768 | tf_op jit(solution)/shard_map/all_to_all | solution.py:284
  35.5 0.8 %scale.1 = (f32[16,768]{1,0:T(8,128)}, f32[1,1]{1,0:T(1,128)}) custom-call(f32[16,256]{1,0:T(8,128)S(1)} %bitcast.5, f32[16,768]{1,0:T(8,128)S(1)} %get-tuple-element.18.gradient), custom_call_target="tpu_custom_call" | custom-call | tf_op jit(solution)/shard_map/scale/pallas_call | solution.py:285
  (6 shorter events, 0.1 us)
Async XLA Ops:
  0.6 0.9 %copy-start = (f32[2,16,768]{2,1,0:T(8,128)S(1)}, f32[2,16,768]{2,1,0:T(8,128)}, u32[]{:S(2)}) copy-start(f32[2,16,768]{2,1,0:T(8,128)} %misfit.3) | copy-start | bytes 294916
  1.5 0.8 %copy-start.2 = (f32[16,768]{1,0:T(8,128)S(1)}, f32[16,768]{1,0:T(8,128)}, u32[]{:S(2)}) copy-start(f32[16,768]{1,0:T(8,128)} %visc.1) | copy-start | bytes 147460
  2.3 0.8 %copy-start.3 = (f32[16,768]{1,0:T(8,128)S(1)}, f32[16,768]{1,0:T(8,128)}, u32[]{:S(2)}) copy-start(f32[16,768]{1,0:T(8,128)} %friction.1) | copy-start | bytes 147460
  3.1 0.8 %copy-start.4 = (s32[16,768]{1,0:T(8,128)S(1)}, s32[16,768]{1,0:T(8,128)}, u32[]{:S(2)}) copy-start(s32[16,768]{1,0:T(8,128)} %ice.1) | copy-start | bytes 147460
  3.9 0.8 %copy-start.5 = (s32[16,768]{1,0:T(8,128)S(1)}, s32[16,768]{1,0:T(8,128)}, u32[]{:S(2)}) copy-start(s32[16,768]{1,0:T(8,128)} %grounded.1) | copy-start | bytes 147460
  4.7 13.1 %copy-start.1 = (f32[2,16,768]{2,1,0:T(8,128)S(1)}, f32[2,16,768]{2,1,0:T(8,128)}, u32[]{:S(2)}) copy-start(f32[2,16,768]{2,1,0:T(8,128)} %velocity.1) | copy-start | bytes 294916
  4.8 7.4 %collective-permute-start = (f32[40,768]{1,0:T(8,128)S(1)}, f32[40,768]{1,0:T(8,128)S(1)}, u32[]{:S(2)}, u32[]{:S(2)}) collective-permute-start(f32[40,768]{1,0:T(8,128)S(1)} %get-tuple-element.13), channel_id=1, source_target_pairs={{0,2},{2,4},{4,6},{6,8},{8,10},{10,12},{12,14},{1,3},{3,5},{5,7},{... | collective-permute-start | bytes 368648 | tf_op jit(solution)/shard_map/ppermute | solution.py:261
  9.6 6.8 %collective-permute-start.1 = (f32[40,768]{1,0:T(8,128)S(1)}, f32[40,768]{1,0:T(8,128)S(1)}, u32[]{:S(2)}, u32[]{:S(2)}) collective-permute-start(f32[40,768]{1,0:T(8,128)S(1)} %get-tuple-element.14), channel_id=1, source_target_pairs={{2,0},{4,2},{6,4},{8,6},{10,8},{12,10},{14,12},{3,1},{5,3},{7,5},{... | collective-permute-start | bytes 368648 | tf_op jit(solution)/shard_map/ppermute | solution.py:262
  12.2 5.6 %collective-permute-start.3 = (f32[40,768]{1,0:T(8,128)S(1)}, f32[40,768]{1,0:T(8,128)S(1)}, u32[]{:S(2)}, u32[]{:S(2)}) collective-permute-start(f32[40,768]{1,0:T(8,128)S(1)} %collective-permute-done.from_up), channel_id=1, source_target_pairs={{0,1},{1,0},{2,3},{3,2},{4,5},{5,4},{6,7},{7,6},{8,9},{9,8},{10,11... | collective-permute-start | bytes 368648 | tf_op jit(solution)/shard_map/ppermute | solution.py:264
  16.4 1.4 %collective-permute-start.4 = (f32[40,768]{1,0:T(8,128)S(1)}, f32[40,768]{1,0:T(8,128)S(1)}, u32[]{:S(2)}, u32[]{:S(2)}) collective-permute-start(f32[40,768]{1,0:T(8,128)S(1)} %collective-permute-done.1.from_down), channel_id=1, source_target_pairs={{0,1},{1,0},{2,3},{3,2},{4,5},{5,4},{6,7},{7,6},{8,9},{9,8},{10,11... | collective-permute-start | bytes 368648 | tf_op jit(solution)/shard_map/ppermute | solution.py:265
  16.4 1.4 %copy-start.6 = (f32[4]{0:T(128)S(1)}, f32[4]{0:T(128)}, u32[]{:S(2)}) copy-start(f32[4]{0:T(128)} %bounds.1) | copy-start | bytes 52
  16.4 1.4 %collective-permute-start.2 = (f32[64,128]{1,0:T(8,128)S(1)}, f32[64,128]{1,0:T(8,128)S(1)}, u32[]{:S(2)}, u32[]{:S(2)}) collective-permute-start(f32[64,128]{1,0:T(8,128)S(1)} %get-tuple-element.15), channel_id=1, source_target_pairs={{0,1},{1,0},{2,3},{3,2},{4,5},{5,4},{6,7},{7,6},{8,9},{9,8},{10,11... | collective-permute-start | bytes 98312 | tf_op jit(solution)/shard_map/ppermute | solution.py:263

commit v2 on v1

--- a/solution.py
+++ b/solution.py
@@ -20,20 +20,57 @@
     return lax.broadcasted_iota(jnp.int32, (8, LANES), 1)
 
 
-def pack_kernel(misfit, visc, friction, ice, grounded, kb, down_send, up_send, side_send):
+def pack_kernel(
+    bounds, misfit, visc, friction, ice, grounded,
+    fields, coefficients, x_send, z_send, side_send,
+    levels, visc_in, friction_in, ice_in, grounded_in, sems,
+):
+    copies = [
+        pltpu.make_async_copy(source, target, sems.at[n])
+        for n, (source, target) in enumerate((
+            (misfit, fields.at[pl.ds(0, 2)]),
+            (visc, visc_in),
+            (ice, ice_in),
+            (friction, friction_in),
+            (grounded, grounded_in),
+            (bounds, levels),
+        ))
+    ]
+    for copy in copies:
+        copy.start()
     rows, cols = visc.shape
     left = lax.axis_index("gy") == 0
-    kb[0] = visc[...] * ice[...].astype(F32)
-    kb[1] = friction[...] * grounded[...].astype(F32)
-    fields = (misfit.at[0], misfit.at[1], kb.at[0], kb.at[1])
-    for n, field in enumerate(fields):
-        down_send[8 * n : 8 * n + 8, :] = field[rows - 8 :, :]
-        down_send[32 + 2 * n : 34 + 2 * n, :] = field[rows - 10 : rows - 8, :]
-        up_send[8 * n : 8 * n + 8, :] = field[:8, :]
-        up_send[32 + 2 * n : 34 + 2 * n, :] = field[8:10, :]
+    low_half = lax.axis_index("gx") % 2 == 0
+    for copy in copies[:5]:
+        copy.wait()
+    fields[2] = visc_in[...] * ice_in[...].astype(F32)
+    fields[3] = friction_in[...] * grounded_in[...].astype(F32)
+    for n in range(4):
+        last, first = fields[n, rows - 8 :, :], fields[n, :8, :]
+        x_send[8 * n : 8 * n + 8, :] = jnp.where(low_half, last, first)
+        z_send[8 * n : 8 * n + 8, :] = jnp.where(low_half, first, last)
+        last, first = fields[n, rows - 10 : rows - 8, :], fields[n, 8:10, :]
+        x_send[32 + 2 * n : 34 + 2 * n, :] = jnp.where(low_half, last, first)
+        z_send[32 + 2 * n : 34 + 2 * n, :] = jnp.where(low_half, first, last)
         side_send[rows * n : rows * n + rows, :] = jnp.where(
-            left, field[:, cols - LANES :], field[:, :LANES]
+            left, fields[n, :, cols - LANES :], fields[n, :, :LANES]
         )
+    copies[5].wait()
+    for sweep in range(2):
+        lower = jnp.full((8, LANES), levels[2 * sweep])
+        upper = jnp.full((8, LANES), levels[2 * sweep + 1])
+        middle = 0.5 * (upper + lower)
+        half = 0.5 * (upper - lower)
+        spread = middle / half
+        factor = 1.0 / spread
+        values = [1.0 / middle]
+        for step in range(DEG - 1):
+            factor_next = 1.0 / (2.0 * spread - factor)
+            values += [factor_next * factor, 2.0 * factor_next / half]
+            factor = factor_next
+        for n, value in enumerate(values):
+            row = 8 * (sweep * (2 * DEG - 1) + n)
+            coefficients[row : row + 8, :] = value
 
 
 def spread_rows(blocks, store):
@@ -47,7 +84,7 @@
 
 
 def main_kernel(
-    bounds, misfit, kb, velocity, from_up, from_down, side, side_up, side_down,
+    coefficients, fields, velocity, from_x, from_z, side, side_x, side_z,
     multiplier, gradient, sums,
     fu, fv, kk, bb, cell, xu, xv, du, dv, ru, rv, cfu, cfv, ckk, cbb, ccell, cxu, cxv, cdu, cdv, mu, mv,
 ):
@@ -55,6 +92,7 @@
     total = rows + 2 * RIM
     column_blocks = cols // LANES
     gx_at, gx_size = lax.axis_index("gx"), lax.axis_size("gx")
+    low_half = gx_at % 2 == 0
     left = lax.axis_index("gy") == 0
 
     def spread(ref, base, height, side_block, target, first_row):
@@ -68,14 +106,12 @@
         spread_rows(blocks, store)
 
     targets = (fu, fv, kk, bb)
-    own = (misfit.at[0], misfit.at[1], kb.at[0], kb.at[1])
     for n in range(4):
         for h in range(0, rows, 8):
-            spread(own[n], h, 8, side[rows * n + h : rows * n + h + 8, :], targets[n], RIM + h)
-    for received, partner, near, far in (
-        (from_up, side_up, RIM - 8, 0),
-        (from_down, side_down, RIM + rows, RIM + rows + 8),
-    ):
+            spread(fields.at[n], h, 8, side[rows * n + h : rows * n + h + 8, :], targets[n], RIM + h)
+    for received, partner, is_above in ((from_x, side_x, jnp.logical_not(low_half)), (from_z, side_z, low_half)):
+        near = jnp.where(is_above, RIM - 8, RIM + rows)
+        far = jnp.where(is_above, 0, RIM + rows + 8)
         edge = jnp.where(left, partner[:, :LANES], partner[:, cols - LANES :])
         for n in range(4):
             spread(received, 8 * n, 8, edge[8 * n : 8 * n + 8], targets[n], near)
@@ -133,20 +169,14 @@
             use(row, u, v, at(f_u, row) - au - b * u, at(f_v, row) - av - b * v)
             here, cell_before = after, cell_here
 
-    def sweep(x_u, x_v, d_u, d_v, f_u, f_v, beta, stiff, lower, upper, count, rim, shift):
-        lower, upper = jnp.full((8, LANES), lower), jnp.full((8, LANES), upper)
-        middle = 0.5 * (upper + lower)
-        half = 0.5 * (upper - lower)
-        spread_ = middle / half
-        factor = 1.0 / spread_
-        inverse = 1.0 / middle
+    def sweep(x_u, x_v, d_u, d_v, f_u, f_v, beta, stiff, table, count, rim, shift):
+        inverse = at(coefficients, table)
         for row in range(count):
             put(x_u, row, at(f_u, row) * inverse)
             put(x_v, row, at(f_v, row) * inverse)
         for step in range(DEG - 1):
-            factor_next = 1.0 / (2.0 * spread_ - factor)
-            keep = factor_next * factor
-            gain = 2.0 * factor_next / half
+            keep = at(coefficients, table + 1 + 2 * step)
+            gain = at(coefficients, table + 2 + 2 * step)
             gains = (gain * above, gain * inside, gain * below)
             first = step == 0
 
@@ -162,10 +192,9 @@
                 put(x_v, row, v + new_v)
 
             residual(x_u, x_v, f_u, f_v, beta, stiff, step + 1, count - step - 1, shift, use)
-            factor = factor_next
 
     stiffness(kk, cell, total, 1)
-    sweep(xu, xv, du, dv, fu, fv, bb, cell, bounds[0], bounds[1], total, RIM, 1)
+    sweep(xu, xv, du, dv, fu, fv, bb, cell, 0, total, RIM, 1)
 
     squares = [jnp.zeros((8, LANES), F32)]
 
@@ -188,7 +217,7 @@
             pair = pair + pltpu.roll(pair, LANES - 1, 1)
             put(target, i, pair if scale is None else scale * pair)
     stiffness(ckk, ccell, coarse_rows, 2)
-    sweep(cxu, cxv, cdu, cdv, cfu, cfv, cbb, ccell, bounds[2], bounds[3], coarse_rows, coarse_rim, 2)
+    sweep(cxu, cxv, cdu, cdv, cfu, cfv, cbb, ccell, 2 * DEG - 1, coarse_rows, coarse_rim, 2)
 
     for i in range(rows // 2):
         for fine, coarse, target in ((xu, cxu, mu), (xv, cxv, mv)):
@@ -214,7 +243,7 @@
                 multiplier[n, h : h + 8, columns] = value
                 term = velocity[n, h : h + 8, columns] * value
                 product = term if product is None else product + term
-            value = -kb[1, h : h + 8, columns] * product
+            value = -fields[3, h : h + 8, columns] * product
             gradient[h : h + 8, columns] = value
             gradient_squares = gradient_squares + value * value
     residual_squares = jnp.sum(squares[0] * mine, axis=0, keepdims=True)
@@ -241,28 +270,39 @@
     whole = pl.BlockSpec(memory_space=pltpu.VMEM)
     params = pltpu.CompilerParams(vmem_limit_bytes=32 * 1024 * 1024)
 
-    kb, down_send, up_send, side_send = pl.pallas_call(
+    held = pl.BlockSpec(memory_space=pltpu.HBM)
+    fields, coefficients, x_send, z_send, side_send = pl.pallas_call(
         pack_kernel,
         out_shape=(
-            shaped((2, rows, cols), F32),
+            shaped((4, rows, cols), F32),
+            shaped((16 * (2 * DEG - 1), LANES), F32),
             shaped((4 * RIM, cols), F32),
             shaped((4 * RIM, cols), F32),
             shaped((4 * rows, LANES), F32),
         ),
-        in_specs=[whole] * 5,
-        out_specs=[whole] * 4,
+        in_specs=[held] * 6,
+        out_specs=[whole] * 5,
+        scratch_shapes=[
+            pltpu.SMEM((4,), F32),
+            pltpu.VMEM((rows, cols), F32),
+            pltpu.VMEM((rows, cols), F32),
+            pltpu.VMEM((rows, cols), jnp.int32),
+            pltpu.VMEM((rows, cols), jnp.int32),
+            pltpu.SemaphoreType.DMA((6,)),
+        ],
         compiler_params=params,
         name="pack",
-    )(misfit, viscosity, friction, ice, grounded)
-
-    down = [(i, i + 1) for i in range(gx_size - 1)]
-    up = [(j, i) for i, j in down]
+    )(*(pltpu.with_memory_space_constraint(x, pltpu.HBM) for x in (bounds, misfit, viscosity, friction, ice, grounded)))
+
+    x_pairs = [(i, i ^ 1) for i in range(gx_size) if i ^ 1 < gx_size]
+    z_pairs = [(i, j) for i in range(1, gx_size - 1, 2) for j in (i + 1,)]
+    z_pairs += [(j, i) for i, j in z_pairs]
     swap = [(0, 1), (1, 0)]
-    from_up = lax.ppermute(down_send, "gx", down)
-    from_down = lax.ppermute(up_send, "gx", up)
+    from_x = lax.ppermute(x_send, "gx", x_pairs)
+    from_z = lax.ppermute(z_send, "gx", z_pairs)
     side = lax.ppermute(side_send, "gy", swap)
-    side_up = lax.ppermute(from_up, "gy", swap)
-    side_down = lax.ppermute(from_down, "gy", swap)
+    side_x = lax.ppermute(from_x, "gy", swap)
+    side_z = lax.ppermute(from_z, "gy", swap)
 
     fine = pltpu.VMEM((8 * total, LANES), F32)
     coarse = pltpu.VMEM((4 * total, LANES), F32)
@@ -274,12 +314,12 @@
             shaped((rows, cols), F32),
             shaped((peers, 2 * LANES), F32),
         ),
-        in_specs=[pl.BlockSpec(memory_space=pltpu.SMEM)] + [whole] * 8,
+        in_specs=[whole] * 8,
         out_specs=[whole] * 3,
         scratch_shapes=[fine] * 11 + [coarse] * 9 + [owned] * 2,
         compiler_params=params,
         name="leg",
-    )(bounds, misfit, kb, velocity, from_up, from_down, side, side_up, side_down)
+    )(coefficients, fields, velocity, from_x, from_z, side, side_x, side_z)
 
     gathered = lax.all_to_all(sums, AXES, 0, 0, tiled=True)
     scaled, norm = pl.pallas_call(

time: 36.8 us -> 31.1 us (0.85)
  local copies, waits for them, and re-layouts: 4.1 us -> 0.02 us
  blocking collectives: 12.1 us -> 15.3 us
  starting transfers between devices: 6.65 us -> 4.17 us
  waiting for transfers between devices: 6.35 us -> 3.87 us
  Pallas kernels: 6.36 us -> 6.91 us
    unnamed x15 -> x3, local copies, waits for them, and re-layouts: 4.09 us -> 0.01 us
    all_to_all x1, blocking collectives: 12.1 us -> 15.3 us  [body(): gathered = lax.all_to_all(sums, AXES, 0, 0, tiled=True)]
    ppermute x4, waiting for transfers between devices: 5.48 us -> 2.66 us  [the longest x1 2.66 us: body(): from_x = lax.ppermute(x_send, 'gx', x_pairs)]
    ppermute x4, starting transfers between devices: 6.15 us -> 4.17 us  [the longest x1 3 us: body(): from_x = lax.ppermute(x_send, 'gx', x_pairs)]
    pallas_call x1, Pallas kernels: 0.04 us -> 1.1 us  [body(): pl.pallas_call(pack_kernel, out_shape=(shaped((4, rows, cols), F32), shap...]
    pallas_call x1, Pallas kernels: 5.56 us -> 5.05 us  [body(): pl.pallas_call(main_kernel, out_shape=(shaped((2, rows, cols), F32), shap...]
    ppermute x1, starting transfers between devices: 0.51 us -> 0.01 us  [body(): side = lax.ppermute(side_send, 'gy', swap)]
  transfers between devices with their start and end apart: 5 -> 5, of which waited for: 3 -> 2; matrix products, arithmetic and copies ran while one was open for 0% -> 0% of each run, Pallas kernels for 0% -> 0%
where the time goes in v2:
time: 31.1 us; the launch traced here: 30.9 us
  blocking collectives  15.3 us (49%)
  Pallas kernels  6.91 us (22%)
  starting transfers between devices  4.17 us (13%)
  waiting for transfers between devices  3.87 us (12%)
  between operations  0.67 us (2%)
    all_to_all x1, blocking collectives, body(): gathered = lax.all_to_all(sums, AXES, 0, 0, tiled=True)  15.3 us
    pallas_call x1, Pallas kernels, body(): pl.pallas_call(main_kernel, out_shape=(shaped((2, rows, cols), F32), shap...  5.05 us
    ppermute x1, starting transfers between devices, body(): from_x = lax.ppermute(x_send, 'gx', x_pairs)  3 us
    ppermute x1, waiting for transfers between devices, body(): from_x = lax.ppermute(x_send, 'gx', x_pairs)  2.66 us
    ppermute x1, waiting for transfers between devices, body(): side = lax.ppermute(side_send, 'gy', swap)  1.2 us
    pallas_call x1, Pallas kernels, body(): pl.pallas_call(pack_kernel, out_shape=(shaped((4, rows, cols), F32), shap...  1.1 us
    pallas_call x1, Pallas kernels, body(): pl.pallas_call(functools.partial(scale_kernel, nodes), out_shape=(shaped(...  0.76 us
    ppermute x1, starting transfers between devices, body(): from_z = lax.ppermute(z_send, 'gx', z_pairs)  0.66 us
  transfers between devices with their start and end apart: 5, of which 2 were waited for; matrix products, arithmetic and copies ran while one was open for 0% of the time, Pallas kernels for 0%

profile of v2, /device:TPU:0, one launch (start us, length us, event | category | flops | bytes accessed | tf_op | source)
XLA Modules:
  0.0 30.9 jit_solution(6334908072615538164)
XLA Ops:
  0.6 0.0 copy-start
  0.6 1.1 %pack.1 = (f32[4,16,768]{2,1,0:T(8,128)S(1)}, f32[112,128]{1,0:T(8,128)S(1)}, f32[40,768]{1,0:T(8,128)S(1)}, f32[40,768]{1,0:T(8,128)S(1)}, f32[64,128]{1,0:T(8,128)S(1)}) custom-call(f32[4]{0:T(128)} %bounds.1, f32[2,16,768]{2,1,0:T(8,128)} %misfit.1, f32[16,768]{1,0:T(8,128)} %visc.1, f32[16,768]{1,0:T(8,128)} %friction.1, s32[16,768]{1,0:T(8,128)} %ice.1, ...), custom_call_target="tpu_custom_call" | custom-call | tf_op jit(solution)/shard_map/pack/pallas_call | solution.py:274
  1.7 3.0 %collective-permute-start = (f32[40,768]{1,0:T(8,128)S(1)}, f32[40,768]{1,0:T(8,128)S(1)}, u32[]{:S(2)}, u32[]{:S(2)}) collective-permute-start(f32[40,768]{1,0:T(8,128)S(1)} %get-tuple-element.15), channel_id=1, source_target_pairs={{0,2},{2,0},{4,6},{6,4},{8,10},{10,8},{12,14},{14,12},{1,3},{3,1},... | collective-permute-start | bytes 368648 | tf_op jit(solution)/shard_map/ppermute | solution.py:301
  4.8 0.7 %collective-permute-start.1 = (f32[40,768]{1,0:T(8,128)S(1)}, f32[40,768]{1,0:T(8,128)S(1)}, u32[]{:S(2)}, u32[]{:S(2)}) collective-permute-start(f32[40,768]{1,0:T(8,128)S(1)} %get-tuple-element.16), channel_id=1, source_target_pairs={{2,4},{6,8},{10,12},{4,2},{8,6},{12,10},{3,5},{7,9},{11,13},{5,3},... | collective-permute-start | bytes 368648 | tf_op jit(solution)/shard_map/ppermute | solution.py:302
  5.4 2.7 %collective-permute-done.from_x = f32[40,768]{1,0:T(8,128)S(1)} collective-permute-done((f32[40,768]{1,0:T(8,128)S(1)}, f32[40,768]{1,0:T(8,128)S(1)}, u32[]{:S(2)}, u32[]{:S(2)}) %collective-permute-start) | collective-permute-done | bytes 122912 | tf_op jit(solution)/shard_map/ppermute | solution.py:301
  8.1 0.0 collective-permute-start.3
  8.1 0.0 collective-permute-done.1.from_z
  8.1 0.5 %collective-permute-start.4 = (f32[40,768]{1,0:T(8,128)S(1)}, f32[40,768]{1,0:T(8,128)S(1)}, u32[]{:S(2)}, u32[]{:S(2)}) collective-permute-start(f32[40,768]{1,0:T(8,128)S(1)} %collective-permute-done.1.from_z), channel_id=1, source_target_pairs={{0,1},{1,0},{2,3},{3,2},{4,5},{5,4},{6,7},{7,6},{8,9},{9,8},{10,11... | collective-permute-start | bytes 368648 | tf_op jit(solution)/shard_map/ppermute | solution.py:305
  8.6 0.0 collective-permute-start.2
  8.6 1.2 %collective-permute-done.2.side = f32[64,128]{1,0:T(8,128)S(1)} collective-permute-done((f32[64,128]{1,0:T(8,128)S(1)}, f32[64,128]{1,0:T(8,128)S(1)}, u32[]{:S(2)}, u32[]{:S(2)}) %collective-permute-start.2) | collective-permute-done | bytes 32800 | tf_op jit(solution)/shard_map/ppermute | solution.py:303
  9.8 0.0 collective-permute-done.3.side_x
  9.8 0.0 collective-permute-done.4.side_z
  9.8 0.0 copy-done
  9.8 5.1 %leg.1 = (f32[2,16,768]{2,1,0:T(8,128)}, f32[16,768]{1,0:T(8,128)S(1)}, f32[16,256]{1,0:T(8,128)S(1)}) custom-call(f32[112,128]{1,0:T(8,128)S(1)} %get-tuple-element.13.coefficients, f32[4,16,768]{2,1,0:T(8,128)S(1)} %get-tuple-element.14.fields, f32[2,16,768]{2,1,0:T(8,128)S(1)} %copy-done, f32[40,768]{1,0:T(8,128)S(1)} %collective-permute-done.from_x, ...), custom_call_target="tpu_custom_call" | custom-call | tf_op jit(solution)/shard_map/leg/pallas_call | solution.py:310
  14.9 15.3 %all_to_all.11 = f32[16,1,256]{2,1,0:T(1,128)S(1)} all-to-all(f32[16,1,256]{2,1,0:T(1,128)S(1)} %copy.10), channel_id=1, replica_groups=mesh['grp'=2,'gx'=8,'gy'=2] {'gx','gy'}, dimensions={0} | all-to-all | bytes 32768 | tf_op jit(solution)/shard_map/all_to_all | solution.py:324
  30.2 0.8 %scale.1 = (f32[16,768]{1,0:T(8,128)}, f32[1,1]{1,0:T(1,128)}) custom-call(f32[16,256]{1,0:T(8,128)S(1)} %bitcast.5, f32[16,768]{1,0:T(8,128)S(1)} %get-tuple-element.20.gradient), custom_call_target="tpu_custom_call" | custom-call | tf_op jit(solution)/shard_map/scale/pallas_call | solution.py:325
  (2 shorter events, 0.0 us)
Async XLA Ops:
  0.6 9.2 %copy-start = (f32[2,16,768]{2,1,0:T(8,128)S(1)}, f32[2,16,768]{2,1,0:T(8,128)}, u32[]{:S(2)}) copy-start(f32[2,16,768]{2,1,0:T(8,128)} %velocity.1) | copy-start | bytes 294916
  1.7 6.3 %collective-permute-start = (f32[40,768]{1,0:T(8,128)S(1)}, f32[40,768]{1,0:T(8,128)S(1)}, u32[]{:S(2)}, u32[]{:S(2)}) collective-permute-start(f32[40,768]{1,0:T(8,128)S(1)} %get-tuple-element.15), channel_id=1, source_target_pairs={{0,2},{2,0},{4,6},{6,4},{8,10},{10,8},{12,14},{14,12},{1,3},{3,1},... | collective-permute-start | bytes 368648 | tf_op jit(solution)/shard_map/ppermute | solution.py:301
  4.8 3.3 %collective-permute-start.1 = (f32[40,768]{1,0:T(8,128)S(1)}, f32[40,768]{1,0:T(8,128)S(1)}, u32[]{:S(2)}, u32[]{:S(2)}) collective-permute-start(f32[40,768]{1,0:T(8,128)S(1)} %get-tuple-element.16), channel_id=1, source_target_pairs={{2,4},{6,8},{10,12},{4,2},{8,6},{12,10},{3,5},{7,9},{11,13},{5,3},... | collective-permute-start | bytes 368648 | tf_op jit(solution)/shard_map/ppermute | solution.py:302
  8.1 1.7 %collective-permute-start.3 = (f32[40,768]{1,0:T(8,128)S(1)}, f32[40,768]{1,0:T(8,128)S(1)}, u32[]{:S(2)}, u32[]{:S(2)}) collective-permute-start(f32[40,768]{1,0:T(8,128)S(1)} %collective-permute-done.from_x), channel_id=1, source_target_pairs={{0,1},{1,0},{2,3},{3,2},{4,5},{5,4},{6,7},{7,6},{8,9},{9,8},{10,11... | collective-permute-start | bytes 368648 | tf_op jit(solution)/shard_map/ppermute | solution.py:304
  8.1 1.7 %collective-permute-start.4 = (f32[40,768]{1,0:T(8,128)S(1)}, f32[40,768]{1,0:T(8,128)S(1)}, u32[]{:S(2)}, u32[]{:S(2)}) collective-permute-start(f32[40,768]{1,0:T(8,128)S(1)} %collective-permute-done.1.from_z), channel_id=1, source_target_pairs={{0,1},{1,0},{2,3},{3,2},{4,5},{5,4},{6,7},{7,6},{8,9},{9,8},{10,11... | collective-permute-start | bytes 368648 | tf_op jit(solution)/shard_map/ppermute | solution.py:305
  8.6 1.2 %collective-permute-start.2 = (f32[64,128]{1,0:T(8,128)S(1)}, f32[64,128]{1,0:T(8,128)S(1)}, u32[]{:S(2)}, u32[]{:S(2)}) collective-permute-start(f32[64,128]{1,0:T(8,128)S(1)} %get-tuple-element.17), channel_id=1, source_target_pairs={{0,1},{1,0},{2,3},{3,2},{4,5},{5,4},{6,7},{7,6},{8,9},{9,8},{10,11... | collective-permute-start | bytes 98312 | tf_op jit(solution)/shard_map/ppermute | solution.py:303

commit v3 on v2

--- a/solution.py
+++ b/solution.py
@@ -87,6 +87,7 @@
     coefficients, fields, velocity, from_x, from_z, side, side_x, side_z,
     multiplier, gradient, sums,
     fu, fv, kk, bb, cell, xu, xv, du, dv, ru, rv, cfu, cfv, ckk, cbb, ccell, cxu, cxv, cdu, cdv, mu, mv,
+    nxu, nxv, nu, nv, tu, tv,
 ):
     rows, cols = gradient.shape
     total = rows + 2 * RIM
@@ -94,6 +95,8 @@
     gx_at, gx_size = lax.axis_index("gx"), lax.axis_size("gx")
     low_half = gx_at % 2 == 0
     left = lax.axis_index("gy") == 0
+
+    next_, here_part, shifted_part = (nxu, nxv), (nu, nv), (tu, tv)
 
     def spread(ref, base, height, side_block, target, first_row):
         blocks = [ref[base : base + height, LANES * j : LANES * j + LANES] for j in range(column_blocks)]
@@ -140,73 +143,73 @@
                 put(target, row - 1, 0.125 * (paired + now))
             paired = now
 
-    def residual(x_u, x_v, f_u, f_v, beta, stiff, low, high, shift, use):
+    def shifted(value, shift):
+        return pltpu.roll(value, LANES - shift, 1)
+
+    def forces(x, stiff, low, high, shift):
         def gradients(row):
-            u, v = at(x_u, row), at(x_v, row)
-            ru_, rv_ = pltpu.roll(u, LANES - shift, 1), pltpu.roll(v, LANES - shift, 1)
-            return u, v, u + ru_, v + rv_, ru_ - u, rv_ - v
-
-        def forces(row, one, two):
-            a, b = two[2] - one[2], two[5] + one[5]
-            c, d = two[4] + one[4], two[3] - one[3]
+            u, v = at(x[0], row), at(x[1], row)
+            next_u, next_v = at(next_[0], row), at(next_[1], row)
+            return u + next_u, v + next_v, next_u - u, next_v - v
+
+        def cells(row, one, two):
+            a, b = two[0] - one[0], two[3] + one[3]
+            c, d = two[2] + one[2], two[1] - one[1]
             s = at(stiff, row)
             both = a + b
             return s * (both + a), s * (both + b), (0.5 * s) * (c + d)
 
-        before = gradients(low - 1)
         here = gradients(low)
-        cell_before = forces(low - 1, before, here)
+        before = cells(low - 1, gradients(low - 1), here)
         for row in range(low, high):
             after = gradients(row + 1)
-            cell_here = forces(row, here, after)
-            shear = cell_before[2] + cell_here[2]
-            shear_step = cell_before[2] - cell_here[2]
-            px, qy = cell_before[0] - cell_here[0], cell_before[1] + cell_here[1]
-            au = (px - shear) + pltpu.roll(px + shear, shift, 1)
-            av = (shear_step - qy) + pltpu.roll(shear_step + qy, shift, 1)
-            u, v = here[0], here[1]
-            b = at(beta, row)
-            use(row, u, v, at(f_u, row) - au - b * u, at(f_v, row) - av - b * v)
-            here, cell_before = after, cell_here
-
-    def sweep(x_u, x_v, d_u, d_v, f_u, f_v, beta, stiff, table, count, rim, shift):
+            now = cells(row, here, after)
+            shear, shear_step = before[2] + now[2], before[2] - now[2]
+            normal_step, normal = before[0] - now[0], before[1] + now[1]
+            put(here_part[0], row, normal_step - shear)
+            put(here_part[1], row, shear_step - normal)
+            put(shifted_part[0], row, pltpu.roll(normal_step + shear, shift, 1))
+            put(shifted_part[1], row, pltpu.roll(shear_step + normal, shift, 1))
+            here, before = after, now
+
+    def remaining(n, x_row, f, beta, row):
+        return (at(f[n], row) - at(beta, row) * x_row) - (at(here_part[n], row) + at(shifted_part[n], row))
+
+    def sweep(x, old, f, beta, stiff, table, count, rim, shift):
         inverse = at(coefficients, table)
         for row in range(count):
-            put(x_u, row, at(f_u, row) * inverse)
-            put(x_v, row, at(f_v, row) * inverse)
+            for n in range(2):
+                value = at(f[n], row) * inverse
+                put(x[n], row, value)
+                put(next_[n], row, shifted(value, shift))
         for step in range(DEG - 1):
             keep = at(coefficients, table + 1 + 2 * step)
             gain = at(coefficients, table + 2 + 2 * step)
             gains = (gain * above, gain * inside, gain * below)
-            first = step == 0
-
-            def use(row, u, v, gu, gv):
+            low, high = step + 1, count - step - 1
+            forces(x, stiff, low, high, shift)
+            for row in range(low, high):
                 part = gains[0 if row < rim else 2 if row >= count - rim else 1]
-                old_u = u if first else at(d_u, row)
-                old_v = v if first else at(d_v, row)
-                new_u = keep * old_u + part * gu
-                new_v = keep * old_v + part * gv
-                put(d_u, row, new_u)
-                put(d_v, row, new_v)
-                put(x_u, row, u + new_u)
-                put(x_v, row, v + new_v)
-
-            residual(x_u, x_v, f_u, f_v, beta, stiff, step + 1, count - step - 1, shift, use)
+                for n in range(2):
+                    value = at(x[n], row)
+                    change = value if step == 0 else value - at(old[n], row)
+                    value = value + keep * change + part * remaining(n, value, f, beta, row)
+                    put(old[n], row, value)
+                    put(next_[n], row, shifted(value, shift))
+            x, old = old, x
+        return x
 
     stiffness(kk, cell, total, 1)
-    sweep(xu, xv, du, dv, fu, fv, bb, cell, 0, total, RIM, 1)
-
-    squares = [jnp.zeros((8, LANES), F32)]
-
-    def keep_residual(row, u, v, gu, gv):
+    x = sweep((xu, xv), (du, dv), (fu, fv), bb, cell, 0, total, RIM, 1)
+    forces(x, cell, DEG, total - DEG, 1)
+    squares = jnp.zeros((8, LANES), F32)
+    for row in range(DEG, total - DEG):
         part = above if row < RIM else below if row >= RIM + rows else inside
-        gu, gv = gu * part, gv * part
-        put(ru, row, gu)
-        put(rv, row, gv)
-        if RIM <= row < RIM + rows:
-            squares[0] = squares[0] + (gu * gu + gv * gv)
-
-    residual(xu, xv, fu, fv, bb, cell, DEG, total - DEG, 1, keep_residual)
+        for n in range(2):
+            value = part * remaining(n, at(x[n], row), (fu, fv), bb, row)
+            put((ru, rv)[n], row, value)
+            if RIM <= row < RIM + rows:
+                squares = squares + value * value
 
     coarse_rim = (RIM - DEG) // 2
     coarse_rows = rows // 2 + 2 * coarse_rim
@@ -217,10 +220,10 @@
             pair = pair + pltpu.roll(pair, LANES - 1, 1)
             put(target, i, pair if scale is None else scale * pair)
     stiffness(ckk, ccell, coarse_rows, 2)
-    sweep(cxu, cxv, cdu, cdv, cfu, cfv, cbb, ccell, 2 * DEG - 1, coarse_rows, coarse_rim, 2)
+    coarse_x = sweep((cxu, cxv), (cdu, cdv), (cfu, cfv), cbb, ccell, 2 * DEG - 1, coarse_rows, coarse_rim, 2)
 
     for i in range(rows // 2):
-        for fine, coarse, target in ((xu, cxu, mu), (xv, cxv, mv)):
+        for fine, coarse, target in zip(x, coarse_x, (mu, mv)):
             correction = at(coarse, coarse_rim + i)
             correction = jnp.where(even, correction, pltpu.roll(correction, 1, 1))
             for row in (2 * i, 2 * i + 1):
@@ -246,7 +249,7 @@
             value = -fields[3, h : h + 8, columns] * product
             gradient[h : h + 8, columns] = value
             gradient_squares = gradient_squares + value * value
-    residual_squares = jnp.sum(squares[0] * mine, axis=0, keepdims=True)
+    residual_squares = jnp.sum(squares * mine, axis=0, keepdims=True)
     gradient_squares = jnp.sum(gradient_squares, axis=0, keepdims=True)
     pair = jnp.concatenate([residual_squares, gradient_squares], axis=1)
     sums[...] = jnp.broadcast_to(pair, sums.shape)
@@ -316,7 +319,7 @@
         ),
         in_specs=[whole] * 8,
         out_specs=[whole] * 3,
-        scratch_shapes=[fine] * 11 + [coarse] * 9 + [owned] * 2,
+        scratch_shapes=[fine] * 11 + [coarse] * 9 + [owned] * 2 + [fine] * 6,
         compiler_params=params,
         name="leg",
     )(coefficients, fields, velocity, from_x, from_z, side, side_x, side_z)

time: 31.1 us -> 28.5 us (0.916)
  Pallas kernels: 6.91 us -> 4.33 us
    pallas_call x1, Pallas kernels: 5.05 us -> 2.47 us  [body(): pl.pallas_call(main_kernel, out_shape=(shaped((2, rows, cols), F32), shap...]
where the time goes in v3:
time: 28.5 us; the launch traced here: 28.3 us
  blocking collectives  15.3 us (54%)
  Pallas kernels  4.33 us (15%)
  starting transfers between devices  4.17 us (15%)
  waiting for transfers between devices  3.87 us (14%)
  between operations  0.67 us (2%)
    all_to_all x1, blocking collectives, body(): gathered = lax.all_to_all(sums, AXES, 0, 0, tiled=True)  15.3 us
    ppermute x1, starting transfers between devices, body(): from_x = lax.ppermute(x_send, 'gx', x_pairs)  3 us
    ppermute x1, waiting for transfers between devices, body(): from_x = lax.ppermute(x_send, 'gx', x_pairs)  2.66 us
    pallas_call x1, Pallas kernels, body(): pl.pallas_call(main_kernel, out_shape=(shaped((2, rows, cols), F32), shap...  2.47 us
    ppermute x1, waiting for transfers between devices, body(): side = lax.ppermute(side_send, 'gy', swap)  1.2 us
    pallas_call x1, Pallas kernels, body(): pl.pallas_call(pack_kernel, out_shape=(shaped((4, rows, cols), F32), shap...  1.1 us
    pallas_call x1, Pallas kernels, body(): pl.pallas_call(functools.partial(scale_kernel, nodes), out_shape=(shaped(...  0.76 us
    ppermute x1, starting transfers between devices, body(): from_z = lax.ppermute(z_send, 'gx', z_pairs)  0.66 us
  transfers between devices with their start and end apart: 5, of which 2 were waited for; matrix products, arithmetic and copies ran while one was open for 0% of the time, Pallas kernels for 0%

profile of v3, /device:TPU:0, one launch (start us, length us, event | category | flops | bytes accessed | tf_op | source)
XLA Modules:
  0.0 28.3 jit_solution(9262470455514518783)
XLA Ops:
  0.6 0.0 copy-start
  0.6 1.1 %pack.1 = (f32[4,16,768]{2,1,0:T(8,128)S(1)}, f32[112,128]{1,0:T(8,128)S(1)}, f32[40,768]{1,0:T(8,128)S(1)}, f32[40,768]{1,0:T(8,128)S(1)}, f32[64,128]{1,0:T(8,128)S(1)}) custom-call(f32[4]{0:T(128)} %bounds.1, f32[2,16,768]{2,1,0:T(8,128)} %misfit.1, f32[16,768]{1,0:T(8,128)} %visc.1, f32[16,768]{1,0:T(8,128)} %friction.1, s32[16,768]{1,0:T(8,128)} %ice.1, ...), custom_call_target="tpu_custom_call" | custom-call | tf_op jit(solution)/shard_map/pack/pallas_call | solution.py:277
  1.7 3.0 %collective-permute-start = (f32[40,768]{1,0:T(8,128)S(1)}, f32[40,768]{1,0:T(8,128)S(1)}, u32[]{:S(2)}, u32[]{:S(2)}) collective-permute-start(f32[40,768]{1,0:T(8,128)S(1)} %get-tuple-element.15), channel_id=1, source_target_pairs={{0,2},{2,0},{4,6},{6,4},{8,10},{10,8},{12,14},{14,12},{1,3},{3,1},... | collective-permute-start | bytes 368648 | tf_op jit(solution)/shard_map/ppermute | solution.py:304
  4.8 0.7 %collective-permute-start.1 = (f32[40,768]{1,0:T(8,128)S(1)}, f32[40,768]{1,0:T(8,128)S(1)}, u32[]{:S(2)}, u32[]{:S(2)}) collective-permute-start(f32[40,768]{1,0:T(8,128)S(1)} %get-tuple-element.16), channel_id=1, source_target_pairs={{2,4},{6,8},{10,12},{4,2},{8,6},{12,10},{3,5},{7,9},{11,13},{5,3},... | collective-permute-start | bytes 368648 | tf_op jit(solution)/shard_map/ppermute | solution.py:305
  5.4 2.7 %collective-permute-done.from_x = f32[40,768]{1,0:T(8,128)S(1)} collective-permute-done((f32[40,768]{1,0:T(8,128)S(1)}, f32[40,768]{1,0:T(8,128)S(1)}, u32[]{:S(2)}, u32[]{:S(2)}) %collective-permute-start) | collective-permute-done | bytes 122912 | tf_op jit(solution)/shard_map/ppermute | solution.py:304
  8.1 0.0 collective-permute-start.3
  8.1 0.0 collective-permute-done.1.from_z
  8.1 0.5 %collective-permute-start.4 = (f32[40,768]{1,0:T(8,128)S(1)}, f32[40,768]{1,0:T(8,128)S(1)}, u32[]{:S(2)}, u32[]{:S(2)}) collective-permute-start(f32[40,768]{1,0:T(8,128)S(1)} %collective-permute-done.1.from_z), channel_id=1, source_target_pairs={{0,1},{1,0},{2,3},{3,2},{4,5},{5,4},{6,7},{7,6},{8,9},{9,8},{10,11... | collective-permute-start | bytes 368648 | tf_op jit(solution)/shard_map/ppermute | solution.py:308
  8.6 0.0 collective-permute-start.2
  8.6 1.2 %collective-permute-done.2.side = f32[64,128]{1,0:T(8,128)S(1)} collective-permute-done((f32[64,128]{1,0:T(8,128)S(1)}, f32[64,128]{1,0:T(8,128)S(1)}, u32[]{:S(2)}, u32[]{:S(2)}) %collective-permute-start.2) | collective-permute-done | bytes 32800 | tf_op jit(solution)/shard_map/ppermute | solution.py:306
  9.8 0.0 collective-permute-done.3.side_x
  9.8 0.0 collective-permute-done.4.side_z
  9.8 0.0 copy-done
  9.8 2.5 %leg.1 = (f32[2,16,768]{2,1,0:T(8,128)}, f32[16,768]{1,0:T(8,128)S(1)}, f32[16,256]{1,0:T(8,128)S(1)}) custom-call(f32[112,128]{1,0:T(8,128)S(1)} %get-tuple-element.13.coefficients, f32[4,16,768]{2,1,0:T(8,128)S(1)} %get-tuple-element.14.fields, f32[2,16,768]{2,1,0:T(8,128)S(1)} %copy-done, f32[40,768]{1,0:T(8,128)S(1)} %collective-permute-done.from_x, ...), custom_call_target="tpu_custom_call" | custom-call | tf_op jit(solution)/shard_map/leg/pallas_call | solution.py:313
  12.3 15.3 %all_to_all.11 = f32[16,1,256]{2,1,0:T(1,128)S(1)} all-to-all(f32[16,1,256]{2,1,0:T(1,128)S(1)} %copy.10), channel_id=1, replica_groups=mesh['grp'=2,'gx'=8,'gy'=2] {'gx','gy'}, dimensions={0} | all-to-all | bytes 32768 | tf_op jit(solution)/shard_map/all_to_all | solution.py:327
  27.6 0.8 %scale.1 = (f32[16,768]{1,0:T(8,128)}, f32[1,1]{1,0:T(1,128)}) custom-call(f32[16,256]{1,0:T(8,128)S(1)} %bitcast.5, f32[16,768]{1,0:T(8,128)S(1)} %get-tuple-element.20.gradient), custom_call_target="tpu_custom_call" | custom-call | tf_op jit(solution)/shard_map/scale/pallas_call | solution.py:328
  (2 shorter events, 0.0 us)
Async XLA Ops:
  0.6 9.2 %copy-start = (f32[2,16,768]{2,1,0:T(8,128)S(1)}, f32[2,16,768]{2,1,0:T(8,128)}, u32[]{:S(2)}) copy-start(f32[2,16,768]{2,1,0:T(8,128)} %velocity.1) | copy-start | bytes 294916
  1.7 6.3 %collective-permute-start = (f32[40,768]{1,0:T(8,128)S(1)}, f32[40,768]{1,0:T(8,128)S(1)}, u32[]{:S(2)}, u32[]{:S(2)}) collective-permute-start(f32[40,768]{1,0:T(8,128)S(1)} %get-tuple-element.15), channel_id=1, source_target_pairs={{0,2},{2,0},{4,6},{6,4},{8,10},{10,8},{12,14},{14,12},{1,3},{3,1},... | collective-permute-start | bytes 368648 | tf_op jit(solution)/shard_map/ppermute | solution.py:304
  4.8 3.3 %collective-permute-start.1 = (f32[40,768]{1,0:T(8,128)S(1)}, f32[40,768]{1,0:T(8,128)S(1)}, u32[]{:S(2)}, u32[]{:S(2)}) collective-permute-start(f32[40,768]{1,0:T(8,128)S(1)} %get-tuple-element.16), channel_id=1, source_target_pairs={{2,4},{6,8},{10,12},{4,2},{8,6},{12,10},{3,5},{7,9},{11,13},{5,3},... | collective-permute-start | bytes 368648 | tf_op jit(solution)/shard_map/ppermute | solution.py:305
  8.1 1.7 %collective-permute-start.3 = (f32[40,768]{1,0:T(8,128)S(1)}, f32[40,768]{1,0:T(8,128)S(1)}, u32[]{:S(2)}, u32[]{:S(2)}) collective-permute-start(f32[40,768]{1,0:T(8,128)S(1)} %collective-permute-done.from_x), channel_id=1, source_target_pairs={{0,1},{1,0},{2,3},{3,2},{4,5},{5,4},{6,7},{7,6},{8,9},{9,8},{10,11... | collective-permute-start | bytes 368648 | tf_op jit(solution)/shard_map/ppermute | solution.py:307
  8.1 1.7 %collective-permute-start.4 = (f32[40,768]{1,0:T(8,128)S(1)}, f32[40,768]{1,0:T(8,128)S(1)}, u32[]{:S(2)}, u32[]{:S(2)}) collective-permute-start(f32[40,768]{1,0:T(8,128)S(1)} %collective-permute-done.1.from_z), channel_id=1, source_target_pairs={{0,1},{1,0},{2,3},{3,2},{4,5},{5,4},{6,7},{7,6},{8,9},{9,8},{10,11... | collective-permute-start | bytes 368648 | tf_op jit(solution)/shard_map/ppermute | solution.py:308
  8.6 1.2 %collective-permute-start.2 = (f32[64,128]{1,0:T(8,128)S(1)}, f32[64,128]{1,0:T(8,128)S(1)}, u32[]{:S(2)}, u32[]{:S(2)}) collective-permute-start(f32[64,128]{1,0:T(8,128)S(1)} %get-tuple-element.17), channel_id=1, source_target_pairs={{0,1},{1,0},{2,3},{3,2},{4,5},{5,4},{6,7},{7,6},{8,9},{9,8},{10,11... | collective-permute-start | bytes 98312 | tf_op jit(solution)/shard_map/ppermute | solution.py:306

commit v4 on v3

--- a/solution.py
+++ b/solution.py
@@ -40,7 +40,9 @@
         copy.start()
     rows, cols = visc.shape
     left = lax.axis_index("gy") == 0
-    low_half = lax.axis_index("gx") % 2 == 0
+    at, last_at = lax.axis_index("gx"), lax.axis_size("gx") - 1
+    low_half = at % 2 == 0
+    at_end = (at == 0) | (at == last_at)
     for copy in copies[:5]:
         copy.wait()
     fields[2] = visc_in[...] * ice_in[...].astype(F32)
@@ -48,10 +50,10 @@
     for n in range(4):
         last, first = fields[n, rows - 8 :, :], fields[n, :8, :]
         x_send[8 * n : 8 * n + 8, :] = jnp.where(low_half, last, first)
-        z_send[8 * n : 8 * n + 8, :] = jnp.where(low_half, first, last)
+        z_send[8 * n : 8 * n + 8, :] = jnp.where(at_end, 0.0, jnp.where(low_half, first, last))
         last, first = fields[n, rows - 10 : rows - 8, :], fields[n, 8:10, :]
         x_send[32 + 2 * n : 34 + 2 * n, :] = jnp.where(low_half, last, first)
-        z_send[32 + 2 * n : 34 + 2 * n, :] = jnp.where(low_half, first, last)
+        z_send[32 + 2 * n : 34 + 2 * n, :] = jnp.where(at_end, 0.0, jnp.where(low_half, first, last))
         side_send[rows * n : rows * n + rows, :] = jnp.where(
             left, fields[n, :, cols - LANES :], fields[n, :, :LANES]
         )
@@ -255,17 +257,26 @@
     sums[...] = jnp.broadcast_to(pair, sums.shape)
 
 
-def scale_kernel(nodes, gathered, gradient, scaled, norm):
+def scale_kernel(nodes, gathered, gradient, held_multiplier, scaled, norm, multiplier, scaled_out, norm_out, sems):
+    copies = [
+        pltpu.make_async_copy(source, target, sems.at[n])
+        for n, (source, target) in enumerate(((held_multiplier, multiplier), (norm_out, norm), (scaled_out, scaled)))
+    ]
+    copies[0].start()
     residual_total = jnp.sum(gathered[:, :LANES], keepdims=True)
     gradient_total = jnp.sum(gathered[:, LANES:], keepdims=True)
-    scaled[...] = gradient[...] / jnp.sqrt(gradient_total / nodes + 1e-06)
-    norm[...] = jnp.sqrt(residual_total / (2 * nodes))
+    norm_out[...] = jnp.sqrt(residual_total / (2 * nodes))
+    copies[1].start()
+    scaled_out[...] = gradient[...] / jnp.sqrt(gradient_total / nodes + 1e-06)
+    copies[2].start()
+    for copy in copies:
+        copy.wait()
 
 
 def body(misfit, velocity, viscosity, friction, ice, grounded, bounds):
     rows, cols = viscosity.shape
     gx_size, gy_size = lax.axis_size("gx"), lax.axis_size("gy")
-    assert gy_size == 2 and cols == 96 * SEGS and rows == 16
+    assert gy_size == 2 and gx_size % 2 == 0 and cols == 96 * SEGS and rows == 16
     peers = gx_size * gy_size
     nodes = rows * cols * peers
     total = rows + 2 * RIM
@@ -297,24 +308,25 @@
         name="pack",
     )(*(pltpu.with_memory_space_constraint(x, pltpu.HBM) for x in (bounds, misfit, viscosity, friction, ice, grounded)))
 
-    x_pairs = [(i, i ^ 1) for i in range(gx_size) if i ^ 1 < gx_size]
-    z_pairs = [(i, j) for i in range(1, gx_size - 1, 2) for j in (i + 1,)]
-    z_pairs += [(j, i) for i, j in z_pairs]
+    x_pairs = [(i, i ^ 1) for i in range(gx_size)]
+    z_pairs = [(2 * i + c, 2 * j + c) for i in range(1, gx_size - 1) for j in (i + 1 if i % 2 else i - 1,) for c in (0, 1)]
+    z_pairs += [(2 * i + c, 2 * i + 1 - c) for i in (0, gx_size - 1) for c in (0, 1)]
     swap = [(0, 1), (1, 0)]
     from_x = lax.ppermute(x_send, "gx", x_pairs)
-    from_z = lax.ppermute(z_send, "gx", z_pairs)
+    from_z = lax.ppermute(z_send, AXES, z_pairs)
     side = lax.ppermute(side_send, "gy", swap)
+    from_x, from_z, side = lax.optimization_barrier((from_x, from_z, side))
     side_x = lax.ppermute(from_x, "gy", swap)
     side_z = lax.ppermute(from_z, "gy", swap)
 
     fine = pltpu.VMEM((8 * total, LANES), F32)
     coarse = pltpu.VMEM((4 * total, LANES), F32)
     owned = pltpu.VMEM((8 * rows, LANES), F32)
-    multiplier, gradient, sums = pl.pallas_call(
+    held_multiplier, gradient, sums = pl.pallas_call(
         main_kernel,
         out_shape=(
-            shaped((2, rows, cols), F32),
-            shaped((rows, cols), F32),
+            pltpu.VMEM((2, rows, cols), F32),
+            pltpu.VMEM((rows, cols), F32),
             shaped((peers, 2 * LANES), F32),
         ),
         in_specs=[whole] * 8,
@@ -325,14 +337,23 @@
     )(coefficients, fields, velocity, from_x, from_z, side, side_x, side_z)
 
     gathered = lax.all_to_all(sums, AXES, 0, 0, tiled=True)
-    scaled, norm = pl.pallas_call(
+    scaled, norm, multiplier = pl.pallas_call(
         functools.partial(scale_kernel, nodes),
-        out_shape=(shaped((rows, cols), F32), shaped((1, 1), F32)),
-        in_specs=[whole] * 2,
-        out_specs=[whole] * 2,
+        out_shape=(
+            pltpu.HBM((rows, cols), F32),
+            pltpu.HBM((1, 1), F32),
+            pltpu.HBM((2, rows, cols), F32),
+        ),
+        in_specs=[whole] * 3,
+        out_specs=[held] * 3,
+        scratch_shapes=[
+            pltpu.VMEM((rows, cols), F32),
+            pltpu.VMEM((1, 1), F32),
+            pltpu.SemaphoreType.DMA((3,)),
+        ],
         compiler_params=params,
         name="scale",
-    )(gathered, gradient)
+    )(gathered, gradient, held_multiplier)
     return multiplier, scaled, norm.reshape(1)
 
 

time: 28.5 us -> 26.6 us (0.933)
  blocking collectives: 15.3 us -> 12.3 us
  waiting for transfers between devices: 3.87 us -> 5.7 us
  Pallas kernels: 4.33 us -> 3.73 us
    all_to_all x1, blocking collectives: 15.3 us -> 12.3 us  [body(): gathered = lax.all_to_all(sums, AXES, 0, 0, tiled=True)]
    ppermute x1, waiting for transfers between devices: 2.66 us -> 3.83 us  [body(): from_x = lax.ppermute(x_send, 'gx', x_pairs)]
    ppermute x1, waiting for transfers between devices: 0.01 us -> 0.83 us  [body(): side_x = lax.ppermute(from_x, 'gy', swap)]
    ppermute x1, starting transfers between devices: 0.66 us -> 0.01 us  [body(): from_z = lax.ppermute(z_send, AXES, z_pairs)]
    pallas_call x2, Pallas kernels: 3.24 us -> 2.62 us  [the longest x1 1.84 us: body(): pl.pallas_call(main_kernel, out_shape=(pltpu.VMEM((2, rows, cols), F32),...]
    ppermute x1, starting transfers between devices: 0.01 us -> 0.51 us  [body(): side = lax.ppermute(side_send, 'gy', swap)]
    ppermute x1, waiting for transfers between devices: 1.2 us -> 0.87 us  [body(): side = lax.ppermute(side_send, 'gy', swap)]
  transfers between devices with their start and end apart: 5 -> 5, of which waited for: 2 -> 4; matrix products, arithmetic and copies ran while one was open for 0% -> 0% of each run, Pallas kernels for 0% -> 0%
where the time goes in v4:
time: 26.6 us; the launch traced here: 26.4 us
  blocking collectives  12.3 us (46%)
  waiting for transfers between devices  5.7 us (21%)
  starting transfers between devices  4.02 us (15%)
  Pallas kernels  3.73 us (14%)
  between operations  0.66 us (2%)
    all_to_all x1, blocking collectives, body(): gathered = lax.all_to_all(sums, AXES, 0, 0, tiled=True)  12.3 us
    ppermute x1, waiting for transfers between devices, body(): from_x = lax.ppermute(x_send, 'gx', x_pairs)  3.83 us
    ppermute x1, starting transfers between devices, body(): from_x = lax.ppermute(x_send, 'gx', x_pairs)  3 us
    pallas_call x1, Pallas kernels, body(): pl.pallas_call(main_kernel, out_shape=(pltpu.VMEM((2, rows, cols), F32),...  1.84 us
    pallas_call x1, Pallas kernels, body(): pl.pallas_call(pack_kernel, out_shape=(shaped((4, rows, cols), F32), shap...  1.1 us
    ppermute x1, waiting for transfers between devices, body(): side = lax.ppermute(side_send, 'gy', swap)  0.87 us
    ppermute x1, waiting for transfers between devices, body(): side_x = lax.ppermute(from_x, 'gy', swap)  0.83 us
    pallas_call x1, Pallas kernels, body(): pl.pallas_call(functools.partial(scale_kernel, nodes), out_shape=(pltpu.H...  0.79 us
  transfers between devices with their start and end apart: 5, of which 4 were waited for; matrix products, arithmetic and copies ran while one was open for 0% of the time, Pallas kernels for 0%

profile of v4, /device:TPU:0, one launch (start us, length us, event | category | flops | bytes accessed | tf_op | source)
XLA Modules:
  0.0 26.4 jit_solution(10566736377290665887)
XLA Ops:
  0.6 0.0 copy-start
  0.6 1.1 %pack.1 = (f32[4,16,768]{2,1,0:T(8,128)S(1)}, f32[112,128]{1,0:T(8,128)S(1)}, f32[40,768]{1,0:T(8,128)S(1)}, f32[40,768]{1,0:T(8,128)S(1)}, f32[64,128]{1,0:T(8,128)S(1)}) custom-call(f32[4]{0:T(128)} %bounds.1, f32[2,16,768]{2,1,0:T(8,128)} %misfit.1, f32[16,768]{1,0:T(8,128)} %visc.1, f32[16,768]{1,0:T(8,128)} %friction.1, s32[16,768]{1,0:T(8,128)} %ice.1, ...), custom_call_target="tpu_custom_call" | custom-call | tf_op jit(solution)/shard_map/pack/pallas_call | solution.py:288
  1.8 3.0 %collective-permute-start = (f32[40,768]{1,0:T(8,128)S(1)}, f32[40,768]{1,0:T(8,128)S(1)}, u32[]{:S(2)}, u32[]{:S(2)}) collective-permute-start(f32[40,768]{1,0:T(8,128)S(1)} %get-tuple-element.19), channel_id=1, source_target_pairs={{0,2},{2,0},{4,6},{6,4},{8,10},{10,8},{12,14},{14,12},{1,3},{3,1},... | collective-permute-start | bytes 368648 | tf_op jit(solution)/shard_map/ppermute | solution.py:315
  4.8 0.0 collective-permute-start.1
  4.8 0.5 %collective-permute-start.2 = (f32[64,128]{1,0:T(8,128)S(1)}, f32[64,128]{1,0:T(8,128)S(1)}, u32[]{:S(2)}, u32[]{:S(2)}) collective-permute-start(f32[64,128]{1,0:T(8,128)S(1)} %get-tuple-element.21), channel_id=1, source_target_pairs={{0,1},{1,0},{2,3},{3,2},{4,5},{5,4},{6,7},{7,6},{8,9},{9,8},{10,11... | collective-permute-start | bytes 98312 | tf_op jit(solution)/shard_map/ppermute | solution.py:317
  5.3 0.9 %collective-permute-done.2.side = f32[64,128]{1,0:T(8,128)S(1)} collective-permute-done((f32[64,128]{1,0:T(8,128)S(1)}, f32[64,128]{1,0:T(8,128)S(1)}, u32[]{:S(2)}, u32[]{:S(2)}) %collective-permute-start.2) | collective-permute-done | bytes 32800 | tf_op jit(solution)/shard_map/ppermute | solution.py:317
  6.1 3.8 %collective-permute-done.from_x = f32[40,768]{1,0:T(8,128)S(1)} collective-permute-done((f32[40,768]{1,0:T(8,128)S(1)}, f32[40,768]{1,0:T(8,128)S(1)}, u32[]{:S(2)}, u32[]{:S(2)}) %collective-permute-start) | collective-permute-done | bytes 122912 | tf_op jit(solution)/shard_map/ppermute | solution.py:315
  10.0 0.0 collective-permute-done.1.from_z
  10.0 0.0 collective-permute-start.3
  10.0 0.5 %collective-permute-start.4 = (f32[40,768]{1,0:T(8,128)S(1)}, f32[40,768]{1,0:T(8,128)S(1)}, u32[]{:S(2)}, u32[]{:S(2)}) collective-permute-start(f32[40,768]{1,0:T(8,128)S(1)} %collective-permute-done.1.from_z), channel_id=1, source_target_pairs={{0,1},{1,0},{2,3},{3,2},{4,5},{5,4},{6,7},{7,6},{8,9},{9,8},{10,11... | collective-permute-start | bytes 368648 | tf_op jit(solution)/shard_map/ppermute | solution.py:320
  10.5 0.8 %collective-permute-done.3.side_x = f32[40,768]{1,0:T(8,128)S(1)} collective-permute-done((f32[40,768]{1,0:T(8,128)S(1)}, f32[40,768]{1,0:T(8,128)S(1)}, u32[]{:S(2)}, u32[]{:S(2)}) %collective-permute-start.3) | collective-permute-done | bytes 122912 | tf_op jit(solution)/shard_map/ppermute | solution.py:319
  11.3 0.2 collective-permute-done.4.side_z
  11.5 0.0 copy-done
  11.5 1.8 %leg.1 = (f32[2,16,768]{2,1,0:T(8,128)S(1)}, f32[16,768]{1,0:T(8,128)S(1)}, f32[16,256]{1,0:T(8,128)S(1)}) custom-call(f32[112,128]{1,0:T(8,128)S(1)} %get-tuple-element.17.coefficients, f32[4,16,768]{2,1,0:T(8,128)S(1)} %get-tuple-element.18.fields, f32[2,16,768]{2,1,0:T(8,128)S(1)} %copy-done, f32[40,768]{1,0:T(8,128)S(1)} %collective-permute-done.from_x, ...), custom_call_target="tpu_custom_call" | custom-call | tf_op jit(solution)/shard_map/leg/pallas_call | solution.py:325
  13.4 12.3 %all_to_all.11 = f32[16,1,256]{2,1,0:T(1,128)S(1)} all-to-all(f32[16,1,256]{2,1,0:T(1,128)S(1)} %copy.10), channel_id=1, replica_groups=mesh['grp'=2,'gx'=8,'gy'=2] {'gx','gy'}, dimensions={0} | all-to-all | bytes 32768 | tf_op jit(solution)/shard_map/all_to_all | solution.py:339
  25.6 0.8 %scale.1 = (f32[16,768]{1,0:T(8,128)}, f32[1,1]{1,0:T(1,128)}, f32[2,16,768]{2,1,0:T(8,128)}) custom-call(f32[16,256]{1,0:T(8,128)S(1)} %bitcast.5, f32[16,768]{1,0:T(8,128)S(1)} %get-tuple-element.26.gradient, f32[2,16,768]{2,1,0:T(8,128)S(1)} %get-tuple-element.27.held_multiplier), custom_call_target="tpu_custom_call" | custom-call | tf_op jit(solution)/shard_map/scale/pallas_call | solution.py:340
  (2 shorter events, 0.0 us)
Async XLA Ops:
  0.6 10.9 %copy-start = (f32[2,16,768]{2,1,0:T(8,128)S(1)}, f32[2,16,768]{2,1,0:T(8,128)}, u32[]{:S(2)}) copy-start(f32[2,16,768]{2,1,0:T(8,128)} %velocity.1) | copy-start | bytes 294916
  1.8 8.2 %collective-permute-start = (f32[40,768]{1,0:T(8,128)S(1)}, f32[40,768]{1,0:T(8,128)S(1)}, u32[]{:S(2)}, u32[]{:S(2)}) collective-permute-start(f32[40,768]{1,0:T(8,128)S(1)} %get-tuple-element.19), channel_id=1, source_target_pairs={{0,2},{2,0},{4,6},{6,4},{8,10},{10,8},{12,14},{14,12},{1,3},{3,1},... | collective-permute-start | bytes 368648 | tf_op jit(solution)/shard_map/ppermute | solution.py:315
  4.8 5.2 %collective-permute-start.1 = (f32[40,768]{1,0:T(8,128)S(1)}, f32[40,768]{1,0:T(8,128)S(1)}, u32[]{:S(2)}, u32[]{:S(2)}) collective-permute-start(f32[40,768]{1,0:T(8,128)S(1)} %get-tuple-element.20), channel_id=1, source_target_pairs={{2,4},{3,5},{4,2},{5,3},{6,8},{7,9},{8,6},{9,7},{10,12},{11,13},{1... | collective-permute-start | bytes 368648 | tf_op jit(solution)/shard_map/ppermute | solution.py:316
  4.8 1.4 %collective-permute-start.2 = (f32[64,128]{1,0:T(8,128)S(1)}, f32[64,128]{1,0:T(8,128)S(1)}, u32[]{:S(2)}, u32[]{:S(2)}) collective-permute-start(f32[64,128]{1,0:T(8,128)S(1)} %get-tuple-element.21), channel_id=1, source_target_pairs={{0,1},{1,0},{2,3},{3,2},{4,5},{5,4},{6,7},{7,6},{8,9},{9,8},{10,11... | collective-permute-start | bytes 98312 | tf_op jit(solution)/shard_map/ppermute | solution.py:317
  10.0 1.3 %collective-permute-start.3 = (f32[40,768]{1,0:T(8,128)S(1)}, f32[40,768]{1,0:T(8,128)S(1)}, u32[]{:S(2)}, u32[]{:S(2)}) collective-permute-start(f32[40,768]{1,0:T(8,128)S(1)} %collective-permute-done.from_x), channel_id=1, source_target_pairs={{0,1},{1,0},{2,3},{3,2},{4,5},{5,4},{6,7},{7,6},{8,9},{9,8},{10,11... | collective-permute-start | bytes 368648 | tf_op jit(solution)/shard_map/ppermute | solution.py:319
  10.0 1.5 %collective-permute-start.4 = (f32[40,768]{1,0:T(8,128)S(1)}, f32[40,768]{1,0:T(8,128)S(1)}, u32[]{:S(2)}, u32[]{:S(2)}) collective-permute-start(f32[40,768]{1,0:T(8,128)S(1)} %collective-permute-done.1.from_z), channel_id=1, source_target_pairs={{0,1},{1,0},{2,3},{3,2},{4,5},{5,4},{6,7},{7,6},{8,9},{9,8},{10,11... | collective-permute-start | bytes 368648 | tf_op jit(solution)/shard_map/ppermute | solution.py:320

commit v5 on v4

--- a/solution.py
+++ b/solution.py
@@ -22,7 +22,7 @@
 
 def pack_kernel(
     bounds, misfit, visc, friction, ice, grounded,
-    fields, coefficients, x_send, z_send, side_send,
+    fields, coefficients, x_send, z_send, side_send, x_corner, z_corner,
     levels, visc_in, friction_in, ice_in, grounded_in, sems,
 ):
     copies = [
@@ -57,6 +57,8 @@
         side_send[rows * n : rows * n + rows, :] = jnp.where(
             left, fields[n, :, cols - LANES :], fields[n, :, :LANES]
         )
+    for source, target in ((x_send, x_corner), (z_send, z_corner)):
+        target[...] = jnp.where(left, source[:, cols - LANES :], source[:, :LANES])
     copies[5].wait()
     for sweep in range(2):
         lower = jnp.full((8, LANES), levels[2 * sweep])
@@ -117,7 +119,7 @@
     for received, partner, is_above in ((from_x, side_x, jnp.logical_not(low_half)), (from_z, side_z, low_half)):
         near = jnp.where(is_above, RIM - 8, RIM + rows)
         far = jnp.where(is_above, 0, RIM + rows + 8)
-        edge = jnp.where(left, partner[:, :LANES], partner[:, cols - LANES :])
+        edge = partner[...]
         for n in range(4):
             spread(received, 8 * n, 8, edge[8 * n : 8 * n + 8], targets[n], near)
             spread(received, 32 + 2 * n, 2, edge[32 + 2 * n : 34 + 2 * n], targets[n], far)
@@ -285,7 +287,7 @@
     params = pltpu.CompilerParams(vmem_limit_bytes=32 * 1024 * 1024)
 
     held = pl.BlockSpec(memory_space=pltpu.HBM)
-    fields, coefficients, x_send, z_send, side_send = pl.pallas_call(
+    fields, coefficients, x_send, z_send, side_send, x_corner, z_corner = pl.pallas_call(
         pack_kernel,
         out_shape=(
             shaped((4, rows, cols), F32),
@@ -293,9 +295,11 @@
             shaped((4 * RIM, cols), F32),
             shaped((4 * RIM, cols), F32),
             shaped((4 * rows, LANES), F32),
+            shaped((4 * RIM, LANES), F32),
+            shaped((4 * RIM, LANES), F32),
         ),
         in_specs=[held] * 6,
-        out_specs=[whole] * 5,
+        out_specs=[whole] * 7,
         scratch_shapes=[
             pltpu.SMEM((4,), F32),
             pltpu.VMEM((rows, cols), F32),
@@ -315,9 +319,8 @@
     from_x = lax.ppermute(x_send, "gx", x_pairs)
     from_z = lax.ppermute(z_send, AXES, z_pairs)
     side = lax.ppermute(side_send, "gy", swap)
-    from_x, from_z, side = lax.optimization_barrier((from_x, from_z, side))
-    side_x = lax.ppermute(from_x, "gy", swap)
-    side_z = lax.ppermute(from_z, "gy", swap)
+    side_x = lax.ppermute(x_corner, AXES, [(2 * i + c, 2 * j + 1 - c) for i, j in x_pairs for c in (0, 1)])
+    side_z = lax.ppermute(z_corner, AXES, [(i, j ^ 1 if 1 < i < 2 * gx_size - 2 else j) for i, j in z_pairs])
 
     fine = pltpu.VMEM((8 * total, LANES), F32)
     coarse = pltpu.VMEM((4 * total, LANES), F32)

time: 26.6 us -> 25.8 us (0.970)
  waiting for transfers between devices: 5.7 us -> 2.98 us
  starting transfers between devices: 4.02 us -> 6.16 us
  blocking collectives: 12.3 us -> 12 us
    ppermute x1, waiting for transfers between devices: 3.83 us -> 0.01 us  [body(): from_x = lax.ppermute(x_send, 'gx', x_pairs)]
    ppermute x2, starting transfers between devices: 0.51 us -> 2.65 us  [the longest x1 2.64 us: body(): lax.ppermute(x_corner, AXES, [(2 * i + c, 2 * j + 1 - c) for i, j in x_pa...]
    ppermute x2, waiting for transfers between devices: 1 us -> 2.97 us  [the longest x1 2.96 us: body(): lax.ppermute(x_corner, AXES, [(2 * i + c, 2 * j + 1 - c) for i, j in x_pa...]
    ppermute x1, waiting for transfers between devices: 0.87 us -> 0.01 us  [body(): side = lax.ppermute(side_send, 'gy', swap)]
    all_to_all x1, blocking collectives: 12.3 us -> 12 us  [body(): gathered = lax.all_to_all(sums, AXES, 0, 0, tiled=True)]
  transfers between devices with their start and end apart: 5 -> 5, of which waited for: 4 -> 1; matrix products, arithmetic and copies ran while one was open for 0% -> 0% of each run, Pallas kernels for 0% -> 0%
where the time goes in v5:
time: 25.8 us; the launch traced here: 25.6 us
  blocking collectives  12 us (47%)
  starting transfers between devices  6.16 us (24%)
  Pallas kernels  3.74 us (14%)
  waiting for transfers between devices  2.98 us (12%)
  between operations  0.68 us (3%)
    all_to_all x1, blocking collectives, body(): gathered = lax.all_to_all(sums, AXES, 0, 0, tiled=True)  12 us
    ppermute x1, starting transfers between devices, body(): from_x = lax.ppermute(x_send, 'gx', x_pairs)  3 us
    ppermute x1, waiting for transfers between devices, body(): lax.ppermute(x_corner, AXES, [(2 * i + c, 2 * j + 1 - c) for i, j in x_pa...  2.96 us
    ppermute x1, starting transfers between devices, body(): lax.ppermute(x_corner, AXES, [(2 * i + c, 2 * j + 1 - c) for i, j in x_pa...  2.64 us
    pallas_call x1, Pallas kernels, body(): pl.pallas_call(main_kernel, out_shape=(pltpu.VMEM((2, rows, cols), F32),...  1.84 us
    pallas_call x1, Pallas kernels, body(): pl.pallas_call(pack_kernel, out_shape=(shaped((4, rows, cols), F32), shap...  1.11 us
    pallas_call x1, Pallas kernels, body(): pl.pallas_call(functools.partial(scale_kernel, nodes), out_shape=(pltpu.H...  0.79 us
  transfers between devices with their start and end apart: 5, of which 1 were waited for; matrix products, arithmetic and copies ran while one was open for 0% of the time, Pallas kernels for 0%

profile of v5, /device:TPU:0, one launch (start us, length us, event | category | flops | bytes accessed | tf_op | source)
XLA Modules:
  0.0 25.6 jit_solution(5059186285389318544)
XLA Ops:
  0.6 0.0 copy-start
  0.6 1.1 %pack.1 = (f32[4,16,768]{2,1,0:T(8,128)S(1)}, f32[112,128]{1,0:T(8,128)S(1)}, f32[40,768]{1,0:T(8,128)S(1)}, f32[40,768]{1,0:T(8,128)S(1)}, f32[64,128]{1,0:T(8,...) custom-call(f32[4]{0:T(128)} %bounds.1, f32[2,16,768]{2,1,0:T(8,128)} %misfit.1, f32[16,768]{1,0:T(8,128)} %visc.1, ...), custom_call_target="tpu_custom_call" | custom-call | tf_op jit(solution)/shard_map/pack/pallas_call | solution.py:290
  1.8 3.0 %collective-permute-start = (f32[40,768]{1,0:T(8,128)S(1)}, f32[40,768]{1,0:T(8,128)S(1)}, u32[]{:S(2)}, u32[]{:S(2)}) collective-permute-start(f32[40,768]{1,0:T(8,128)S(1)} %get-tuple-element.18), channel_id=1, source_target_pairs={{0,2},{2,0},{4,6},{6,4},{8,10},{10,8},{12,14},{14,12},{1,3},{3,1},... | collective-permute-start | bytes 368648 | tf_op jit(solution)/shard_map/ppermute | solution.py:319
  4.8 0.0 collective-permute-start.1
  4.8 0.5 %collective-permute-start.2 = (f32[64,128]{1,0:T(8,128)S(1)}, f32[64,128]{1,0:T(8,128)S(1)}, u32[]{:S(2)}, u32[]{:S(2)}) collective-permute-start(f32[64,128]{1,0:T(8,128)S(1)} %get-tuple-element.20), channel_id=1, source_target_pairs={{0,1},{1,0},{2,3},{3,2},{4,5},{5,4},{6,7},{7,6},{8,9},{9,8},{10,11... | collective-permute-start | bytes 98312 | tf_op jit(solution)/shard_map/ppermute | solution.py:321
  5.3 2.6 %collective-permute-start.3 = (f32[40,128]{1,0:T(8,128)S(1)}, f32[40,128]{1,0:T(8,128)S(1)}, u32[]{:S(2)}, u32[]{:S(2)}) collective-permute-start(f32[40,128]{1,0:T(8,128)S(1)} %get-tuple-element.21), channel_id=1, source_target_pairs={{0,3},{1,2},{2,1},{3,0},{4,7},{5,6},{6,5},{7,4},{8,11},{9,10},{10,... | collective-permute-start | bytes 61448 | tf_op jit(solution)/shard_map/ppermute | solution.py:322
  7.9 0.0 collective-permute-start.4
  7.9 3.0 %collective-permute-done.3.side_x = f32[40,128]{1,0:T(8,128)S(1)} collective-permute-done((f32[40,128]{1,0:T(8,128)S(1)}, f32[40,128]{1,0:T(8,128)S(1)}, u32[]{:S(2)}, u32[]{:S(2)}) %collective-permute-start.3) | collective-permute-done | bytes 20512 | tf_op jit(solution)/shard_map/ppermute | solution.py:322
  10.9 0.0 collective-permute-done.4.side_z
  10.9 0.0 collective-permute-done.2.side
  10.9 0.0 collective-permute-done.from_x
  10.9 0.0 collective-permute-done.1.from_z
  10.9 0.0 copy-done
  10.9 1.8 %leg.1 = (f32[2,16,768]{2,1,0:T(8,128)S(1)}, f32[16,768]{1,0:T(8,128)S(1)}, f32[16,256]{1,0:T(8,128)S(1)}) custom-call(f32[112,128]{1,0:T(8,128)S(1)} %get-tuple-element.16.coefficients, f32[4,16,768]{2,1,0:T(8,128)S(1)} %get-tuple-element.17.fields, f32[2,16,768]{2,1,0:T(8,128)S(1)} %copy-done, f32[40,768]{1,0:T(8,128)S(1)} %collective-permute-done.from_x, ...), custom_call_target="tpu_custom_call" | custom-call | tf_op jit(solution)/shard_map/leg/pallas_call | solution.py:328
  12.8 12.0 %all_to_all.11 = f32[16,1,256]{2,1,0:T(1,128)S(1)} all-to-all(f32[16,1,256]{2,1,0:T(1,128)S(1)} %copy.10), channel_id=1, replica_groups=mesh['grp'=2,'gx'=8,'gy'=2] {'gx','gy'}, dimensions={0} | all-to-all | bytes 32768 | tf_op jit(solution)/shard_map/all_to_all | solution.py:342
  24.8 0.8 %scale.1 = (f32[16,768]{1,0:T(8,128)}, f32[1,1]{1,0:T(1,128)}, f32[2,16,768]{2,1,0:T(8,128)}) custom-call(f32[16,256]{1,0:T(8,128)S(1)} %bitcast.5, f32[16,768]{1,0:T(8,128)S(1)} %get-tuple-element.24.gradient, f32[2,16,768]{2,1,0:T(8,128)S(1)} %get-tuple-element.25.held_multiplier), custom_call_target="tpu_custom_call" | custom-call | tf_op jit(solution)/shard_map/scale/pallas_call | solution.py:343
  (2 shorter events, 0.0 us)
Async XLA Ops:
  0.6 10.3 %copy-start = (f32[2,16,768]{2,1,0:T(8,128)S(1)}, f32[2,16,768]{2,1,0:T(8,128)}, u32[]{:S(2)}) copy-start(f32[2,16,768]{2,1,0:T(8,128)} %velocity.1) | copy-start | bytes 294916
  1.8 9.1 %collective-permute-start = (f32[40,768]{1,0:T(8,128)S(1)}, f32[40,768]{1,0:T(8,128)S(1)}, u32[]{:S(2)}, u32[]{:S(2)}) collective-permute-start(f32[40,768]{1,0:T(8,128)S(1)} %get-tuple-element.18), channel_id=1, source_target_pairs={{0,2},{2,0},{4,6},{6,4},{8,10},{10,8},{12,14},{14,12},{1,3},{3,1},... | collective-permute-start | bytes 368648 | tf_op jit(solution)/shard_map/ppermute | solution.py:319
  4.8 6.1 %collective-permute-start.1 = (f32[40,768]{1,0:T(8,128)S(1)}, f32[40,768]{1,0:T(8,128)S(1)}, u32[]{:S(2)}, u32[]{:S(2)}) collective-permute-start(f32[40,768]{1,0:T(8,128)S(1)} %get-tuple-element.19), channel_id=1, source_target_pairs={{2,4},{3,5},{4,2},{5,3},{6,8},{7,9},{8,6},{9,7},{10,12},{11,13},{1... | collective-permute-start | bytes 368648 | tf_op jit(solution)/shard_map/ppermute | solution.py:320
  4.8 6.1 %collective-permute-start.2 = (f32[64,128]{1,0:T(8,128)S(1)}, f32[64,128]{1,0:T(8,128)S(1)}, u32[]{:S(2)}, u32[]{:S(2)}) collective-permute-start(f32[64,128]{1,0:T(8,128)S(1)} %get-tuple-element.20), channel_id=1, source_target_pairs={{0,1},{1,0},{2,3},{3,2},{4,5},{5,4},{6,7},{7,6},{8,9},{9,8},{10,11... | collective-permute-start | bytes 98312 | tf_op jit(solution)/shard_map/ppermute | solution.py:321
  5.3 5.6 %collective-permute-start.3 = (f32[40,128]{1,0:T(8,128)S(1)}, f32[40,128]{1,0:T(8,128)S(1)}, u32[]{:S(2)}, u32[]{:S(2)}) collective-permute-start(f32[40,128]{1,0:T(8,128)S(1)} %get-tuple-element.21), channel_id=1, source_target_pairs={{0,3},{1,2},{2,1},{3,0},{4,7},{5,6},{6,5},{7,4},{8,11},{9,10},{10,... | collective-permute-start | bytes 61448 | tf_op jit(solution)/shard_map/ppermute | solution.py:322
  7.9 3.0 %collective-permute-start.4 = (f32[40,128]{1,0:T(8,128)S(1)}, f32[40,128]{1,0:T(8,128)S(1)}, u32[]{:S(2)}, u32[]{:S(2)}) collective-permute-start(f32[40,128]{1,0:T(8,128)S(1)} %get-tuple-element.22), channel_id=1, source_target_pairs={{2,5},{3,4},{4,3},{5,2},{6,9},{7,8},{8,7},{9,6},{10,13},{11,12},{1... | collective-permute-start | bytes 61448 | tf_op jit(solution)/shard_map/ppermute | solution.py:323

commit v6 on v5

--- a/solution.py
+++ b/solution.py
@@ -57,8 +57,17 @@
         side_send[rows * n : rows * n + rows, :] = jnp.where(
             left, fields[n, :, cols - LANES :], fields[n, :, :LANES]
         )
+    own_columns = lane_ids() // EDGE == lax.broadcasted_iota(jnp.int32, (8, LANES), 0)
     for source, target in ((x_send, x_corner), (z_send, z_corner)):
-        target[...] = jnp.where(left, source[:, cols - LANES :], source[:, :LANES])
+        for q in range(RIM // 2):
+            last, first = source[8 * q : 8 * q + 8, cols - LANES :], source[8 * q : 8 * q + 8, :LANES]
+            columns = jnp.where(
+                left,
+                pltpu.roll(last, EDGE, 1, stride=EDGE, stride_axis=0),
+                pltpu.roll(first, 0, 1, stride=EDGE, stride_axis=0),
+            )
+            target[q : q + 1, :] = jnp.sum(jnp.where(own_columns, columns, 0.0), axis=0, keepdims=True)
+        target[RIM // 2 :, :] = jnp.zeros((8 - RIM // 2, LANES), F32)
     copies[5].wait()
     for sweep in range(2):
         lower = jnp.full((8, LANES), levels[2 * sweep])
@@ -91,7 +100,7 @@
     coefficients, fields, velocity, from_x, from_z, side, side_x, side_z,
     multiplier, gradient, sums,
     fu, fv, kk, bb, cell, xu, xv, du, dv, ru, rv, cfu, cfv, ckk, cbb, ccell, cxu, cxv, cdu, cdv, mu, mv,
-    nxu, nxv, nu, nv, tu, tv,
+    nxu, nxv, nu, nv, tu, tv, cell_before, corner,
 ):
     rows, cols = gradient.shape
     total = rows + 2 * RIM
@@ -101,6 +110,7 @@
     left = lax.axis_index("gy") == 0
 
     next_, here_part, shifted_part = (nxu, nxv), (nu, nv), (tu, tv)
+    previous = here_part
 
     def spread(ref, base, height, side_block, target, first_row):
         blocks = [ref[base : base + height, LANES * j : LANES * j + LANES] for j in range(column_blocks)]
@@ -119,10 +129,14 @@
     for received, partner, is_above in ((from_x, side_x, jnp.logical_not(low_half)), (from_z, side_z, low_half)):
         near = jnp.where(is_above, RIM - 8, RIM + rows)
         far = jnp.where(is_above, 0, RIM + rows + 8)
-        edge = partner[...]
+        rolled = [pltpu.roll(partner[...], (LANES - EDGE * i) % LANES, 1) if i else partner[...] for i in range(8)]
+        for i in range(8):
+            columns = jnp.where(left, rolled[i], rolled[(i + 1) % 8])
+            corner[pl.ds(i, RIM // 2, stride=8), :] = columns[: RIM // 2]
+        edge = corner
         for n in range(4):
-            spread(received, 8 * n, 8, edge[8 * n : 8 * n + 8], targets[n], near)
-            spread(received, 32 + 2 * n, 2, edge[32 + 2 * n : 34 + 2 * n], targets[n], far)
+            spread(received, 8 * n, 8, edge[8 * n : 8 * n + 8, :], targets[n], near)
+            spread(received, 32 + 2 * n, 2, edge[32 + 2 * n : 34 + 2 * n, :], targets[n], far)
 
     lanes = lane_ids()
     column = 96 * lax.broadcasted_iota(jnp.int32, (8, LANES), 0) + lanes - EDGE
@@ -203,6 +217,66 @@
             x, old = old, x
         return x
 
+    def short_sweep(x, old, f, beta, stiff, table, count, rim, shift):
+        for row in range(count - 1):
+            put(cell_before, row, pltpu.roll(at(stiff, row), shift, 1))
+
+        def keep_both(n, row, value):
+            put(next_[n], row, shifted(value, shift))
+            put(previous[n], row, pltpu.roll(value, shift, 1))
+
+        def gradients(row):
+            u, v = at(x[0], row), at(x[1], row)
+            next_u, next_v = at(next_[0], row), at(next_[1], row)
+            last_u, last_v = at(previous[0], row), at(previous[1], row)
+            return (
+                (u + next_u, v + next_v, next_u - u, next_v - v),
+                (u + last_u, v + last_v, u - last_u, v - last_v),
+            )
+
+        def cells(row, one, two):
+            values = []
+            for stiff_, one_, two_ in zip((stiff, cell_before), one, two):
+                a, b = two_[0] - one_[0], two_[3] + one_[3]
+                c, d = two_[2] + one_[2], two_[1] - one_[1]
+                s = at(stiff_, row)
+                both = a + b
+                values.append((s * (both + a), s * (both + b), (0.5 * s) * (c + d)))
+            return values
+
+        inverse = at(coefficients, table)
+        for row in range(count):
+            for n in range(2):
+                value = at(f[n], row) * inverse
+                put(x[n], row, value)
+                keep_both(n, row, value)
+        for step in range(DEG - 1):
+            keep = at(coefficients, table + 1 + 2 * step)
+            gain = at(coefficients, table + 2 + 2 * step)
+            gains = (gain * above, gain * inside, gain * below)
+            low, high = step + 1, count - step - 1
+            here = gradients(low)
+            before = cells(low - 1, gradients(low - 1), here)
+            for row in range(low, high):
+                after = gradients(row + 1)
+                now = cells(row, here, after)
+                (xx0, yy0, xy0), (xx1, yy1, xy1) = (
+                    (p[0] - q[0], p[1] + q[1], (p[2] + q[2], p[2] - q[2])) for p, q in zip(before, now)
+                )
+                applied = ((xx0 - xy0[0]) + (xx1 + xy1[0]), (xy0[1] - yy0) + (xy1[1] + yy1))
+                part = gains[0 if row < rim else 2 if row >= count - rim else 1]
+                for n in range(2):
+                    value = at(x[n], row)
+                    change = value if step == 0 else value - at(old[n], row)
+                    left_over = (at(f[n], row) - at(beta, row) * value) - applied[n]
+                    value = value + keep * change + part * left_over
+                    put(old[n], row, value)
+                    if step < DEG - 2:
+                        keep_both(n, row, value)
+                here, before = after, now
+            x, old = old, x
+        return x
+
     stiffness(kk, cell, total, 1)
     x = sweep((xu, xv), (du, dv), (fu, fv), bb, cell, 0, total, RIM, 1)
     forces(x, cell, DEG, total - DEG, 1)
@@ -224,7 +298,7 @@
             pair = pair + pltpu.roll(pair, LANES - 1, 1)
             put(target, i, pair if scale is None else scale * pair)
     stiffness(ckk, ccell, coarse_rows, 2)
-    coarse_x = sweep((cxu, cxv), (cdu, cdv), (cfu, cfv), cbb, ccell, 2 * DEG - 1, coarse_rows, coarse_rim, 2)
+    coarse_x = short_sweep((cxu, cxv), (cdu, cdv), (cfu, cfv), cbb, ccell, 2 * DEG - 1, coarse_rows, coarse_rim, 2)
 
     for i in range(rows // 2):
         for fine, coarse, target in zip(x, coarse_x, (mu, mv)):
@@ -295,8 +369,8 @@
             shaped((4 * RIM, cols), F32),
             shaped((4 * RIM, cols), F32),
             shaped((4 * rows, LANES), F32),
-            shaped((4 * RIM, LANES), F32),
-            shaped((4 * RIM, LANES), F32),
+            shaped((8, LANES), F32),
+            shaped((8, LANES), F32),
         ),
         in_specs=[held] * 6,
         out_specs=[whole] * 7,
@@ -334,7 +408,7 @@
         ),
         in_specs=[whole] * 8,
         out_specs=[whole] * 3,
-        scratch_shapes=[fine] * 11 + [coarse] * 9 + [owned] * 2 + [fine] * 6,
+        scratch_shapes=[fine] * 11 + [coarse] * 9 + [owned] * 2 + [fine] * 6 + [coarse, pltpu.VMEM((4 * RIM, LANES), F32)],
         compiler_params=params,
         name="leg",
     )(coefficients, fields, velocity, from_x, from_z, side, side_x, side_z)

time: 25.8 us -> 25.3 us (0.981)
  waiting for transfers between devices: 2.98 us -> 2.32 us
    ppermute x1, waiting for transfers between devices: 2.96 us -> 2.31 us  [body(): lax.ppermute(x_corner, AXES, [(2 * i + c, 2 * j + 1 - c) for i, j in x_pa...]
where the time goes in v6:
time: 25.3 us; the launch traced here: 25.1 us
  blocking collectives  12.1 us (48%)
  starting transfers between devices  6.16 us (24%)
  Pallas kernels  3.84 us (15%)
  waiting for transfers between devices  2.32 us (9%)
  between operations  0.68 us (3%)
    all_to_all x1, blocking collectives, body(): gathered = lax.all_to_all(sums, AXES, 0, 0, tiled=True)  12.1 us
    ppermute x1, starting transfers between devices, body(): from_x = lax.ppermute(x_send, 'gx', x_pairs)  3 us
    ppermute x1, starting transfers between devices, body(): lax.ppermute(x_corner, AXES, [(2 * i + c, 2 * j + 1 - c) for i, j in x_pa...  2.64 us
    ppermute x1, waiting for transfers between devices, body(): lax.ppermute(x_corner, AXES, [(2 * i + c, 2 * j + 1 - c) for i, j in x_pa...  2.31 us
    pallas_call x1, Pallas kernels, body(): pl.pallas_call(main_kernel, out_shape=(pltpu.VMEM((2, rows, cols), F32),...  1.86 us
    pallas_call x1, Pallas kernels, body(): pl.pallas_call(pack_kernel, out_shape=(shaped((4, rows, cols), F32), shap...  1.19 us
    pallas_call x1, Pallas kernels, body(): pl.pallas_call(functools.partial(scale_kernel, nodes), out_shape=(pltpu.H...  0.79 us
    ppermute x1, starting transfers between devices, body(): side = lax.ppermute(side_send, 'gy', swap)  0.51 us
  transfers between devices with their start and end apart: 5, of which 1 were waited for; matrix products, arithmetic and copies ran while one was open for 0% of the time, Pallas kernels for 0%

profile of v6, /device:TPU:0, one launch (start us, length us, event | category | flops | bytes accessed | tf_op | source)
XLA Modules:
  0.0 25.1 jit_solution(3288703718947986074)
XLA Ops:
  0.6 0.0 copy-start
  0.6 1.2 %pack.1 = (f32[4,16,768]{2,1,0:T(8,128)S(1)}, f32[112,128]{1,0:T(8,128)S(1)}, f32[40,768]{1,0:T(8,128)S(1)}, f32[40,768]{1,0:T(8,128)S(1)}, f32[64,128]{1,0:T(8,...) custom-call(f32[4]{0:T(128)} %bounds.1, f32[2,16,768]{2,1,0:T(8,128)} %misfit.1, f32[16,768]{1,0:T(8,128)} %visc.1, ...), custom_call_target="tpu_custom_call" | custom-call | tf_op jit(solution)/shard_map/pack/pallas_call | solution.py:364
  1.8 3.0 %collective-permute-start = (f32[40,768]{1,0:T(8,128)S(1)}, f32[40,768]{1,0:T(8,128)S(1)}, u32[]{:S(2)}, u32[]{:S(2)}) collective-permute-start(f32[40,768]{1,0:T(8,128)S(1)} %get-tuple-element.18), channel_id=1, source_target_pairs={{0,2},{2,0},{4,6},{6,4},{8,10},{10,8},{12,14},{14,12},{1,3},{3,1},... | collective-permute-start | bytes 368648 | tf_op jit(solution)/shard_map/ppermute | solution.py:393
  4.8 0.0 collective-permute-start.1
  4.8 0.5 %collective-permute-start.2 = (f32[64,128]{1,0:T(8,128)S(1)}, f32[64,128]{1,0:T(8,128)S(1)}, u32[]{:S(2)}, u32[]{:S(2)}) collective-permute-start(f32[64,128]{1,0:T(8,128)S(1)} %get-tuple-element.20), channel_id=1, source_target_pairs={{0,1},{1,0},{2,3},{3,2},{4,5},{5,4},{6,7},{7,6},{8,9},{9,8},{10,11... | collective-permute-start | bytes 98312 | tf_op jit(solution)/shard_map/ppermute | solution.py:395
  5.4 2.6 %collective-permute-start.3 = (f32[8,128]{1,0:T(8,128)S(1)}, f32[8,128]{1,0:T(8,128)S(1)}, u32[]{:S(2)}, u32[]{:S(2)}) collective-permute-start(f32[8,128]{1,0:T(8,128)S(1)} %get-tuple-element.21), channel_id=1, source_target_pairs={{0,3},{1,2},{2,1},{3,0},{4,7},{5,6},{6,5},{7,4},{8,11},{9,10},{10,... | collective-permute-start | bytes 12296 | tf_op jit(solution)/shard_map/ppermute | solution.py:396
  8.0 0.0 collective-permute-start.4
  8.0 2.3 %collective-permute-done.3.side_x = f32[8,128]{1,0:T(8,128)S(1)} collective-permute-done((f32[8,128]{1,0:T(8,128)S(1)}, f32[8,128]{1,0:T(8,128)S(1)}, u32[]{:S(2)}, u32[]{:S(2)}) %collective-permute-start.3) | collective-permute-done | bytes 4128 | tf_op jit(solution)/shard_map/ppermute | solution.py:396
  10.3 0.0 collective-permute-done.4.side_z
  10.3 0.0 collective-permute-done.2.side
  10.3 0.0 collective-permute-done.from_x
  10.3 0.0 collective-permute-done.1.from_z
  10.3 0.0 copy-done
  10.3 1.9 %leg.1 = (f32[2,16,768]{2,1,0:T(8,128)S(1)}, f32[16,768]{1,0:T(8,128)S(1)}, f32[16,256]{1,0:T(8,128)S(1)}) custom-call(f32[112,128]{1,0:T(8,128)S(1)} %get-tuple-element.16.coefficients, f32[4,16,768]{2,1,0:T(8,128)S(1)} %get-tuple-element.17.fields, f32[2,16,768]{2,1,0:T(8,128)S(1)} %copy-done, f32[40,768]{1,0:T(8,128)S(1)} %collective-permute-done.from_x, ...), custom_call_target="tpu_custom_call" | custom-call | tf_op jit(solution)/shard_map/leg/pallas_call | solution.py:402
  12.2 12.1 %all_to_all.11 = f32[16,1,256]{2,1,0:T(1,128)S(1)} all-to-all(f32[16,1,256]{2,1,0:T(1,128)S(1)} %copy.10), channel_id=1, replica_groups=mesh['grp'=2,'gx'=8,'gy'=2] {'gx','gy'}, dimensions={0} | all-to-all | bytes 32768 | tf_op jit(solution)/shard_map/all_to_all | solution.py:416
  24.4 0.8 %scale.1 = (f32[16,768]{1,0:T(8,128)}, f32[1,1]{1,0:T(1,128)}, f32[2,16,768]{2,1,0:T(8,128)}) custom-call(f32[16,256]{1,0:T(8,128)S(1)} %bitcast.5, f32[16,768]{1,0:T(8,128)S(1)} %get-tuple-element.24.gradient, f32[2,16,768]{2,1,0:T(8,128)S(1)} %get-tuple-element.25.held_multiplier), custom_call_target="tpu_custom_call" | custom-call | tf_op jit(solution)/shard_map/scale/pallas_call | solution.py:417
  (2 shorter events, 0.0 us)
Async XLA Ops:
  0.6 9.7 %copy-start = (f32[2,16,768]{2,1,0:T(8,128)S(1)}, f32[2,16,768]{2,1,0:T(8,128)}, u32[]{:S(2)}) copy-start(f32[2,16,768]{2,1,0:T(8,128)} %velocity.1) | copy-start | bytes 294916
  1.8 8.5 %collective-permute-start = (f32[40,768]{1,0:T(8,128)S(1)}, f32[40,768]{1,0:T(8,128)S(1)}, u32[]{:S(2)}, u32[]{:S(2)}) collective-permute-start(f32[40,768]{1,0:T(8,128)S(1)} %get-tuple-element.18), channel_id=1, source_target_pairs={{0,2},{2,0},{4,6},{6,4},{8,10},{10,8},{12,14},{14,12},{1,3},{3,1},... | collective-permute-start | bytes 368648 | tf_op jit(solution)/shard_map/ppermute | solution.py:393
  4.8 5.5 %collective-permute-start.1 = (f32[40,768]{1,0:T(8,128)S(1)}, f32[40,768]{1,0:T(8,128)S(1)}, u32[]{:S(2)}, u32[]{:S(2)}) collective-permute-start(f32[40,768]{1,0:T(8,128)S(1)} %get-tuple-element.19), channel_id=1, source_target_pairs={{2,4},{3,5},{4,2},{5,3},{6,8},{7,9},{8,6},{9,7},{10,12},{11,13},{1... | collective-permute-start | bytes 368648 | tf_op jit(solution)/shard_map/ppermute | solution.py:394
  4.8 5.5 %collective-permute-start.2 = (f32[64,128]{1,0:T(8,128)S(1)}, f32[64,128]{1,0:T(8,128)S(1)}, u32[]{:S(2)}, u32[]{:S(2)}) collective-permute-start(f32[64,128]{1,0:T(8,128)S(1)} %get-tuple-element.20), channel_id=1, source_target_pairs={{0,1},{1,0},{2,3},{3,2},{4,5},{5,4},{6,7},{7,6},{8,9},{9,8},{10,11... | collective-permute-start | bytes 98312 | tf_op jit(solution)/shard_map/ppermute | solution.py:395
  5.4 5.0 %collective-permute-start.3 = (f32[8,128]{1,0:T(8,128)S(1)}, f32[8,128]{1,0:T(8,128)S(1)}, u32[]{:S(2)}, u32[]{:S(2)}) collective-permute-start(f32[8,128]{1,0:T(8,128)S(1)} %get-tuple-element.21), channel_id=1, source_target_pairs={{0,3},{1,2},{2,1},{3,0},{4,7},{5,6},{6,5},{7,4},{8,11},{9,10},{10,... | collective-permute-start | bytes 12296 | tf_op jit(solution)/shard_map/ppermute | solution.py:396
  8.0 2.3 %collective-permute-start.4 = (f32[8,128]{1,0:T(8,128)S(1)}, f32[8,128]{1,0:T(8,128)S(1)}, u32[]{:S(2)}, u32[]{:S(2)}) collective-permute-start(f32[8,128]{1,0:T(8,128)S(1)} %get-tuple-element.22), channel_id=1, source_target_pairs={{2,5},{3,4},{4,3},{5,2},{6,9},{7,8},{8,7},{9,6},{10,13},{11,12},{1... | collective-permute-start | bytes 12296 | tf_op jit(solution)/shard_map/ppermute | solution.py:397

commit v7 on v5

v7 whole, which is shorter than its diff:
```python
import functools

import jax
import jax.numpy as jnp
from jax import lax
from jax.experimental import pallas as pl
from jax.experimental.pallas import tpu as pltpu
from jax.sharding import PartitionSpec as P

DEG = 4
LANES = 128
SEGS = 8
RIM = 10
EDGE = 16
F32 = jnp.float32
AXES = ("gx", "gy")


def lane_ids():
    return lax.broadcasted_iota(jnp.int32, (8, LANES), 1)


def pack_kernel(
    bounds, misfit, visc, friction, ice, grounded,
    fields, coefficients, x_send, z_send, side_send, x_corner, z_corner,
    levels, visc_in, friction_in, ice_in, grounded_in, sems,
):
    copies = [
        pltpu.make_async_copy(source, target, sems.at[n])
        for n, (source, target) in enumerate((
            (misfit, fields.at[pl.ds(0, 2)]),
            (visc, visc_in),
            (ice, ice_in),
            (friction, friction_in),
            (grounded, grounded_in),
            (bounds, levels),
        ))
    ]
    for copy in copies:
        copy.start()
    rows, cols = visc.shape
    left = lax.axis_index("gy") == 0
    at, last_at = lax.axis_index("gx"), lax.axis_size("gx") - 1
    low_half = at % 2 == 0
    at_end = (at == 0) | (at == last_at)
    for copy in copies[:5]:
        copy.wait()
    fields[2] = visc_in[...] * ice_in[...].astype(F32)
    fields[3] = friction_in[...] * grounded_in[...].astype(F32)
    for n in range(4):
        last, first = fields[n, rows - 8 :, :], fields[n, :8, :]
        x_send[8 * n : 8 * n + 8, :] = jnp.where(low_half, last, first)
        z_send[8 * n : 8 * n + 8, :] = jnp.where(at_end, 0.0, jnp.where(low_half, first, last))
        last, first = fields[n, rows - 10 : rows - 8, :], fields[n, 8:10, :]
        x_send[32 + 2 * n : 34 + 2 * n, :] = jnp.where(low_half, last, first)
        z_send[32 + 2 * n : 34 + 2 * n, :] = jnp.where(at_end, 0.0, jnp.where(low_half, first, last))
        side_send[rows * n : rows * n + rows, :] = jnp.where(
            left, fields[n, :, cols - LANES :], fields[n, :, :LANES]
        )
    own_columns = lane_ids() // EDGE == lax.broadcasted_iota(jnp.int32, (8, LANES), 0)
    for source, target in ((x_send, x_corner), (z_send, z_corner)):
        for q in range(RIM // 2):
            last, first = source[8 * q : 8 * q + 8, cols - LANES :], source[8 * q : 8 * q + 8, :LANES]
            columns = jnp.where(
                left,
                pltpu.roll(last, EDGE, 1, stride=EDGE, stride_axis=0),
                pltpu.roll(first, 0, 1, stride=EDGE, stride_axis=0),
            )
            target[q : q + 1, :] = jnp.sum(jnp.where(own_columns, columns, 0.0), axis=0, keepdims=True)
        target[RIM // 2 :, :] = jnp.zeros((8 - RIM // 2, LANES), F32)
    copies[5].wait()
    for sweep in range(2):
        lower = jnp.full((8, LANES), levels[2 * sweep])
        upper = jnp.full((8, LANES), levels[2 * sweep + 1])
        middle = 0.5 * (upper + lower)
        half = 0.5 * (upper - lower)
        spread = middle / half
        factor = 1.0 / spread
        values = [1.0 / middle]
        for step in range(DEG - 1):
            factor_next = 1.0 / (2.0 * spread - factor)
            values += [factor_next * factor, 2.0 * factor_next / half]
            factor = factor_next
        for n, value in enumerate(values):
            row = 8 * (sweep * (2 * DEG - 1) + n)
            coefficients[row : row + 8, :] = value


class Rows:
    def __init__(self, *pieces):
        self.pieces = pieces

    def place(self, row):
        for first, end, ref, start in self.pieces:
            if first <= row < end:
                return ref, slice(8 * (row - first + start), 8 * (row - first + start) + 8)
        raise IndexError(row)


def at(array, row):
    ref, place = array.place(row)
    return ref[place, :]


def put(array, row, value):
    ref, place = array.place(row)
    ref[place, :] = value


def to_left(value, shift):
    return pltpu.roll(value, LANES - shift, 1)


def to_right(value, shift):
    return pltpu.roll(value, shift, 1)


def spread(ref, base, height, left, side_block, target, first_row):
    blocks = [ref[base : base + height, LANES * j : LANES * j + LANES] for j in range(ref.shape[1] // LANES)]
    zero = jnp.zeros((height, LANES), F32)
    if side_block is None:
        blocks = [zero] + blocks + [zero]
    else:
        blocks = [jnp.where(left, zero, side_block)] + blocks + [jnp.where(left, side_block, zero)]
    lanes = lax.broadcasted_iota(jnp.int32, (height, LANES), 1)
    for s in range(SEGS):
        start = 96 * s - EDGE
        first = start // LANES
        offset = start - LANES * first
        merged = jnp.where(lanes >= offset, blocks[first + 1], blocks[first + 2])
        target[pl.ds(first_row * 8 + s, height, stride=8), :] = to_left(merged, offset)


def inside_columns(left, cols):
    column = 96 * lax.broadcasted_iota(jnp.int32, (8, LANES), 0) + lane_ids() - EDGE
    return jnp.where(left, (column >= 0).astype(F32), (column < cols).astype(F32))


def own_columns():
    lanes = lane_ids()
    return ((lanes >= EDGE) & (lanes < LANES - EDGE)).astype(F32)


def stiffness(visc, target, first, last, shift):
    paired = None
    for row in range(first, last + 1):
        k = at(visc, row)
        now = k + to_left(k, shift)
        if row > first:
            put(target, row - 1, 0.125 * (paired + now))
        paired = now


def edge_gradients(here, there):
    return here[0] + there[0], here[1] + there[1], there[0] - here[0], there[1] - here[1]


def cell_forces(s, one, two):
    a, b = two[0] - one[0], two[3] + one[3]
    c, d = two[2] + one[2], two[1] - one[1]
    both = a + b
    return s * (both + a), s * (both + b), (0.5 * s) * (c + d)


def forces(x, following, stiff, near, far, low, high, shift):
    def gradients(row):
        return edge_gradients([at(part, row) for part in x], [at(part, row) for part in following])

    here = gradients(low)
    before = cell_forces(at(stiff, low - 1), gradients(low - 1), here)
    for row in range(low, high):
        after = gradients(row + 1)
        now = cell_forces(at(stiff, row), here, after)
        shear, shear_step = before[2] + now[2], before[2] - now[2]
        normal_step, normal = before[0] - now[0], before[1] + now[1]
        put(near[0], row, normal_step - shear)
        put(near[1], row, shear_step - normal)
        put(far[0], row, to_right(normal_step + shear, shift))
        put(far[1], row, to_right(shear_step + normal, shift))
        here, before = after, now


def remaining(n, value, f, beta, near, far, row):
    return (at(f[n], row) - at(beta, row) * value) - (at(near[n], row) + at(far[n], row))


def begin(x, following, f, coefficients, rows, shift):
    inverse = coefficients[:8, :]
    for row in rows:
        for n in range(2):
            value = at(f[n], row) * inverse
            put(x[n], row, value)
            put(following[n], row, to_left(value, shift))


def advance(levels, followings, f, beta, stiff, near, far, coefficients, step, spans, mask_of):
    keep = coefficients[8 + 16 * step : 16 + 16 * step, :]
    gain = coefficients[16 + 16 * step : 24 + 16 * step, :]
    gains = {}
    x, new = levels[step], levels[step + 1]
    for low, high in spans:
        forces(x, followings[step], stiff, near, far, low, high, 1)
        for row in range(low, high):
            mask = mask_of(row)
            part = gains.setdefault(id(mask), gain * mask)
            for n in range(2):
                value = at(x[n], row)
                change = value if step == 0 else value - at(levels[step - 1][n], row)
                value = value + keep * change + part * remaining(n, value, f, beta, near, far, row)
                put(new[n], row, value)
                put(followings[step + 1][n], row, to_left(value, 1))


def restrict(source, target, i, scale=None):
    row = DEG + 2 * i
    pair = at(source, row) + at(source, row + 1)
    pair = pair + to_left(pair, 1)
    put(target, i, pair if scale is None else scale * pair)


def pairs_of(refs):
    return [tuple(refs[n : n + 2]) for n in range(0, len(refs), 2)]


def middle_kernel(coefficients, fields, side, *refs):
    rows, cols = fields.shape[1:]
    end = RIM + rows
    left = lax.axis_index("gy") == 0
    outs, scratch = refs[:-4], refs[-4:]
    own, cell_ref, squares_out = outs[:4], outs[4], outs[5]
    level_refs, following_refs = pairs_of(outs[6 : 6 + 2 * DEG]), pairs_of(outs[6 + 2 * DEG : 6 + 4 * DEG])
    residual_refs, coarse_refs = outs[6 + 4 * DEG : 8 + 4 * DEG], outs[8 + 4 * DEG :]
    for n in range(4):
        for h in range(0, rows, 8):
            spread(fields.at[n], h, 8, left, side[rows * n + h : rows * n + h + 8, :], own[n], h)

    def whole_rows(ref):
        return Rows((RIM, end, ref, 0))

    f_u, f_v, visc, beta = (whole_rows(ref) for ref in own)
    f = (f_u, f_v)
    cell = whole_rows(cell_ref)
    levels = [tuple(map(whole_rows, pair)) for pair in level_refs]
    followings = [tuple(map(whole_rows, pair)) for pair in following_refs]
    near, far = (tuple(map(whole_rows, pair)) for pair in pairs_of(scratch))
    inside = inside_columns(left, cols)
    stiffness(visc, cell, RIM, end - 1, 1)
    begin(levels[0], followings[0], f, coefficients, range(RIM, end), 1)
    for step in range(DEG - 1):
        span = (RIM + step + 1, end - step - 1)
        advance(levels, followings, f, beta, cell, near, far, coefficients, step, (span,), lambda row: inside)
    residual = tuple(map(whole_rows, residual_refs))
    low, high = RIM + DEG, end - DEG
    forces(levels[-1], followings[-1], cell, near, far, low, high, 1)
    squares = jnp.zeros((8, LANES), F32)
    for row in range(low, high):
        for n in range(2):
            value = inside * remaining(n, at(levels[-1][n], row), f, beta, near, far, row)
            put(residual[n], row, value)
            squares = squares + value * value
    squares_out[...] = squares
    rim = (RIM - DEG) // 2
    coarse = [Rows((rim, rim + rows // 2, ref, 0)) for ref in coarse_refs]
    for i in range(rim, rim + rows // 2):
        restrict(visc, coarse[0], i, 0.25)
        restrict(beta, coarse[1], i)
        if low <= DEG + 2 * i < high:
            restrict(residual[0], coarse[2], i)
            restrict(residual[1], coarse[3], i)


def main_kernel(coefficients, fields, velocity, from_x, from_z, side_x, side_z, middle, outs, scratch):
    multiplier, gradient, sums = outs
    scratch = list(scratch)
    rows, cols = gradient.shape
    total, end = rows + 2 * RIM, RIM + rows
    gx_at, gx_size = lax.axis_index("gx"), lax.axis_size("gx")
    low_half = gx_at % 2 == 0
    left = lax.axis_index("gy") == 0
    own, cell_ref, squares_ref = middle[:4], middle[4], middle[5]
    level_refs, following_refs = pairs_of(middle[6 : 6 + 2 * DEG]), pairs_of(middle[6 + 2 * DEG : 6 + 4 * DEG])
    residual_refs, coarse_refs = middle[6 + 4 * DEG : 8 + 4 * DEG], middle[8 + 4 * DEG :]

    def take(count):
        taken = scratch[:count]
        del scratch[:count]
        return taken

    rims = take(4)
    joint = [Rows((0, rows, ref, 0)) for ref in take(2)]
    for received, partner, corner, is_above in (
        (from_x, side_x, take(1)[0], jnp.logical_not(low_half)),
        (from_z, side_z, take(1)[0], low_half),
    ):
        near = jnp.where(is_above, RIM - 8, RIM)
        far = jnp.where(is_above, 0, RIM + 8)
        rolled = [to_left(partner[...], EDGE * i) if i else partner[...] for i in range(8)]
        for i in range(8):
            columns = jnp.where(left, rolled[i], rolled[(i + 1) % 8])
            corner[pl.ds(i, RIM // 2, stride=8), :] = columns[: RIM // 2]
        for n in range(4):
            spread(received, 8 * n, 8, left, corner[8 * n : 8 * n + 8, :], rims[n], near)
            spread(received, 32 + 2 * n, 2, left, corner[32 + 2 * n : 34 + 2 * n, :], rims[n], far)

    def joined(full, ref, margin):
        return Rows(
            (0, RIM + margin, full, 0),
            (RIM + margin, end - margin, ref, margin),
            (end - margin, total, full, end - margin),
        )

    f_u, f_v, visc, beta = (
        Rows((0, RIM, rim, 0), (RIM, end, ref, 0), (end, total, rim, RIM)) for rim, ref in zip(rims, own)
    )
    f = (f_u, f_v)
    cell_full = take(1)[0]
    cell = Rows((0, RIM, cell_full, 0), (RIM, end - 1, cell_ref, 0), (end - 1, total, cell_full, end - 1))
    levels = [tuple(joined(take(1)[0], ref, n) for ref in pair) for n, pair in enumerate(level_refs)]
    followings = [tuple(joined(take(1)[0], ref, n) for ref in pair) for n, pair in enumerate(following_refs)]
    residual = tuple(joined(take(1)[0], ref, DEG) for ref in residual_refs)
    near, far = (tuple(Rows((0, total, ref, 0)) for ref in take(2)) for _ in range(2))

    inside = inside_columns(left, cols)
    above = inside * jnp.where(gx_at > 0, 1.0, 0.0)
    below = inside * jnp.where(gx_at < gx_size - 1, 1.0, 0.0)

    def mask_of(row):
        return above if row < RIM else below if row >= end else inside

    stiffness(visc, cell, 0, RIM, 1)
    stiffness(visc, cell, end - 1, total - 1, 1)
    begin(levels[0], followings[0], f, coefficients, [*range(RIM), *range(end, total)], 1)
    for step in range(DEG - 1):
        spans = ((step + 1, RIM + step + 1), (end - step - 1, total - step - 1))
        advance(levels, followings, f, beta, cell, near, far, coefficients, step, spans, mask_of)
    x = levels[-1]
    squares = squares_ref[...]
    for low, high in ((DEG, RIM + DEG), (end - DEG, total - DEG)):
        forces(x, followings[-1], cell, near, far, low, high, 1)
        for row in range(low, high):
            for n in range(2):
                value = mask_of(row) * remaining(n, at(x[n], row), f, beta, near, far, row)
                put(residual[n], row, value)
                if RIM <= row < end:
                    squares = squares + value * value

    coarse_rim = (RIM - DEG) // 2
    count = rows // 2 + 2 * coarse_rim

    def coarse_joined(ref, margin):
        first, last = coarse_rim + margin, count - coarse_rim - margin
        full = take(1)[0]
        return Rows((0, first, full, 0), (first, last, ref, margin), (last, count, full, last))

    margins = (0, 0, DEG // 2, DEG // 2)
    coarse = [coarse_joined(ref, margin) for ref, margin in zip(coarse_refs, margins)]
    for source, target, margin, scale in zip((visc, beta, *residual), coarse, margins, (0.25, None, None, None)):
        for i in [*range(coarse_rim + margin), *range(count - coarse_rim - margin, count)]:
            restrict(source, target, i, scale)

    def plain():
        return Rows((0, count, take(1)[0], 0))

    stiff, stiff_before = plain(), plain()
    stiffness(coarse[0], stiff, 0, count - 1, 2)
    for row in range(count - 1):
        put(stiff_before, row, to_right(at(stiff, row), 2))
    c_beta, c_f = coarse[1], coarse[2:]
    c_x, c_old, following, previous = ((plain(), plain()) for _ in range(4))
    table = 8 * (2 * DEG - 1)

    def keep_both(n, row, value):
        put(following[n], row, to_left(value, 2))
        put(previous[n], row, to_right(value, 2))

    def gradients(row):
        here = [at(part, row) for part in c_x]
        after = [at(part, row) for part in following]
        before = [at(part, row) for part in previous]
        return edge_gradients(here, after), edge_gradients(before, here)

    def cells(row, one, two):
        return [cell_forces(at(s, row), p, q) for s, p, q in zip((stiff, stiff_before), one, two)]

    inverse = coefficients[table : table + 8, :]
    for row in range(count):
        for n in range(2):
            value = at(c_f[n], row) * inverse
            put(c_x[n], row, value)
            keep_both(n, row, value)
    for step in range(DEG - 1):
        keep = coefficients[table + 8 + 16 * step : table + 16 + 16 * step, :]
        gain = coefficients[table + 16 + 16 * step : table + 24 + 16 * step, :]
        gains = (gain * above, gain * inside, gain * below)
        low, high = step + 1, count - step - 1
        here = gradients(low)
        before = cells(low - 1, gradients(low - 1), here)
        for row in range(low, high):
            after = gradients(row + 1)
            now = cells(row, here, after)
            (xx0, yy0, xy0), (xx1, yy1, xy1) = (
                (p[0] - q[0], p[1] + q[1], (p[2] + q[2], p[2] - q[2])) for p, q in zip(before, now)
            )
            applied = ((xx0 - xy0[0]) + (xx1 + xy1[0]), (xy0[1] - yy0) + (xy1[1] + yy1))
            part = gains[0 if row < coarse_rim else 2 if row >= count - coarse_rim else 1]
            for n in range(2):
                value = at(c_x[n], row)
                change = value if step == 0 else value - at(c_old[n], row)
                left_over = (at(c_f[n], row) - at(c_beta, row) * value) - applied[n]
                value = value + keep * change + part * left_over
                put(c_old[n], row, value)
                if step < DEG - 2:
                    keep_both(n, row, value)
            here, before = after, now
        c_x, c_old = c_old, c_x

    lanes = lane_ids()
    for i in range(rows // 2):
        for n in range(2):
            correction = at(c_x[n], coarse_rim + i)
            correction = jnp.where(lanes % 2 == 0, correction, to_right(correction, 1))
            for row in (2 * i, 2 * i + 1):
                put(joint[n], row, at(x[n], RIM + row) + correction)

    gradient_squares = jnp.zeros((8, LANES), F32)
    for h in range(0, rows, 8):
        for j in range(cols // LANES):
            s = (LANES * j) // 96
            shift = LANES * j - 96 * s + EDGE
            border = 96 * (s + 1) - LANES * j
            columns = slice(LANES * j, LANES * j + LANES)
            product = None
            for n in range(2):
                source = joint[n].pieces[0][2]
                one = source[pl.ds(8 * h + s, 8, stride=8), :]
                two = source[pl.ds(8 * h + s + 1, 8, stride=8), :]
                value = jnp.where(lanes < border, to_left(one, shift), to_right(two, (96 - shift) % LANES))
                multiplier[n, h : h + 8, columns] = value
                term = velocity[n, h : h + 8, columns] * value
                product = term if product is None else product + term
            value = -fields[3, h : h + 8, columns] * product
            gradient[h : h + 8, columns] = value
            gradient_squares = gradient_squares + value * value
    pair = [jnp.sum(value, axis=0, keepdims=True) for value in (squares * own_columns(), gradient_squares)]
    sums[...] = jnp.broadcast_to(jnp.concatenate(pair, axis=1), sums.shape)


def scale_kernel(nodes, gathered, gradient, held_multiplier, scaled, norm, multiplier, scaled_out, norm_out, sems):
    copies = [
        pltpu.make_async_copy(source, target, sems.at[n])
        for n, (source, target) in enumerate(((held_multiplier, multiplier), (norm_out, norm), (scaled_out, scaled)))
    ]
    copies[0].start()
    residual_total = jnp.sum(gathered[:, :LANES], keepdims=True)
    gradient_total = jnp.sum(gathered[:, LANES:], keepdims=True)
    norm_out[...] = jnp.sqrt(residual_total / (2 * nodes))
    copies[1].start()
    scaled_out[...] = gradient[...] / jnp.sqrt(gradient_total / nodes + 1e-06)
    copies[2].start()
    for copy in copies:
        copy.wait()


def body(misfit, velocity, viscosity, friction, ice, grounded, bounds):
    rows, cols = viscosity.shape
    gx_size, gy_size = lax.axis_size("gx"), lax.axis_size("gy")
    assert gy_size == 2 and gx_size % 2 == 0 and cols == 96 * SEGS and rows == 16
    peers = gx_size * gy_size
    nodes = rows * cols * peers
    total = rows + 2 * RIM
    shaped = jax.ShapeDtypeStruct
    whole = pl.BlockSpec(memory_space=pltpu.VMEM)
    params = pltpu.CompilerParams(vmem_limit_bytes=32 * 1024 * 1024)

    held = pl.BlockSpec(memory_space=pltpu.HBM)
    fields, coefficients, x_send, z_send, side_send, x_corner, z_corner = pl.pallas_call(
        pack_kernel,
        out_shape=(
            shaped((4, rows, cols), F32),
            shaped((16 * (2 * DEG - 1), LANES), F32),
            shaped((4 * RIM, cols), F32),
            shaped((4 * RIM, cols), F32),
            shaped((4 * rows, LANES), F32),
            shaped((8, LANES), F32),
            shaped((8, LANES), F32),
        ),
        in_specs=[held] * 6,
        out_specs=[whole] * 7,
        scratch_shapes=[
            pltpu.SMEM((4,), F32),
            pltpu.VMEM((rows, cols), F32),
            pltpu.VMEM((rows, cols), F32),
            pltpu.VMEM((rows, cols), jnp.int32),
            pltpu.VMEM((rows, cols), jnp.int32),
            pltpu.SemaphoreType.DMA((6,)),
        ],
        compiler_params=params,
        name="pack",
    )(*(pltpu.with_memory_space_constraint(x, pltpu.HBM) for x in (bounds, misfit, viscosity, friction, ice, grounded)))

    x_pairs = [(i, i ^ 1) for i in range(gx_size)]
    z_pairs = [(2 * i + c, 2 * j + c) for i in range(1, gx_size - 1) for j in (i + 1 if i % 2 else i - 1,) for c in (0, 1)]
    z_pairs += [(2 * i + c, 2 * i + 1 - c) for i in (0, gx_size - 1) for c in (0, 1)]
    swap = [(0, 1), (1, 0)]
    from_x = lax.ppermute(x_send, "gx", x_pairs)
    from_z = lax.ppermute(z_send, AXES, z_pairs)
    side = lax.ppermute(side_send, "gy", swap)
    side_x = lax.ppermute(x_corner, AXES, [(2 * i + c, 2 * j + 1 - c) for i, j in x_pairs for c in (0, 1)])
    side_z = lax.ppermute(z_corner, AXES, [(i, j ^ 1 if 1 < i < 2 * gx_size - 2 else j) for i, j in z_pairs])

    fine = pltpu.VMEM((8 * total, LANES), F32)
    coarse = pltpu.VMEM((4 * total, LANES), F32)
    owned = pltpu.VMEM((8 * rows, LANES), F32)
    halved = pltpu.VMEM((4 * rows, LANES), F32)
    middle = pl.pallas_call(
        middle_kernel,
        out_shape=[owned] * 5 + [pltpu.VMEM((8, LANES), F32)] + [owned] * (4 * DEG + 2) + [halved] * 4,
        in_specs=[whole] * 3,
        out_specs=[whole] * (12 + 4 * DEG),
        scratch_shapes=[owned] * 4,
        compiler_params=params,
        name="middle",
    )(coefficients, fields, side)

    def leg_kernel(coefficients, fields, velocity, from_x, from_z, side_x, side_z, *refs):
        done, refs = refs[: len(middle)], refs[len(middle) :]
        main_kernel(coefficients, fields, velocity, from_x, from_z, side_x, side_z, done, refs[:3], refs[3:])

    rim = pltpu.VMEM((16 * RIM, LANES), F32)
    corner = pltpu.VMEM((4 * RIM, LANES), F32)
    held_multiplier, gradient, sums = pl.pallas_call(
        leg_kernel,
        out_shape=(
            pltpu.VMEM((2, rows, cols), F32),
            pltpu.VMEM((rows, cols), F32),
            shaped((peers, 2 * LANES), F32),
        ),
        in_specs=[whole] * (7 + len(middle)),
        out_specs=[whole] * 3,
        scratch_shapes=[rim] * 4 + [owned] * 2 + [corner] * 2 + [fine] * (7 + 4 * DEG) + [coarse] * 14,
        compiler_params=params,
        name="leg",
    )(coefficients, fields, velocity, from_x, from_z, side_x, side_z, *middle)

    gathered = lax.all_to_all(sums, AXES, 0, 0, tiled=True)
    scaled, norm, multiplier = pl.pallas_call(
        functools.partial(scale_kernel, nodes),
        out_shape=(
            pltpu.HBM((rows, cols), F32),
            pltpu.HBM((1, 1), F32),
            pltpu.HBM((2, rows, cols), F32),
        ),
        in_specs=[whole] * 3,
        out_specs=[held] * 3,
        scratch_shapes=[
            pltpu.VMEM((rows, cols), F32),
            pltpu.VMEM((1, 1), F32),
            pltpu.SemaphoreType.DMA((3,)),
        ],
        compiler_params=params,
        name="scale",
    )(gathered, gradient, held_multiplier)
    return multiplier, scaled, norm.reshape(1)


def solution(mesh):
    tile = P(("grp", "gx"), "gy")
    pair = P(None, ("grp", "gx"), "gy")
    return jax.shard_map(
        body,
        mesh=mesh,
        in_specs=(pair, pair, tile, tile, tile, tile, P("grp")),
        out_specs=(pair, tile, P("grp")),
        check_vma=False,
    )
```

time: 25.8 us -> 25.1 us (0.973)
  waiting for transfers between devices: 2.98 us -> 1.41 us
  Pallas kernels: 3.74 us -> 4.55 us
    ppermute x1, waiting for transfers between devices: 2.96 us -> 1.4 us  [body(): lax.ppermute(x_corner, AXES, [(2 * i + c, 2 * j + 1 - c) for i, j in x_pa...]
    pallas_call x1 -> x2, Pallas kernels: 1.84 us -> 2.61 us  [the longest x1 1.71 us: body(): pl.pallas_call(leg_kernel, out_shape=(pltpu.VMEM((2, rows, cols), F32), p...]
  transfers between devices with their start and end apart: 5 -> 5, of which waited for: 1 -> 1; matrix products, arithmetic and copies ran while one was open for 0% -> 0% of each run, Pallas kernels for 0% -> 4%
where the time goes in v7:
time: 25.1 us; the launch traced here: 24.9 us
  blocking collectives  12.1 us (48%)
  starting transfers between devices  6.16 us (25%)
  Pallas kernels  4.55 us (18%)
  waiting for transfers between devices  1.41 us (6%)
  between operations  0.67 us (3%)
    all_to_all x1, blocking collectives, body(): gathered = lax.all_to_all(sums, AXES, 0, 0, tiled=True)  12.1 us
    ppermute x1, starting transfers between devices, body(): from_x = lax.ppermute(x_send, 'gx', x_pairs)  3 us
    ppermute x1, starting transfers between devices, body(): lax.ppermute(x_corner, AXES, [(2 * i + c, 2 * j + 1 - c) for i, j in x_pa...  2.64 us
    pallas_call x1, Pallas kernels, body(): pl.pallas_call(leg_kernel, out_shape=(pltpu.VMEM((2, rows, cols), F32), p...  1.71 us
    ppermute x1, waiting for transfers between devices, body(): lax.ppermute(x_corner, AXES, [(2 * i + c, 2 * j + 1 - c) for i, j in x_pa...  1.4 us
    pallas_call x1, Pallas kernels, body(): pl.pallas_call(pack_kernel, out_shape=(shaped((4, rows, cols), F32), shap...  1.15 us
    pallas_call x1, Pallas kernels, body(): pl.pallas_call(middle_kernel, out_shape=[owned] * 5 + [pltpu.VMEM((8, LAN...  0.9 us
    pallas_call x1, Pallas kernels, body(): pl.pallas_call(functools.partial(scale_kernel, nodes), out_shape=(pltpu.H...  0.79 us
  transfers between devices with their start and end apart: 5, of which 1 were waited for; matrix products, arithmetic and copies ran while one was open for 0% of the time, Pallas kernels for 4%

profile of v7, /device:TPU:0, one launch (start us, length us, event | category | flops | bytes accessed | tf_op | source)
XLA Modules:
  0.0 24.9 jit_solution(16614766467012951839)
XLA Ops:
  0.6 1.2 %pack.1 = (f32[4,16,768]{2,1,0:T(8,128)S(1)}, f32[112,128]{1,0:T(8,128)S(1)}, f32[40,768]{1,0:T(8,128)S(1)}, f32[40,768]{1,0:T(8,128)S(1)}, f32[64,128]{1,0:T(8,...) custom-call(f32[4]{0:T(128)} %bounds.1, f32[2,16,768]{2,1,0:T(8,128)} %misfit.1, f32[16,768]{1,0:T(8,128)} %visc.1, ...), custom_call_target="tpu_custom_call" | custom-call | tf_op jit(solution)/shard_map/pack/pallas_call | solution.py:476
  1.8 3.0 %collective-permute-start = (f32[40,768]{1,0:T(8,128)S(1)}, f32[40,768]{1,0:T(8,128)S(1)}, u32[]{:S(2)}, u32[]{:S(2)}) collective-permute-start(f32[40,768]{1,0:T(8,128)S(1)} %get-tuple-element.46), channel_id=1, source_target_pairs={{0,2},{2,0},{4,6},{6,4},{8,10},{10,8},{12,14},{14,12},{1,3},{3,1},... | collective-permute-start | bytes 368648 | tf_op jit(solution)/shard_map/ppermute | solution.py:505
  4.8 0.0 collective-permute-start.1
  4.8 0.5 %collective-permute-start.4 = (f32[64,128]{1,0:T(8,128)S(1)}, f32[64,128]{1,0:T(8,128)S(1)}, u32[]{:S(2)}, u32[]{:S(2)}) collective-permute-start(f32[64,128]{1,0:T(8,128)S(1)} %get-tuple-element.50), channel_id=1, source_target_pairs={{0,1},{1,0},{2,3},{3,2},{4,5},{5,4},{6,7},{7,6},{8,9},{9,8},{10,11... | collective-permute-start | bytes 98312 | tf_op jit(solution)/shard_map/ppermute | solution.py:507
  5.3 2.6 %collective-permute-start.2 = (f32[8,128]{1,0:T(8,128)S(1)}, f32[8,128]{1,0:T(8,128)S(1)}, u32[]{:S(2)}, u32[]{:S(2)}) collective-permute-start(f32[8,128]{1,0:T(8,128)S(1)} %get-tuple-element.48), channel_id=1, source_target_pairs={{0,3},{1,2},{2,1},{3,0},{4,7},{5,6},{6,5},{7,4},{8,11},{9,10},{10,... | collective-permute-start | bytes 12296 | tf_op jit(solution)/shard_map/ppermute | solution.py:508
  8.0 0.0 collective-permute-start.3
  8.0 0.0 collective-permute-done.4.side
  8.0 0.0 copy-start
  8.0 0.9 %middle.1 = (f32[128,128]{1,0:T(8,128)S(1)}, f32[128,128]{1,0:T(8,128)S(1)}, f32[128,128]{1,0:T(8,128)S(1)}, f32[128,128]{1,0:T(8,128)S(1)}, f32[128,128]{1,0:T(...) custom-call(f32[112,128]{1,0:T(8,128)S(1)} %get-tuple-element.44.coe, ...), custom_call_target="tpu_custom_call" | custom-call | tf_op jit(solution)/shard_map/middle/pallas_call | solution.py:515
  8.9 1.4 %collective-permute-done.2.side_x = f32[8,128]{1,0:T(8,128)S(1)} collective-permute-done((f32[8,128]{1,0:T(8,128)S(1)}, f32[8,128]{1,0:T(8,128)S(1)}, u32[]{:S(2)}, u32[]{:S(2)}) %collective-permute-start.2) | collective-permute-done | bytes 4128 | tf_op jit(solution)/shard_map/ppermute | solution.py:508
  10.3 0.0 collective-permute-done.3.side_z
  10.3 0.0 collective-permute-done.from_x
  10.3 0.0 collective-permute-done.1.from_z
  10.3 0.0 copy-done
  10.3 1.7 %leg.1 = (f32[2,16,768]{2,1,0:T(8,128)S(1)}, f32[16,768]{1,0:T(8,128)S(1)}, f32[16,256]{1,0:T(8,128)S(1)}) custom-call(f32[112,128]{1,0:T(8,128)S(1)} %get-tuple-element.44.coefficients, f32[4,16,768]{2,1,0:T(8,128)S(1)} %get-tuple-element.45.fields, f32[2,16,768]{2,1,0:T(8,128)S(1)} %copy-done, f32[40,768]{1,0:T(8,128)S(1)} %collective-permute-done.from_x, ...), custom_call_target="tpu_custom_call" | custom-call | tf_op jit(solution)/shard_map/leg/pallas_call | solution.py:531
  12.0 12.1 %all_to_all.11 = f32[16,1,256]{2,1,0:T(1,128)S(1)} all-to-all(f32[16,1,256]{2,1,0:T(1,128)S(1)} %copy.10), channel_id=1, replica_groups=mesh['grp'=2,'gx'=8,'gy'=2] {'gx','gy'}, dimensions={0} | all-to-all | bytes 32768 | tf_op jit(solution)/shard_map/all_to_all | solution.py:545
  24.1 0.8 %scale.1 = (f32[16,768]{1,0:T(8,128)}, f32[1,1]{1,0:T(1,128)}, f32[2,16,768]{2,1,0:T(8,128)}) custom-call(f32[16,256]{1,0:T(8,128)S(1)} %bitcast.5, f32[16,768]{1,0:T(8,128)S(1)} %get-tuple-element.80.gradient, f32[2,16,768]{2,1,0:T(8,128)S(1)} %get-tuple-element.81.held_multiplier), custom_call_target="tpu_custom_call" | custom-call | tf_op jit(solution)/shard_map/scale/pallas_call | solution.py:546
  (2 shorter events, 0.0 us)
Async XLA Ops:
  1.8 8.5 %collective-permute-start = (f32[40,768]{1,0:T(8,128)S(1)}, f32[40,768]{1,0:T(8,128)S(1)}, u32[]{:S(2)}, u32[]{:S(2)}) collective-permute-start(f32[40,768]{1,0:T(8,128)S(1)} %get-tuple-element.46), channel_id=1, source_target_pairs={{0,2},{2,0},{4,6},{6,4},{8,10},{10,8},{12,14},{14,12},{1,3},{3,1},... | collective-permute-start | bytes 368648 | tf_op jit(solution)/shard_map/ppermute | solution.py:505
  4.8 5.5 %collective-permute-start.1 = (f32[40,768]{1,0:T(8,128)S(1)}, f32[40,768]{1,0:T(8,128)S(1)}, u32[]{:S(2)}, u32[]{:S(2)}) collective-permute-start(f32[40,768]{1,0:T(8,128)S(1)} %get-tuple-element.47), channel_id=1, source_target_pairs={{2,4},{3,5},{4,2},{5,3},{6,8},{7,9},{8,6},{9,7},{10,12},{11,13},{1... | collective-permute-start | bytes 368648 | tf_op jit(solution)/shard_map/ppermute | solution.py:506
  4.8 3.2 %collective-permute-start.4 = (f32[64,128]{1,0:T(8,128)S(1)}, f32[64,128]{1,0:T(8,128)S(1)}, u32[]{:S(2)}, u32[]{:S(2)}) collective-permute-start(f32[64,128]{1,0:T(8,128)S(1)} %get-tuple-element.50), channel_id=1, source_target_pairs={{0,1},{1,0},{2,3},{3,2},{4,5},{5,4},{6,7},{7,6},{8,9},{9,8},{10,11... | collective-permute-start | bytes 98312 | tf_op jit(solution)/shard_map/ppermute | solution.py:507
  5.3 5.0 %collective-permute-start.2 = (f32[8,128]{1,0:T(8,128)S(1)}, f32[8,128]{1,0:T(8,128)S(1)}, u32[]{:S(2)}, u32[]{:S(2)}) collective-permute-start(f32[8,128]{1,0:T(8,128)S(1)} %get-tuple-element.48), channel_id=1, source_target_pairs={{0,3},{1,2},{2,1},{3,0},{4,7},{5,6},{6,5},{7,4},{8,11},{9,10},{10,... | collective-permute-start | bytes 12296 | tf_op jit(solution)/shard_map/ppermute | solution.py:508
  8.0 2.3 %collective-permute-start.3 = (f32[8,128]{1,0:T(8,128)S(1)}, f32[8,128]{1,0:T(8,128)S(1)}, u32[]{:S(2)}, u32[]{:S(2)}) collective-permute-start(f32[8,128]{1,0:T(8,128)S(1)} %get-tuple-element.49), channel_id=1, source_target_pairs={{2,5},{3,4},{4,3},{5,2},{6,9},{7,8},{8,7},{9,6},{10,13},{11,12},{1... | collective-permute-start | bytes 12296 | tf_op jit(solution)/shard_map/ppermute | solution.py:509
  8.0 2.3 %copy-start = (f32[2,16,768]{2,1,0:T(8,128)S(1)}, f32[2,16,768]{2,1,0:T(8,128)}, u32[]{:S(2)}) copy-start(f32[2,16,768]{2,1,0:T(8,128)} %velocity.1) | copy-start | bytes 294916

commit v8 on v7

--- a/solution.py
+++ b/solution.py
@@ -47,18 +47,24 @@
         copy.wait()
     fields[2] = visc_in[...] * ice_in[...].astype(F32)
     fields[3] = friction_in[...] * grounded_in[...].astype(F32)
+    sublanes = lax.broadcasted_iota(jnp.int32, (8, cols), 0)
+    down_tail = up_tail = jnp.zeros((8, cols), F32)
     for n in range(4):
         last, first = fields[n, rows - 8 :, :], fields[n, :8, :]
         x_send[8 * n : 8 * n + 8, :] = jnp.where(low_half, last, first)
         z_send[8 * n : 8 * n + 8, :] = jnp.where(at_end, 0.0, jnp.where(low_half, first, last))
-        last, first = fields[n, rows - 10 : rows - 8, :], fields[n, 8:10, :]
-        x_send[32 + 2 * n : 34 + 2 * n, :] = jnp.where(low_half, last, first)
-        z_send[32 + 2 * n : 34 + 2 * n, :] = jnp.where(at_end, 0.0, jnp.where(low_half, first, last))
+        here = sublanes // 2 == n
+        down_tail = jnp.where(here, pltpu.roll(fields[n, rows - 16 : rows - 8, :], (2 * n + 2) % 8, 0), down_tail)
+        up_tail = jnp.where(here, pltpu.roll(fields[n, 8:16, :], 2 * n, 0), up_tail)
         side_send[rows * n : rows * n + rows, :] = jnp.where(
             left, fields[n, :, cols - LANES :], fields[n, :, :LANES]
         )
-    own_columns = lane_ids() // EDGE == lax.broadcasted_iota(jnp.int32, (8, LANES), 0)
+    x_send[32:, :] = jnp.where(low_half, down_tail, up_tail)
+    z_send[32:, :] = jnp.where(at_end, 0.0, jnp.where(low_half, up_tail, down_tail))
+    sublanes = sublanes[:, :LANES]
+    own_columns_of = lane_ids() // EDGE == sublanes
     for source, target in ((x_send, x_corner), (z_send, z_corner)):
+        packed = jnp.zeros((8, LANES), F32)
         for q in range(RIM // 2):
             last, first = source[8 * q : 8 * q + 8, cols - LANES :], source[8 * q : 8 * q + 8, :LANES]
             columns = jnp.where(
@@ -66,8 +72,9 @@
                 pltpu.roll(last, EDGE, 1, stride=EDGE, stride_axis=0),
                 pltpu.roll(first, 0, 1, stride=EDGE, stride_axis=0),
             )
-            target[q : q + 1, :] = jnp.sum(jnp.where(own_columns, columns, 0.0), axis=0, keepdims=True)
-        target[RIM // 2 :, :] = jnp.zeros((8 - RIM // 2, LANES), F32)
+            row = jnp.sum(jnp.where(own_columns_of, columns, 0.0), axis=0, keepdims=True)
+            packed = jnp.where(sublanes == q, row, packed)
+        target[...] = packed
     copies[5].wait()
     for sweep in range(2):
         lower = jnp.full((8, LANES), levels[2 * sweep])
@@ -138,7 +145,7 @@
 
 def own_columns():
     lanes = lane_ids()
-    return ((lanes >= EDGE) & (lanes < LANES - EDGE)).astype(F32)
+    return (lanes >= EDGE) & (lanes < LANES - EDGE)
 
 
 def stiffness(visc, target, first, last, shift):
@@ -211,11 +218,15 @@
                 put(followings[step + 1][n], row, to_left(value, 1))
 
 
-def restrict(source, target, i, scale=None):
+def restrict(source, i, lanes, scale=None):
     row = DEG + 2 * i
     pair = at(source, row) + at(source, row + 1)
-    pair = pair + to_left(pair, 1)
-    put(target, i, pair if scale is None else scale * pair)
+    if scale is not None:
+        pair = scale * pair
+    even, odd = lanes != "odd", lanes != "even"
+    if even and odd:
+        return jnp.where(lane_ids() % 2 == 0, pair + to_left(pair, 1), pair + to_right(pair, 1))
+    return pair + (to_left(pair, 1) if even else to_right(pair, 1))
 
 
 def pairs_of(refs):
@@ -262,11 +273,11 @@
     rim = (RIM - DEG) // 2
     coarse = [Rows((rim, rim + rows // 2, ref, 0)) for ref in coarse_refs]
     for i in range(rim, rim + rows // 2):
-        restrict(visc, coarse[0], i, 0.25)
-        restrict(beta, coarse[1], i)
+        put(coarse[0], i, restrict(visc, i, "both", 0.25))
+        put(coarse[1], i, restrict(beta, i, "both"))
         if low <= DEG + 2 * i < high:
-            restrict(residual[0], coarse[2], i)
-            restrict(residual[1], coarse[3], i)
+            put(coarse[2], i, restrict(residual[0], i, "both"))
+            put(coarse[3], i, restrict(residual[1], i, "both"))
 
 
 def main_kernel(coefficients, fields, velocity, from_x, from_z, side_x, side_z, middle, outs, scratch):
@@ -287,20 +298,18 @@
         return taken
 
     rims = take(4)
+    tails = take(1)[0]
     joint = [Rows((0, rows, ref, 0)) for ref in take(2)]
     for received, partner, corner, is_above in (
         (from_x, side_x, take(1)[0], jnp.logical_not(low_half)),
         (from_z, side_z, take(1)[0], low_half),
     ):
-        near = jnp.where(is_above, RIM - 8, RIM)
-        far = jnp.where(is_above, 0, RIM + 8)
+        first_row = jnp.where(is_above, 0, 8)
         rolled = [to_left(partner[...], EDGE * i) if i else partner[...] for i in range(8)]
         for i in range(8):
-            columns = jnp.where(left, rolled[i], rolled[(i + 1) % 8])
-            corner[pl.ds(i, RIM // 2, stride=8), :] = columns[: RIM // 2]
-        for n in range(4):
-            spread(received, 8 * n, 8, left, corner[8 * n : 8 * n + 8, :], rims[n], near)
-            spread(received, 32 + 2 * n, 2, left, corner[32 + 2 * n : 34 + 2 * n, :], rims[n], far)
+            corner[pl.ds(i, 8, stride=8), :] = jnp.where(left, rolled[i], rolled[(i + 1) % 8])
+        for n, target in enumerate((*rims, tails)):
+            spread(received, 8 * n, 8, left, corner[8 * n : 8 * n + 8, :], target, first_row)
 
     def joined(full, ref, margin):
         return Rows(
@@ -310,7 +319,14 @@
         )
 
     f_u, f_v, visc, beta = (
-        Rows((0, RIM, rim, 0), (RIM, end, ref, 0), (end, total, rim, RIM)) for rim, ref in zip(rims, own)
+        Rows(
+            (0, RIM - 8, tails, 2 * n),
+            (RIM - 8, RIM, rims[n], 0),
+            (RIM, end, own[n], 0),
+            (end, end + 8, rims[n], 8),
+            (end + 8, total, tails, 8 + 2 * n),
+        )
+        for n in range(4)
     )
     f = (f_u, f_v)
     cell_full = take(1)[0]
@@ -344,83 +360,81 @@
                 if RIM <= row < end:
                     squares = squares + value * value
 
+    even = lane_ids() % 2 == 0
     coarse_rim = (RIM - DEG) // 2
-    count = rows // 2 + 2 * coarse_rim
-
-    def coarse_joined(ref, margin):
-        first, last = coarse_rim + margin, count - coarse_rim - margin
-        full = take(1)[0]
-        return Rows((0, first, full, 0), (first, last, ref, margin), (last, count, full, last))
-
-    margins = (0, 0, DEG // 2, DEG // 2)
-    coarse = [coarse_joined(ref, margin) for ref, margin in zip(coarse_refs, margins)]
-    for source, target, margin, scale in zip((visc, beta, *residual), coarse, margins, (0.25, None, None, None)):
-        for i in [*range(coarse_rim + margin), *range(count - coarse_rim - margin, count)]:
-            restrict(source, target, i, scale)
+    half = rows // 4
+    count = half + 2 * coarse_rim
 
     def plain():
         return Rows((0, count, take(1)[0], 0))
 
+    def packed(source, ref, margin, scale):
+        first, last = coarse_rim + margin, coarse_rim + 2 * half - margin
+        target = plain()
+        for j in range(count):
+            i, k = j, j + half
+            one = at(Rows((first, last, ref, margin)), i) if first <= i < last else restrict(source, i, "even", scale)
+            two = at(Rows((first, last, ref, margin)), k) if first <= k < last else restrict(source, k, "odd", scale)
+            put(target, j, jnp.where(even, one, two))
+        return target
+
+    c_visc, c_beta, *c_f = (
+        packed(source, ref, margin, scale)
+        for source, ref, margin, scale in zip(
+            (visc, beta, *residual), coarse_refs, (0, 0, DEG // 2, DEG // 2), (0.25, None, None, None)
+        )
+    )
+    masks = [
+        jnp.where(even, above if j < coarse_rim else inside, below if j >= count - coarse_rim else inside)
+        for j in range(count)
+    ]
     stiff, stiff_before = plain(), plain()
-    stiffness(coarse[0], stiff, 0, count - 1, 2)
+    stiffness(c_visc, stiff, 0, count - 1, 2)
     for row in range(count - 1):
         put(stiff_before, row, to_right(at(stiff, row), 2))
-    c_beta, c_f = coarse[1], coarse[2:]
-    c_x, c_old, following, previous = ((plain(), plain()) for _ in range(4))
     table = 8 * (2 * DEG - 1)
 
-    def keep_both(n, row, value):
-        put(following[n], row, to_left(value, 2))
-        put(previous[n], row, to_right(value, 2))
-
-    def gradients(row):
-        here = [at(part, row) for part in c_x]
-        after = [at(part, row) for part in following]
-        before = [at(part, row) for part in previous]
+    def gradients(here):
+        after = [to_left(value, 2) for value in here]
+        before = [to_right(value, 2) for value in here]
         return edge_gradients(here, after), edge_gradients(before, here)
 
     def cells(row, one, two):
         return [cell_forces(at(s, row), p, q) for s, p, q in zip((stiff, stiff_before), one, two)]
 
     inverse = coefficients[table : table + 8, :]
-    for row in range(count):
-        for n in range(2):
-            value = at(c_f[n], row) * inverse
-            put(c_x[n], row, value)
-            keep_both(n, row, value)
+    c_x = [[at(part, row) * inverse for part in c_f] for row in range(count)]
+    c_old = c_x
     for step in range(DEG - 1):
         keep = coefficients[table + 8 + 16 * step : table + 16 + 16 * step, :]
         gain = coefficients[table + 16 + 16 * step : table + 24 + 16 * step, :]
-        gains = (gain * above, gain * inside, gain * below)
         low, high = step + 1, count - step - 1
-        here = gradients(low)
-        before = cells(low - 1, gradients(low - 1), here)
+        edges = {row: gradients(c_x[row]) for row in range(low - 1, high + 1)}
+        forces_at = {row: cells(row, edges[row], edges[row + 1]) for row in range(low - 1, high)}
+        c_new = list(c_x)
         for row in range(low, high):
-            after = gradients(row + 1)
-            now = cells(row, here, after)
             (xx0, yy0, xy0), (xx1, yy1, xy1) = (
-                (p[0] - q[0], p[1] + q[1], (p[2] + q[2], p[2] - q[2])) for p, q in zip(before, now)
+                (p[0] - q[0], p[1] + q[1], (p[2] + q[2], p[2] - q[2]))
+                for p, q in zip(forces_at[row - 1], forces_at[row])
             )
             applied = ((xx0 - xy0[0]) + (xx1 + xy1[0]), (xy0[1] - yy0) + (xy1[1] + yy1))
-            part = gains[0 if row < coarse_rim else 2 if row >= count - coarse_rim else 1]
+            part = gain * masks[row]
+            c_new[row] = []
             for n in range(2):
-                value = at(c_x[n], row)
-                change = value if step == 0 else value - at(c_old[n], row)
+                value = c_x[row][n]
+                change = value if step == 0 else value - c_old[row][n]
                 left_over = (at(c_f[n], row) - at(c_beta, row) * value) - applied[n]
-                value = value + keep * change + part * left_over
-                put(c_old[n], row, value)
-                if step < DEG - 2:
-                    keep_both(n, row, value)
-            here, before = after, now
-        c_x, c_old = c_old, c_x
+                c_new[row].append(value + keep * change + part * left_over)
+        c_x, c_old = c_new, c_x
 
     lanes = lane_ids()
-    for i in range(rows // 2):
+    for i in range(half):
         for n in range(2):
-            correction = at(c_x[n], coarse_rim + i)
-            correction = jnp.where(lanes % 2 == 0, correction, to_right(correction, 1))
-            for row in (2 * i, 2 * i + 1):
-                put(joint[n], row, at(x[n], RIM + row) + correction)
+            value = c_x[coarse_rim + i][n]
+            corrections = jnp.where(even, value, to_right(value, 1)), jnp.where(even, to_left(value, 1), value)
+            for first, correction in zip((2 * i, 2 * (i + half)), corrections):
+                for row in (first, first + 1):
+                    put(joint[n], row, at(x[n], RIM + row) + correction)
 
     gradient_squares = jnp.zeros((8, LANES), F32)
     for h in range(0, rows, 8):
@@ -441,7 +455,7 @@
             value = -fields[3, h : h + 8, columns] * product
             gradient[h : h + 8, columns] = value
             gradient_squares = gradient_squares + value * value
-    pair = [jnp.sum(value, axis=0, keepdims=True) for value in (squares * own_columns(), gradient_squares)]
+    pair = [jnp.sum(value, axis=0, keepdims=True) for value in (jnp.where(own_columns(), squares, 0.0), gradient_squares)]
     sums[...] = jnp.broadcast_to(jnp.concatenate(pair, axis=1), sums.shape)
 
 
@@ -526,8 +540,8 @@
         done, refs = refs[: len(middle)], refs[len(middle) :]
         main_kernel(coefficients, fields, velocity, from_x, from_z, side_x, side_z, done, refs[:3], refs[3:])
 
-    rim = pltpu.VMEM((16 * RIM, LANES), F32)
-    corner = pltpu.VMEM((4 * RIM, LANES), F32)
+    rim = pltpu.VMEM((8 * 16, LANES), F32)
+    corner = pltpu.VMEM((8 * 8, LANES), F32)
     held_multiplier, gradient, sums = pl.pallas_call(
         leg_kernel,
         out_shape=(
@@ -537,7 +551,7 @@
         ),
         in_specs=[whole] * (7 + len(middle)),
         out_specs=[whole] * 3,
-        scratch_shapes=[rim] * 4 + [owned] * 2 + [corner] * 2 + [fine] * (7 + 4 * DEG) + [coarse] * 14,
+        scratch_shapes=[rim] * 5 + [owned] * 2 + [corner] * 2 + [fine] * (7 + 4 * DEG) + [coarse] * 14,
         compiler_params=params,
         name="leg",
     )(coefficients, fields, velocity, from_x, from_z, side_x, side_z, *middle)

time: 25.1 us -> 25 us (level)
  no operation moved by 1% of the time
where the time goes in v8:
time: 25 us; the launch traced here: 24.8 us
  blocking collectives  12.1 us (48%)
  starting transfers between devices  6.16 us (25%)
  Pallas kernels  4.41 us (18%)
  waiting for transfers between devices  1.41 us (6%)
  between operations  0.67 us (3%)
    all_to_all x1, blocking collectives, body(): gathered = lax.all_to_all(sums, AXES, 0, 0, tiled=True)  12.1 us
    ppermute x1, starting transfers between devices, body(): from_x = lax.ppermute(x_send, 'gx', x_pairs)  3 us
    ppermute x1, starting transfers between devices, body(): lax.ppermute(x_corner, AXES, [(2 * i + c, 2 * j + 1 - c) for i, j in x_pa...  2.64 us
    pallas_call x1, Pallas kernels, body(): pl.pallas_call(leg_kernel, out_shape=(pltpu.VMEM((2, rows, cols), F32), p...  1.59 us
    ppermute x1, waiting for transfers between devices, body(): lax.ppermute(x_corner, AXES, [(2 * i + c, 2 * j + 1 - c) for i, j in x_pa...  1.4 us
    pallas_call x1, Pallas kernels, body(): pl.pallas_call(pack_kernel, out_shape=(shaped((4, rows, cols), F32), shap...  1.13 us
    pallas_call x1, Pallas kernels, body(): pl.pallas_call(middle_kernel, out_shape=[owned] * 5 + [pltpu.VMEM((8, LAN...  0.9 us
    pallas_call x1, Pallas kernels, body(): pl.pallas_call(functools.partial(scale_kernel, nodes), out_shape=(pltpu.H...  0.79 us
  transfers between devices with their start and end apart: 5, of which 1 were waited for; matrix products, arithmetic and copies ran while one was open for 0% of the time, Pallas kernels for 4%

profile of v8, /device:TPU:0, one launch (start us, length us, event | category | flops | bytes accessed | tf_op | source)
XLA Modules:
  0.0 24.8 jit_solution(16164114796972321182)
XLA Ops:
  0.6 1.1 %pack.1 = (f32[4,16,768]{2,1,0:T(8,128)S(1)}, f32[112,128]{1,0:T(8,128)S(1)}, f32[40,768]{1,0:T(8,128)S(1)}, f32[40,768]{1,0:T(8,128)S(1)}, f32[64,128]{1,0:T(8,...) custom-call(f32[4]{0:T(128)} %bounds.1, f32[2,16,768]{2,1,0:T(8,128)} %misfit.1, f32[16,768]{1,0:T(8,128)} %visc.1, ...), custom_call_target="tpu_custom_call" | custom-call | tf_op jit(solution)/shard_map/pack/pallas_call | solution.py:490
  1.8 3.0 %collective-permute-start = (f32[40,768]{1,0:T(8,128)S(1)}, f32[40,768]{1,0:T(8,128)S(1)}, u32[]{:S(2)}, u32[]{:S(2)}) collective-permute-start(f32[40,768]{1,0:T(8,128)S(1)} %get-tuple-element.46), channel_id=1, source_target_pairs={{0,2},{2,0},{4,6},{6,4},{8,10},{10,8},{12,14},{14,12},{1,3},{3,1},... | collective-permute-start | bytes 368648 | tf_op jit(solution)/shard_map/ppermute | solution.py:519
  4.8 0.0 collective-permute-start.1
  4.8 0.5 %collective-permute-start.4 = (f32[64,128]{1,0:T(8,128)S(1)}, f32[64,128]{1,0:T(8,128)S(1)}, u32[]{:S(2)}, u32[]{:S(2)}) collective-permute-start(f32[64,128]{1,0:T(8,128)S(1)} %get-tuple-element.50), channel_id=1, source_target_pairs={{0,1},{1,0},{2,3},{3,2},{4,5},{5,4},{6,7},{7,6},{8,9},{9,8},{10,11... | collective-permute-start | bytes 98312 | tf_op jit(solution)/shard_map/ppermute | solution.py:521
  5.3 2.6 %collective-permute-start.2 = (f32[8,128]{1,0:T(8,128)S(1)}, f32[8,128]{1,0:T(8,128)S(1)}, u32[]{:S(2)}, u32[]{:S(2)}) collective-permute-start(f32[8,128]{1,0:T(8,128)S(1)} %get-tuple-element.48), channel_id=1, source_target_pairs={{0,3},{1,2},{2,1},{3,0},{4,7},{5,6},{6,5},{7,4},{8,11},{9,10},{10,... | collective-permute-start | bytes 12296 | tf_op jit(solution)/shard_map/ppermute | solution.py:522
  7.9 0.0 collective-permute-start.3
  7.9 0.0 collective-permute-done.4.side
  7.9 0.0 copy-start
  7.9 0.9 %middle.1 = (f32[128,128]{1,0:T(8,128)S(1)}, f32[128,128]{1,0:T(8,128)S(1)}, f32[128,128]{1,0:T(8,128)S(1)}, f32[128,128]{1,0:T(8,128)S(1)}, f32[128,128]{1,0:T(...) custom-call(f32[112,128]{1,0:T(8,128)S(1)} %get-tuple-element.44.coe, ...), custom_call_target="tpu_custom_call" | custom-call | tf_op jit(solution)/shard_map/middle/pallas_call | solution.py:529
  8.8 1.4 %collective-permute-done.2.side_x = f32[8,128]{1,0:T(8,128)S(1)} collective-permute-done((f32[8,128]{1,0:T(8,128)S(1)}, f32[8,128]{1,0:T(8,128)S(1)}, u32[]{:S(2)}, u32[]{:S(2)}) %collective-permute-start.2) | collective-permute-done | bytes 4128 | tf_op jit(solution)/shard_map/ppermute | solution.py:522
  10.2 0.0 collective-permute-done.3.side_z
  10.2 0.0 collective-permute-done.from_x
  10.2 0.0 collective-permute-done.1.from_z
  10.3 0.0 copy-done
  10.3 1.6 %leg.1 = (f32[2,16,768]{2,1,0:T(8,128)S(1)}, f32[16,768]{1,0:T(8,128)S(1)}, f32[16,256]{1,0:T(8,128)S(1)}) custom-call(f32[112,128]{1,0:T(8,128)S(1)} %get-tuple-element.44.coefficients, f32[4,16,768]{2,1,0:T(8,128)S(1)} %get-tuple-element.45.fields, f32[2,16,768]{2,1,0:T(8,128)S(1)} %copy-done, f32[40,768]{1,0:T(8,128)S(1)} %collective-permute-done.from_x, ...), custom_call_target="tpu_custom_call" | custom-call | tf_op jit(solution)/shard_map/leg/pallas_call | solution.py:545
  11.9 12.1 %all_to_all.11 = f32[16,1,256]{2,1,0:T(1,128)S(1)} all-to-all(f32[16,1,256]{2,1,0:T(1,128)S(1)} %copy.10), channel_id=1, replica_groups=mesh['grp'=2,'gx'=8,'gy'=2] {'gx','gy'}, dimensions={0} | all-to-all | bytes 32768 | tf_op jit(solution)/shard_map/all_to_all | solution.py:559
  24.0 0.8 %scale.1 = (f32[16,768]{1,0:T(8,128)}, f32[1,1]{1,0:T(1,128)}, f32[2,16,768]{2,1,0:T(8,128)}) custom-call(f32[16,256]{1,0:T(8,128)S(1)} %bitcast.5, f32[16,768]{1,0:T(8,128)S(1)} %get-tuple-element.80.gradient, f32[2,16,768]{2,1,0:T(8,128)S(1)} %get-tuple-element.81.held_multiplier), custom_call_target="tpu_custom_call" | custom-call | tf_op jit(solution)/shard_map/scale/pallas_call | solution.py:560
  (2 shorter events, 0.0 us)
Async XLA Ops:
  1.8 8.5 %collective-permute-start = (f32[40,768]{1,0:T(8,128)S(1)}, f32[40,768]{1,0:T(8,128)S(1)}, u32[]{:S(2)}, u32[]{:S(2)}) collective-permute-start(f32[40,768]{1,0:T(8,128)S(1)} %get-tuple-element.46), channel_id=1, source_target_pairs={{0,2},{2,0},{4,6},{6,4},{8,10},{10,8},{12,14},{14,12},{1,3},{3,1},... | collective-permute-start | bytes 368648 | tf_op jit(solution)/shard_map/ppermute | solution.py:519
  4.8 5.5 %collective-permute-start.1 = (f32[40,768]{1,0:T(8,128)S(1)}, f32[40,768]{1,0:T(8,128)S(1)}, u32[]{:S(2)}, u32[]{:S(2)}) collective-permute-start(f32[40,768]{1,0:T(8,128)S(1)} %get-tuple-element.47), channel_id=1, source_target_pairs={{2,4},{3,5},{4,2},{5,3},{6,8},{7,9},{8,6},{9,7},{10,12},{11,13},{1... | collective-permute-start | bytes 368648 | tf_op jit(solution)/shard_map/ppermute | solution.py:520
  4.8 3.2 %collective-permute-start.4 = (f32[64,128]{1,0:T(8,128)S(1)}, f32[64,128]{1,0:T(8,128)S(1)}, u32[]{:S(2)}, u32[]{:S(2)}) collective-permute-start(f32[64,128]{1,0:T(8,128)S(1)} %get-tuple-element.50), channel_id=1, source_target_pairs={{0,1},{1,0},{2,3},{3,2},{4,5},{5,4},{6,7},{7,6},{8,9},{9,8},{10,11... | collective-permute-start | bytes 98312 | tf_op jit(solution)/shard_map/ppermute | solution.py:521
  5.3 5.0 %collective-permute-start.2 = (f32[8,128]{1,0:T(8,128)S(1)}, f32[8,128]{1,0:T(8,128)S(1)}, u32[]{:S(2)}, u32[]{:S(2)}) collective-permute-start(f32[8,128]{1,0:T(8,128)S(1)} %get-tuple-element.48), channel_id=1, source_target_pairs={{0,3},{1,2},{2,1},{3,0},{4,7},{5,6},{6,5},{7,4},{8,11},{9,10},{10,... | collective-permute-start | bytes 12296 | tf_op jit(solution)/shard_map/ppermute | solution.py:522
  7.9 2.3 %collective-permute-start.3 = (f32[8,128]{1,0:T(8,128)S(1)}, f32[8,128]{1,0:T(8,128)S(1)}, u32[]{:S(2)}, u32[]{:S(2)}) collective-permute-start(f32[8,128]{1,0:T(8,128)S(1)} %get-tuple-element.49), channel_id=1, source_target_pairs={{2,5},{3,4},{4,3},{5,2},{6,9},{7,8},{8,7},{9,6},{10,13},{11,12},{1... | collective-permute-start | bytes 12296 | tf_op jit(solution)/shard_map/ppermute | solution.py:523
  7.9 2.3 %copy-start = (f32[2,16,768]{2,1,0:T(8,128)S(1)}, f32[2,16,768]{2,1,0:T(8,128)}, u32[]{:S(2)}) copy-start(f32[2,16,768]{2,1,0:T(8,128)} %velocity.1) | copy-start | bytes 294916

commit v9 on v8

--- a/solution.py
+++ b/solution.py
@@ -20,10 +20,24 @@
     return lax.broadcasted_iota(jnp.int32, (8, LANES), 1)
 
 
-def pack_kernel(
-    bounds, misfit, visc, friction, ice, grounded,
-    fields, coefficients, x_send, z_send, side_send, x_corner, z_corner,
-    levels, visc_in, friction_in, ice_in, grounded_in, sems,
+def rim_rows(fields, n, low_half):
+    first, last = fields[n, :8, :], fields[n, 8:16, :]
+    return jnp.where(low_half, last, first), jnp.where(low_half, first, last)
+
+
+def rim_tail(fields, low_half):
+    sublanes = lax.broadcasted_iota(jnp.int32, (8, fields.shape[2]), 0)
+    down = up = jnp.zeros(sublanes.shape, F32)
+    for n in range(4):
+        here = sublanes // 2 == n
+        down = jnp.where(here, pltpu.roll(fields[n, :8, :], (2 * n + 2) % 8, 0), down)
+        up = jnp.where(here, pltpu.roll(fields[n, 8:16, :], 2 * n, 0), up)
+    return jnp.where(low_half, down, up), jnp.where(low_half, up, down)
+
+
+def first_pack_kernel(
+    bounds, misfit, visc, friction, ice, grounded, fields, levels, x_send,
+    levels_in, visc_in, friction_in, ice_in, grounded_in, sems,
 ):
     copies = [
         pltpu.make_async_copy(source, target, sems.at[n])
@@ -33,35 +47,35 @@
             (ice, ice_in),
             (friction, friction_in),
             (grounded, grounded_in),
-            (bounds, levels),
+            (bounds, levels_in),
         ))
     ]
     for copy in copies:
         copy.start()
-    rows, cols = visc.shape
-    left = lax.axis_index("gy") == 0
-    at, last_at = lax.axis_index("gx"), lax.axis_size("gx") - 1
-    low_half = at % 2 == 0
-    at_end = (at == 0) | (at == last_at)
-    for copy in copies[:5]:
+    low_half = lax.axis_index("gx") % 2 == 0
+    for copy in copies:
         copy.wait()
     fields[2] = visc_in[...] * ice_in[...].astype(F32)
     fields[3] = friction_in[...] * grounded_in[...].astype(F32)
-    sublanes = lax.broadcasted_iota(jnp.int32, (8, cols), 0)
-    down_tail = up_tail = jnp.zeros((8, cols), F32)
     for n in range(4):
-        last, first = fields[n, rows - 8 :, :], fields[n, :8, :]
-        x_send[8 * n : 8 * n + 8, :] = jnp.where(low_half, last, first)
-        z_send[8 * n : 8 * n + 8, :] = jnp.where(at_end, 0.0, jnp.where(low_half, first, last))
-        here = sublanes // 2 == n
-        down_tail = jnp.where(here, pltpu.roll(fields[n, rows - 16 : rows - 8, :], (2 * n + 2) % 8, 0), down_tail)
-        up_tail = jnp.where(here, pltpu.roll(fields[n, 8:16, :], 2 * n, 0), up_tail)
+        x_send[8 * n : 8 * n + 8, :] = rim_rows(fields, n, low_half)[0]
+        levels[8 * n : 8 * n + 8, :] = jnp.full((8, LANES), levels_in[n])
+    x_send[32:, :] = rim_tail(fields, low_half)[0]
+
+
+def second_pack_kernel(fields, levels, x_send, coefficients, z_send, side_send, x_corner, z_corner):
+    rows, cols = fields.shape[1:]
+    left = lax.axis_index("gy") == 0
+    position, last_position = lax.axis_index("gx"), lax.axis_size("gx") - 1
+    low_half = position % 2 == 0
+    at_end = (position == 0) | (position == last_position)
+    for n in range(4):
+        z_send[8 * n : 8 * n + 8, :] = jnp.where(at_end, 0.0, rim_rows(fields, n, low_half)[1])
         side_send[rows * n : rows * n + rows, :] = jnp.where(
             left, fields[n, :, cols - LANES :], fields[n, :, :LANES]
         )
-    x_send[32:, :] = jnp.where(low_half, down_tail, up_tail)
-    z_send[32:, :] = jnp.where(at_end, 0.0, jnp.where(low_half, up_tail, down_tail))
-    sublanes = sublanes[:, :LANES]
+    z_send[32:, :] = jnp.where(at_end, 0.0, rim_tail(fields, low_half)[1])
+    sublanes = lax.broadcasted_iota(jnp.int32, (8, LANES), 0)
     own_columns_of = lane_ids() // EDGE == sublanes
     for source, target in ((x_send, x_corner), (z_send, z_corner)):
         packed = jnp.zeros((8, LANES), F32)
@@ -75,17 +89,15 @@
             row = jnp.sum(jnp.where(own_columns_of, columns, 0.0), axis=0, keepdims=True)
             packed = jnp.where(sublanes == q, row, packed)
         target[...] = packed
-    copies[5].wait()
     for sweep in range(2):
-        lower = jnp.full((8, LANES), levels[2 * sweep])
-        upper = jnp.full((8, LANES), levels[2 * sweep + 1])
+        lower, upper = levels[16 * sweep : 16 * sweep + 8, :], levels[16 * sweep + 8 : 16 * sweep + 16, :]
         middle = 0.5 * (upper + lower)
         half = 0.5 * (upper - lower)
-        spread = middle / half
-        factor = 1.0 / spread
+        ratio = middle / half
+        factor = 1.0 / ratio
         values = [1.0 / middle]
         for step in range(DEG - 1):
-            factor_next = 1.0 / (2.0 * spread - factor)
+            factor_next = 1.0 / (2.0 * ratio - factor)
             values += [factor_next * factor, 2.0 * factor_next / half]
             factor = factor_next
         for n, value in enumerate(values):
@@ -169,7 +181,8 @@
     return s * (both + a), s * (both + b), (0.5 * s) * (c + d)
 
 
-def forces(x, following, stiff, near, far, low, high, shift):
+def forces(x, following, stiff, low, high, shift):
+    applied = {}
     def gradients(row):
         return edge_gradients([at(part, row) for part in x], [at(part, row) for part in following])
 
@@ -180,15 +193,16 @@
         now = cell_forces(at(stiff, row), here, after)
         shear, shear_step = before[2] + now[2], before[2] - now[2]
         normal_step, normal = before[0] - now[0], before[1] + now[1]
-        put(near[0], row, normal_step - shear)
-        put(near[1], row, shear_step - normal)
-        put(far[0], row, to_right(normal_step + shear, shift))
-        put(far[1], row, to_right(shear_step + normal, shift))
+        applied[row] = (
+            (normal_step - shear, to_right(normal_step + shear, shift)),
+            (shear_step - normal, to_right(shear_step + normal, shift)),
+        )
         here, before = after, now
-
-
-def remaining(n, value, f, beta, near, far, row):
-    return (at(f[n], row) - at(beta, row) * value) - (at(near[n], row) + at(far[n], row))
+    return applied
+
+
+def remaining(n, value, f, beta, applied, row):
+    return (at(f[n], row) - at(beta, row) * value) - (applied[row][n][0] + applied[row][n][1])
 
 
 def begin(x, following, f, coefficients, rows, shift):
@@ -200,20 +214,22 @@
             put(following[n], row, to_left(value, shift))
 
 
-def advance(levels, followings, f, beta, stiff, near, far, coefficients, step, spans, mask_of):
+def advance(levels, followings, f, beta, stiff, coefficients, step, spans, mask_of):
     keep = coefficients[8 + 16 * step : 16 + 16 * step, :]
     gain = coefficients[16 + 16 * step : 24 + 16 * step, :]
     gains = {}
     x, new = levels[step], levels[step + 1]
+    applied = {}
     for low, high in spans:
-        forces(x, followings[step], stiff, near, far, low, high, 1)
+        applied.update(forces(x, followings[step], stiff, low, high, 1))
+    for low, high in spans:
         for row in range(low, high):
             mask = mask_of(row)
             part = gains.setdefault(id(mask), gain * mask)
             for n in range(2):
                 value = at(x[n], row)
                 change = value if step == 0 else value - at(levels[step - 1][n], row)
-                value = value + keep * change + part * remaining(n, value, f, beta, near, far, row)
+                value = value + keep * change + part * remaining(n, value, f, beta, applied, row)
                 put(new[n], row, value)
                 put(followings[step + 1][n], row, to_left(value, 1))
 
@@ -237,7 +253,7 @@
     rows, cols = fields.shape[1:]
     end = RIM + rows
     left = lax.axis_index("gy") == 0
-    outs, scratch = refs[:-4], refs[-4:]
+    outs = refs
     own, cell_ref, squares_out = outs[:4], outs[4], outs[5]
     level_refs, following_refs = pairs_of(outs[6 : 6 + 2 * DEG]), pairs_of(outs[6 + 2 * DEG : 6 + 4 * DEG])
     residual_refs, coarse_refs = outs[6 + 4 * DEG : 8 + 4 * DEG], outs[8 + 4 * DEG :]
@@ -253,20 +269,19 @@
     cell = whole_rows(cell_ref)
     levels = [tuple(map(whole_rows, pair)) for pair in level_refs]
     followings = [tuple(map(whole_rows, pair)) for pair in following_refs]
-    near, far = (tuple(map(whole_rows, pair)) for pair in pairs_of(scratch))
     inside = inside_columns(left, cols)
     stiffness(visc, cell, RIM, end - 1, 1)
     begin(levels[0], followings[0], f, coefficients, range(RIM, end), 1)
     for step in range(DEG - 1):
         span = (RIM + step + 1, end - step - 1)
-        advance(levels, followings, f, beta, cell, near, far, coefficients, step, (span,), lambda row: inside)
+        advance(levels, followings, f, beta, cell, coefficients, step, (span,), lambda row: inside)
     residual = tuple(map(whole_rows, residual_refs))
     low, high = RIM + DEG, end - DEG
-    forces(levels[-1], followings[-1], cell, near, far, low, high, 1)
+    applied = forces(levels[-1], followings[-1], cell, low, high, 1)
     squares = jnp.zeros((8, LANES), F32)
     for row in range(low, high):
         for n in range(2):
-            value = inside * remaining(n, at(levels[-1][n], row), f, beta, near, far, row)
+            value = inside * remaining(n, at(levels[-1][n], row), f, beta, applied, row)
             put(residual[n], row, value)
             squares = squares + value * value
     squares_out[...] = squares
@@ -334,7 +349,6 @@
     levels = [tuple(joined(take(1)[0], ref, n) for ref in pair) for n, pair in enumerate(level_refs)]
     followings = [tuple(joined(take(1)[0], ref, n) for ref in pair) for n, pair in enumerate(following_refs)]
     residual = tuple(joined(take(1)[0], ref, DEG) for ref in residual_refs)
-    near, far = (tuple(Rows((0, total, ref, 0)) for ref in take(2)) for _ in range(2))
 
     inside = inside_columns(left, cols)
     above = inside * jnp.where(gx_at > 0, 1.0, 0.0)
@@ -348,14 +362,14 @@
     begin(levels[0], followings[0], f, coefficients, [*range(RIM), *range(end, total)], 1)
     for step in range(DEG - 1):
         spans = ((step + 1, RIM + step + 1), (end - step - 1, total - step - 1))
-        advance(levels, followings, f, beta, cell, near, far, coefficients, step, spans, mask_of)
+        advance(levels, followings, f, beta, cell, coefficients, step, spans, mask_of)
     x = levels[-1]
     squares = squares_ref[...]
     for low, high in ((DEG, RIM + DEG), (end - DEG, total - DEG)):
-        forces(x, followings[-1], cell, near, far, low, high, 1)
+        applied = forces(x, followings[-1], cell, low, high, 1)
         for row in range(low, high):
             for n in range(2):
-                value = mask_of(row) * remaining(n, at(x[n], row), f, beta, near, far, row)
+                value = mask_of(row) * remaining(n, at(x[n], row), f, beta, applied, row)
                 put(residual[n], row, value)
                 if RIM <= row < end:
                     squares = squares + value * value
@@ -487,19 +501,12 @@
     params = pltpu.CompilerParams(vmem_limit_bytes=32 * 1024 * 1024)
 
     held = pl.BlockSpec(memory_space=pltpu.HBM)
-    fields, coefficients, x_send, z_send, side_send, x_corner, z_corner = pl.pallas_call(
-        pack_kernel,
-        out_shape=(
-            shaped((4, rows, cols), F32),
-            shaped((16 * (2 * DEG - 1), LANES), F32),
-            shaped((4 * RIM, cols), F32),
-            shaped((4 * RIM, cols), F32),
-            shaped((4 * rows, LANES), F32),
-            shaped((8, LANES), F32),
-            shaped((8, LANES), F32),
-        ),
+    inputs = (bounds, misfit, viscosity, friction, ice, grounded)
+    fields, levels, x_send = pl.pallas_call(
+        first_pack_kernel,
+        out_shape=(shaped((4, rows, cols), F32), shaped((32, LANES), F32), shaped((4 * RIM, cols), F32)),
         in_specs=[held] * 6,
-        out_specs=[whole] * 7,
+        out_specs=[whole] * 3,
         scratch_shapes=[
             pltpu.SMEM((4,), F32),
             pltpu.VMEM((rows, cols), F32),
@@ -509,8 +516,22 @@
             pltpu.SemaphoreType.DMA((6,)),
         ],
         compiler_params=params,
-        name="pack",
-    )(*(pltpu.with_memory_space_constraint(x, pltpu.HBM) for x in (bounds, misfit, viscosity, friction, ice, grounded)))
+        name="first_pack",
+    )(*(pltpu.with_memory_space_constraint(x, pltpu.HBM) for x in inputs))
+    coefficients, z_send, side_send, x_corner, z_corner = pl.pallas_call(
+        second_pack_kernel,
+        out_shape=(
+            shaped((16 * (2 * DEG - 1), LANES), F32),
+            shaped((4 * RIM, cols), F32),
+            shaped((4 * rows, LANES), F32),
+            shaped((8, LANES), F32),
+            shaped((8, LANES), F32),
+        ),
+        in_specs=[whole] * 3,
+        out_specs=[whole] * 5,
+        compiler_params=params,
+        name="second_pack",
+    )(fields, levels, x_send)
 
     x_pairs = [(i, i ^ 1) for i in range(gx_size)]
     z_pairs = [(2 * i + c, 2 * j + c) for i in range(1, gx_size - 1) for j in (i + 1 if i % 2 else i - 1,) for c in (0, 1)]
@@ -531,7 +552,6 @@
         out_shape=[owned] * 5 + [pltpu.VMEM((8, LANES), F32)] + [owned] * (4 * DEG + 2) + [halved] * 4,
         in_specs=[whole] * 3,
         out_specs=[whole] * (12 + 4 * DEG),
-        scratch_shapes=[owned] * 4,
         compiler_params=params,
         name="middle",
     )(coefficients, fields, side)
@@ -551,7 +571,7 @@
         ),
         in_specs=[whole] * (7 + len(middle)),
         out_specs=[whole] * 3,
-        scratch_shapes=[rim] * 5 + [owned] * 2 + [corner] * 2 + [fine] * (7 + 4 * DEG) + [coarse] * 14,
+        scratch_shapes=[rim] * 5 + [owned] * 2 + [corner] * 2 + [fine] * (3 + 4 * DEG) + [coarse] * 14,
         compiler_params=params,
         name="leg",
     )(coefficients, fields, velocity, from_x, from_z, side_x, side_z, *middle)

time: 25 us -> 24.8 us (level)
  waiting for transfers between devices: 1.41 us -> 1.15 us
    ppermute x1, waiting for transfers between devices: 1.4 us -> 1.14 us  [body(): lax.ppermute(x_corner, AXES, [(2 * i + c, 2 * j + 1 - c) for i, j in x_pa...]
    pallas_call x1 -> x2, Pallas kernels: 1.13 us -> 1.11 us  [the longest x1 1.01 us: body(): pl.pallas_call(first_pack_kernel, out_shape=(shaped((4, rows, cols), F32)...]
where the time goes in v9:
time: 24.8 us; the launch traced here: 24.7 us
  blocking collectives  12.2 us (49%)
  starting transfers between devices  6.22 us (25%)
  Pallas kernels  4.39 us (18%)
  waiting for transfers between devices  1.15 us (5%)
  between operations  0.68 us (3%)
    all_to_all x1, blocking collectives, body(): gathered = lax.all_to_all(sums, AXES, 0, 0, tiled=True)  12.2 us
    ppermute x1, starting transfers between devices, body(): from_x = lax.ppermute(x_send, 'gx', x_pairs)  3 us
    ppermute x1, starting transfers between devices, body(): lax.ppermute(x_corner, AXES, [(2 * i + c, 2 * j + 1 - c) for i, j in x_pa...  2.64 us
    pallas_call x1, Pallas kernels, body(): pl.pallas_call(leg_kernel, out_shape=(pltpu.VMEM((2, rows, cols), F32), p...  1.59 us
    ppermute x1, waiting for transfers between devices, body(): lax.ppermute(x_corner, AXES, [(2 * i + c, 2 * j + 1 - c) for i, j in x_pa...  1.14 us
    pallas_call x1, Pallas kernels, body(): pl.pallas_call(first_pack_kernel, out_shape=(shaped((4, rows, cols), F32)...  1.01 us
    pallas_call x1, Pallas kernels, body(): pl.pallas_call(middle_kernel, out_shape=[owned] * 5 + [pltpu.VMEM((8, LAN...  0.9 us
    pallas_call x1, Pallas kernels, body(): pl.pallas_call(functools.partial(scale_kernel, nodes), out_shape=(pltpu.H...  0.79 us
  transfers between devices with their start and end apart: 5, of which 1 were waited for; matrix products, arithmetic and copies ran while one was open for 0% of the time, Pallas kernels for 4%

profile of v9, /device:TPU:0, one launch (start us, length us, event | category | flops | bytes accessed | tf_op | source)
XLA Modules:
  0.0 24.7 jit_solution(18418450725204200446)
XLA Ops:
  0.6 1.0 %first_pack.1 = (f32[4,16,768]{2,1,0:T(8,128)S(1)}, f32[32,128]{1,0:T(8,128)S(1)}, f32[40,768]{1,0:T(8,128)S(1)}) custom-call(f32[4]{0:T(128)} %bounds.1, f32[2,16,768]{2,1,0:T(8,128)} %misfit.1, f32[16,768]{1,0:T(8,128)} %visc.1, f32[16,768]{1,0:T(8,128)} %friction.1, s32[16,768]{1,0:T(8,128)} %ice.1, s32[16,768]{1,0:T(8,128)} %grounded.1), custom_call_target="tpu_custom_call" | custom-call | tf_op jit(solution)/shard_map/first_pack/pallas_call | solution.py:505
  1.6 3.0 %collective-permute-start = (f32[40,768]{1,0:T(8,128)S(1)}, f32[40,768]{1,0:T(8,128)S(1)}, u32[]{:S(2)}, u32[]{:S(2)}) collective-permute-start(f32[40,768]{1,0:T(8,128)S(1)} %get-tuple-element.47.x_send), channel_id=1, source_target_pairs={{0,2},{2,0},{4,6},{6,4},{8,10},{10,8},{12,14},{14,12},{1,3},{3,1},... | collective-permute-start | bytes 368648 | tf_op jit(solution)/shard_map/ppermute | solution.py:540
  4.7 0.1 second_pack.1
  4.8 0.1 collective-permute-start.1
  4.8 0.5 %collective-permute-start.4 = (f32[64,128]{1,0:T(8,128)S(1)}, f32[64,128]{1,0:T(8,128)S(1)}, u32[]{:S(2)}, u32[]{:S(2)}) collective-permute-start(f32[64,128]{1,0:T(8,128)S(1)} %get-tuple-element.52), channel_id=1, source_target_pairs={{0,1},{1,0},{2,3},{3,2},{4,5},{5,4},{6,7},{7,6},{8,9},{9,8},{10,11... | collective-permute-start | bytes 98312 | tf_op jit(solution)/shard_map/ppermute | solution.py:542
  5.3 2.6 %collective-permute-start.2 = (f32[8,128]{1,0:T(8,128)S(1)}, f32[8,128]{1,0:T(8,128)S(1)}, u32[]{:S(2)}, u32[]{:S(2)}) collective-permute-start(f32[8,128]{1,0:T(8,128)S(1)} %get-tuple-element.50), channel_id=1, source_target_pairs={{0,3},{1,2},{2,1},{3,0},{4,7},{5,6},{6,5},{7,4},{8,11},{9,10},{10,... | collective-permute-start | bytes 12296 | tf_op jit(solution)/shard_map/ppermute | solution.py:543
  8.0 0.0 collective-permute-start.3
  8.0 0.0 collective-permute-done.4.side
  8.0 0.0 copy-start
  8.0 0.9 %middle.1 = (f32[128,128]{1,0:T(8,128)S(1)}, f32[128,128]{1,0:T(8,128)S(1)}, f32[128,128]{1,0:T(8,128)S(1)}, f32[128,128]{1,0:T(8,128)S(1)}, f32[128,128]{1,0:T(...) custom-call(f32[112,128]{1,0:T(8,128)S(1)} %get-tuple-element.48.coe, ...), custom_call_target="tpu_custom_call" | custom-call | tf_op jit(solution)/shard_map/middle/pallas_call | solution.py:550
  8.9 1.1 %collective-permute-done.2.side_x = f32[8,128]{1,0:T(8,128)S(1)} collective-permute-done((f32[8,128]{1,0:T(8,128)S(1)}, f32[8,128]{1,0:T(8,128)S(1)}, u32[]{:S(2)}, u32[]{:S(2)}) %collective-permute-start.2) | collective-permute-done | bytes 4128 | tf_op jit(solution)/shard_map/ppermute | solution.py:543
  10.0 0.0 collective-permute-done.3.side_z
  10.0 0.0 collective-permute-done.from_x
  10.0 0.0 collective-permute-done.1.from_z
  10.0 0.0 copy-done
  10.1 1.6 %leg.1 = (f32[2,16,768]{2,1,0:T(8,128)S(1)}, f32[16,768]{1,0:T(8,128)S(1)}, f32[16,256]{1,0:T(8,128)S(1)}) custom-call(f32[112,128]{1,0:T(8,128)S(1)} %get-tuple-element.48.coefficients, f32[4,16,768]{2,1,0:T(8,128)S(1)} %get-tuple-element.45.fields, f32[2,16,768]{2,1,0:T(8,128)S(1)} %copy-done, f32[40,768]{1,0:T(8,128)S(1)} %collective-permute-done.from_x, ...), custom_call_target="tpu_custom_call" | custom-call | tf_op jit(solution)/shard_map/leg/pallas_call | solution.py:565
  11.7 12.2 %all_to_all.11 = f32[16,1,256]{2,1,0:T(1,128)S(1)} all-to-all(f32[16,1,256]{2,1,0:T(1,128)S(1)} %copy.10), channel_id=1, replica_groups=mesh['grp'=2,'gx'=8,'gy'=2] {'gx','gy'}, dimensions={0} | all-to-all | bytes 32768 | tf_op jit(solution)/shard_map/all_to_all | solution.py:579
  23.9 0.8 %scale.1 = (f32[16,768]{1,0:T(8,128)}, f32[1,1]{1,0:T(1,128)}, f32[2,16,768]{2,1,0:T(8,128)}) custom-call(f32[16,256]{1,0:T(8,128)S(1)} %bitcast.5, f32[16,768]{1,0:T(8,128)S(1)} %get-tuple-element.82.gradient, f32[2,16,768]{2,1,0:T(8,128)S(1)} %get-tuple-element.83.held_multiplier), custom_call_target="tpu_custom_call" | custom-call | tf_op jit(solution)/shard_map/scale/pallas_call | solution.py:580
  (2 shorter events, 0.0 us)
Async XLA Ops:
  1.6 8.4 %collective-permute-start = (f32[40,768]{1,0:T(8,128)S(1)}, f32[40,768]{1,0:T(8,128)S(1)}, u32[]{:S(2)}, u32[]{:S(2)}) collective-permute-start(f32[40,768]{1,0:T(8,128)S(1)} %get-tuple-element.47.x_send), channel_id=1, source_target_pairs={{0,2},{2,0},{4,6},{6,4},{8,10},{10,8},{12,14},{14,12},{1,3},{3,1},... | collective-permute-start | bytes 368648 | tf_op jit(solution)/shard_map/ppermute | solution.py:540
  4.8 5.3 %collective-permute-start.1 = (f32[40,768]{1,0:T(8,128)S(1)}, f32[40,768]{1,0:T(8,128)S(1)}, u32[]{:S(2)}, u32[]{:S(2)}) collective-permute-start(f32[40,768]{1,0:T(8,128)S(1)} %get-tuple-element.49), channel_id=1, source_target_pairs={{2,4},{3,5},{4,2},{5,3},{6,8},{7,9},{8,6},{9,7},{10,12},{11,13},{1... | collective-permute-start | bytes 368648 | tf_op jit(solution)/shard_map/ppermute | solution.py:541
  4.8 3.1 %collective-permute-start.4 = (f32[64,128]{1,0:T(8,128)S(1)}, f32[64,128]{1,0:T(8,128)S(1)}, u32[]{:S(2)}, u32[]{:S(2)}) collective-permute-start(f32[64,128]{1,0:T(8,128)S(1)} %get-tuple-element.52), channel_id=1, source_target_pairs={{0,1},{1,0},{2,3},{3,2},{4,5},{5,4},{6,7},{7,6},{8,9},{9,8},{10,11... | collective-permute-start | bytes 98312 | tf_op jit(solution)/shard_map/ppermute | solution.py:542
  5.3 4.7 %collective-permute-start.2 = (f32[8,128]{1,0:T(8,128)S(1)}, f32[8,128]{1,0:T(8,128)S(1)}, u32[]{:S(2)}, u32[]{:S(2)}) collective-permute-start(f32[8,128]{1,0:T(8,128)S(1)} %get-tuple-element.50), channel_id=1, source_target_pairs={{0,3},{1,2},{2,1},{3,0},{4,7},{5,6},{6,5},{7,4},{8,11},{9,10},{10,... | collective-permute-start | bytes 12296 | tf_op jit(solution)/shard_map/ppermute | solution.py:543
  8.0 2.1 %collective-permute-start.3 = (f32[8,128]{1,0:T(8,128)S(1)}, f32[8,128]{1,0:T(8,128)S(1)}, u32[]{:S(2)}, u32[]{:S(2)}) collective-permute-start(f32[8,128]{1,0:T(8,128)S(1)} %get-tuple-element.51), channel_id=1, source_target_pairs={{2,5},{3,4},{4,3},{5,2},{6,9},{7,8},{8,7},{9,6},{10,13},{11,12},{1... | collective-permute-start | bytes 12296 | tf_op jit(solution)/shard_map/ppermute | solution.py:544
  8.0 2.1 %copy-start = (f32[2,16,768]{2,1,0:T(8,128)S(1)}, f32[2,16,768]{2,1,0:T(8,128)}, u32[]{:S(2)}) copy-start(f32[2,16,768]{2,1,0:T(8,128)} %velocity.1) | copy-start | bytes 294916

commit v10 on v9

--- a/solution.py
+++ b/solution.py
@@ -181,7 +181,7 @@
     return s * (both + a), s * (both + b), (0.5 * s) * (c + d)
 
 
-def forces(x, following, stiff, low, high, shift):
+def forces(x, following, stiff, low, high):
     applied = {}
     def gradients(row):
         return edge_gradients([at(part, row) for part in x], [at(part, row) for part in following])
@@ -194,15 +194,15 @@
         shear, shear_step = before[2] + now[2], before[2] - now[2]
         normal_step, normal = before[0] - now[0], before[1] + now[1]
         applied[row] = (
-            (normal_step - shear, to_right(normal_step + shear, shift)),
-            (shear_step - normal, to_right(shear_step + normal, shift)),
+            (normal_step - shear, normal_step + shear),
+            (shear_step - normal, shear_step + normal),
         )
         here, before = after, now
     return applied
 
 
 def remaining(n, value, f, beta, applied, row):
-    return (at(f[n], row) - at(beta, row) * value) - (applied[row][n][0] + applied[row][n][1])
+    return (at(f[n], row) - at(beta, row) * value) - (applied[row][n][0] + to_right(applied[row][n][1], 1))
 
 
 def begin(x, following, f, coefficients, rows, shift):
@@ -221,7 +221,7 @@
     x, new = levels[step], levels[step + 1]
     applied = {}
     for low, high in spans:
-        applied.update(forces(x, followings[step], stiff, low, high, 1))
+        applied.update(forces(x, followings[step], stiff, low, high))
     for low, high in spans:
         for row in range(low, high):
             mask = mask_of(row)
@@ -277,7 +277,7 @@
         advance(levels, followings, f, beta, cell, coefficients, step, (span,), lambda row: inside)
     residual = tuple(map(whole_rows, residual_refs))
     low, high = RIM + DEG, end - DEG
-    applied = forces(levels[-1], followings[-1], cell, low, high, 1)
+    applied = forces(levels[-1], followings[-1], cell, low, high)
     squares = jnp.zeros((8, LANES), F32)
     for row in range(low, high):
         for n in range(2):
@@ -348,7 +348,6 @@
     cell = Rows((0, RIM, cell_full, 0), (RIM, end - 1, cell_ref, 0), (end - 1, total, cell_full, end - 1))
     levels = [tuple(joined(take(1)[0], ref, n) for ref in pair) for n, pair in enumerate(level_refs)]
     followings = [tuple(joined(take(1)[0], ref, n) for ref in pair) for n, pair in enumerate(following_refs)]
-    residual = tuple(joined(take(1)[0], ref, DEG) for ref in residual_refs)
 
     inside = inside_columns(left, cols)
     above = inside * jnp.where(gx_at > 0, 1.0, 0.0)
@@ -365,14 +364,26 @@
         advance(levels, followings, f, beta, cell, coefficients, step, spans, mask_of)
     x = levels[-1]
     squares = squares_ref[...]
+    bases, others = {}, {}
     for low, high in ((DEG, RIM + DEG), (end - DEG, total - DEG)):
-        applied = forces(x, followings[-1], cell, low, high, 1)
+        applied = forces(x, followings[-1], cell, low, high)
         for row in range(low, high):
             for n in range(2):
-                value = mask_of(row) * remaining(n, at(x[n], row), f, beta, applied, row)
-                put(residual[n], row, value)
+                here, other = applied[row][n]
+                bases[n, row] = (at(f[n], row) - at(beta, row) * at(x[n], row)) - here
+                others[n, row] = other
                 if RIM <= row < end:
+                    value = inside * (bases[n, row] - to_right(other, 1))
                     squares = squares + value * value
+
+    def restrict_residual(n, i, lanes):
+        row = DEG + 2 * i
+        base, other = (part[n, row] + part[n, row + 1] for part in (bases, others))
+        if lanes == "even":
+            value = (base - other) + (to_left(base, 1) - to_right(other, 1))
+        else:
+            value = base + (to_right(base - other, 1) - to_right(other, 2))
+        return mask_of(row) * value
 
     even = lane_ids() % 2 == 0
     coarse_rim = (RIM - DEG) // 2
@@ -382,20 +393,27 @@
     def plain():
         return Rows((0, count, take(1)[0], 0))
 
-    def packed(source, ref, margin, scale):
+    def packed(make, ref, margin):
         first, last = coarse_rim + margin, coarse_rim + 2 * half - margin
         target = plain()
         for j in range(count):
             i, k = j, j + half
-            one = at(Rows((first, last, ref, margin)), i) if first <= i < last else restrict(source, i, "even", scale)
-            two = at(Rows((first, last, ref, margin)), k) if first <= k < last else restrict(source, k, "odd", scale)
+            one = at(Rows((first, last, ref, margin)), i) if first <= i < last else make(i, "even")
+            two = at(Rows((first, last, ref, margin)), k) if first <= k < last else make(k, "odd")
             put(target, j, jnp.where(even, one, two))
         return target
 
     c_visc, c_beta, *c_f = (
-        packed(source, ref, margin, scale)
-        for source, ref, margin, scale in zip(
-            (visc, beta, *residual), coarse_refs, (0, 0, DEG // 2, DEG // 2), (0.25, None, None, None)
+        packed(make, ref, margin)
+        for make, ref, margin in zip(
+            (
+                lambda i, lanes: restrict(visc, i, lanes, 0.25),
+                lambda i, lanes: restrict(beta, i, lanes),
+                functools.partial(restrict_residual, 0),
+                functools.partial(restrict_residual, 1),
+            ),
+            coarse_refs,
+            (0, 0, DEG // 2, DEG // 2),
         )
     )
     masks = [
@@ -571,7 +589,7 @@
         ),
         in_specs=[whole] * (7 + len(middle)),
         out_specs=[whole] * 3,
-        scratch_shapes=[rim] * 5 + [owned] * 2 + [corner] * 2 + [fine] * (3 + 4 * DEG) + [coarse] * 14,
+        scratch_shapes=[rim] * 5 + [owned] * 2 + [corner] * 2 + [fine] * (1 + 4 * DEG) + [coarse] * 14,
         compiler_params=params,
         name="leg",
     )(coefficients, fields, velocity, from_x, from_z, side_x, side_z, *middle)

time: 24.8 us -> 24.8 us (level)
  no operation moved by 1% of the time
where the time goes in v10:
time: 24.8 us; the launch traced here: 24.7 us
  blocking collectives  12.2 us (49%)
  starting transfers between devices  6.22 us (25%)
  Pallas kernels  4.37 us (18%)
  waiting for transfers between devices  1.15 us (5%)
  between operations  0.69 us (3%)
    all_to_all x1, blocking collectives, body(): gathered = lax.all_to_all(sums, AXES, 0, 0, tiled=True)  12.2 us
    ppermute x1, starting transfers between devices, body(): from_x = lax.ppermute(x_send, 'gx', x_pairs)  3 us
    ppermute x1, starting transfers between devices, body(): lax.ppermute(x_corner, AXES, [(2 * i + c, 2 * j + 1 - c) for i, j in x_pa...  2.64 us
    pallas_call x1, Pallas kernels, body(): pl.pallas_call(leg_kernel, out_shape=(pltpu.VMEM((2, rows, cols), F32), p...  1.57 us
    ppermute x1, waiting for transfers between devices, body(): lax.ppermute(x_corner, AXES, [(2 * i + c, 2 * j + 1 - c) for i, j in x_pa...  1.14 us
    pallas_call x1, Pallas kernels, body(): pl.pallas_call(first_pack_kernel, out_shape=(shaped((4, rows, cols), F32)...  1.01 us
    pallas_call x1, Pallas kernels, body(): pl.pallas_call(middle_kernel, out_shape=[owned] * 5 + [pltpu.VMEM((8, LAN...  0.9 us
    pallas_call x1, Pallas kernels, body(): pl.pallas_call(functools.partial(scale_kernel, nodes), out_shape=(pltpu.H...  0.79 us
  transfers between devices with their start and end apart: 5, of which 1 were waited for; matrix products, arithmetic and copies ran while one was open for 0% of the time, Pallas kernels for 4%

profile of v10, /device:TPU:0, one launch (start us, length us, event | category | flops | bytes accessed | tf_op | source)
XLA Modules:
  0.0 24.7 jit_solution(95585796801455983)
XLA Ops:
  0.6 1.0 %first_pack.1 = (f32[4,16,768]{2,1,0:T(8,128)S(1)}, f32[32,128]{1,0:T(8,128)S(1)}, f32[40,768]{1,0:T(8,128)S(1)}) custom-call(f32[4]{0:T(128)} %bounds.1, f32[2,16,768]{2,1,0:T(8,128)} %misfit.1, f32[16,768]{1,0:T(8,128)} %visc.1, f32[16,768]{1,0:T(8,128)} %friction.1, s32[16,768]{1,0:T(8,128)} %ice.1, s32[16,768]{1,0:T(8,128)} %grounded.1), custom_call_target="tpu_custom_call" | custom-call | tf_op jit(solution)/shard_map/first_pack/pallas_call | solution.py:523
  1.6 3.0 %collective-permute-start = (f32[40,768]{1,0:T(8,128)S(1)}, f32[40,768]{1,0:T(8,128)S(1)}, u32[]{:S(2)}, u32[]{:S(2)}) collective-permute-start(f32[40,768]{1,0:T(8,128)S(1)} %get-tuple-element.47.x_send), channel_id=1, source_target_pairs={{0,2},{2,0},{4,6},{6,4},{8,10},{10,8},{12,14},{14,12},{1,3},{3,1},... | collective-permute-start | bytes 368648 | tf_op jit(solution)/shard_map/ppermute | solution.py:558
  4.7 0.1 second_pack.1
  4.8 0.1 collective-permute-start.1
  4.8 0.5 %collective-permute-start.4 = (f32[64,128]{1,0:T(8,128)S(1)}, f32[64,128]{1,0:T(8,128)S(1)}, u32[]{:S(2)}, u32[]{:S(2)}) collective-permute-start(f32[64,128]{1,0:T(8,128)S(1)} %get-tuple-element.52), channel_id=1, source_target_pairs={{0,1},{1,0},{2,3},{3,2},{4,5},{5,4},{6,7},{7,6},{8,9},{9,8},{10,11... | collective-permute-start | bytes 98312 | tf_op jit(solution)/shard_map/ppermute | solution.py:560
  5.3 2.6 %collective-permute-start.2 = (f32[8,128]{1,0:T(8,128)S(1)}, f32[8,128]{1,0:T(8,128)S(1)}, u32[]{:S(2)}, u32[]{:S(2)}) collective-permute-start(f32[8,128]{1,0:T(8,128)S(1)} %get-tuple-element.50), channel_id=1, source_target_pairs={{0,3},{1,2},{2,1},{3,0},{4,7},{5,6},{6,5},{7,4},{8,11},{9,10},{10,... | collective-permute-start | bytes 12296 | tf_op jit(solution)/shard_map/ppermute | solution.py:561
  8.0 0.0 collective-permute-start.3
  8.0 0.0 collective-permute-done.4.side
  8.0 0.0 copy-start
  8.0 0.9 %middle.1 = (f32[128,128]{1,0:T(8,128)S(1)}, f32[128,128]{1,0:T(8,128)S(1)}, f32[128,128]{1,0:T(8,128)S(1)}, f32[128,128]{1,0:T(8,128)S(1)}, f32[128,128]{1,0:T(...) custom-call(f32[112,128]{1,0:T(8,128)S(1)} %get-tuple-element.48.coe, ...), custom_call_target="tpu_custom_call" | custom-call | tf_op jit(solution)/shard_map/middle/pallas_call | solution.py:568
  8.9 1.1 %collective-permute-done.2.side_x = f32[8,128]{1,0:T(8,128)S(1)} collective-permute-done((f32[8,128]{1,0:T(8,128)S(1)}, f32[8,128]{1,0:T(8,128)S(1)}, u32[]{:S(2)}, u32[]{:S(2)}) %collective-permute-start.2) | collective-permute-done | bytes 4128 | tf_op jit(solution)/shard_map/ppermute | solution.py:561
  10.0 0.0 collective-permute-done.3.side_z
  10.0 0.0 collective-permute-done.from_x
  10.0 0.0 collective-permute-done.1.from_z
  10.0 0.0 copy-done
  10.1 1.6 %leg.1 = (f32[2,16,768]{2,1,0:T(8,128)S(1)}, f32[16,768]{1,0:T(8,128)S(1)}, f32[16,256]{1,0:T(8,128)S(1)}) custom-call(f32[112,128]{1,0:T(8,128)S(1)} %get-tuple-element.48.coefficients, f32[4,16,768]{2,1,0:T(8,128)S(1)} %get-tuple-element.45.fields, f32[2,16,768]{2,1,0:T(8,128)S(1)} %copy-done, f32[40,768]{1,0:T(8,128)S(1)} %collective-permute-done.from_x, ...), custom_call_target="tpu_custom_call" | custom-call | tf_op jit(solution)/shard_map/leg/pallas_call | solution.py:583
  11.7 12.2 %all_to_all.11 = f32[16,1,256]{2,1,0:T(1,128)S(1)} all-to-all(f32[16,1,256]{2,1,0:T(1,128)S(1)} %copy.10), channel_id=1, replica_groups=mesh['grp'=2,'gx'=8,'gy'=2] {'gx','gy'}, dimensions={0} | all-to-all | bytes 32768 | tf_op jit(solution)/shard_map/all_to_all | solution.py:597
  23.9 0.8 %scale.1 = (f32[16,768]{1,0:T(8,128)}, f32[1,1]{1,0:T(1,128)}, f32[2,16,768]{2,1,0:T(8,128)}) custom-call(f32[16,256]{1,0:T(8,128)S(1)} %bitcast.5, f32[16,768]{1,0:T(8,128)S(1)} %get-tuple-element.82.gradient, f32[2,16,768]{2,1,0:T(8,128)S(1)} %get-tuple-element.83.held_multiplier), custom_call_target="tpu_custom_call" | custom-call | tf_op jit(solution)/shard_map/scale/pallas_call | solution.py:598
  (2 shorter events, 0.0 us)
Async XLA Ops:
  1.6 8.4 %collective-permute-start = (f32[40,768]{1,0:T(8,128)S(1)}, f32[40,768]{1,0:T(8,128)S(1)}, u32[]{:S(2)}, u32[]{:S(2)}) collective-permute-start(f32[40,768]{1,0:T(8,128)S(1)} %get-tuple-element.47.x_send), channel_id=1, source_target_pairs={{0,2},{2,0},{4,6},{6,4},{8,10},{10,8},{12,14},{14,12},{1,3},{3,1},... | collective-permute-start | bytes 368648 | tf_op jit(solution)/shard_map/ppermute | solution.py:558
  4.8 5.3 %collective-permute-start.1 = (f32[40,768]{1,0:T(8,128)S(1)}, f32[40,768]{1,0:T(8,128)S(1)}, u32[]{:S(2)}, u32[]{:S(2)}) collective-permute-start(f32[40,768]{1,0:T(8,128)S(1)} %get-tuple-element.49), channel_id=1, source_target_pairs={{2,4},{3,5},{4,2},{5,3},{6,8},{7,9},{8,6},{9,7},{10,12},{11,13},{1... | collective-permute-start | bytes 368648 | tf_op jit(solution)/shard_map/ppermute | solution.py:559
  4.8 3.1 %collective-permute-start.4 = (f32[64,128]{1,0:T(8,128)S(1)}, f32[64,128]{1,0:T(8,128)S(1)}, u32[]{:S(2)}, u32[]{:S(2)}) collective-permute-start(f32[64,128]{1,0:T(8,128)S(1)} %get-tuple-element.52), channel_id=1, source_target_pairs={{0,1},{1,0},{2,3},{3,2},{4,5},{5,4},{6,7},{7,6},{8,9},{9,8},{10,11... | collective-permute-start | bytes 98312 | tf_op jit(solution)/shard_map/ppermute | solution.py:560
  5.3 4.7 %collective-permute-start.2 = (f32[8,128]{1,0:T(8,128)S(1)}, f32[8,128]{1,0:T(8,128)S(1)}, u32[]{:S(2)}, u32[]{:S(2)}) collective-permute-start(f32[8,128]{1,0:T(8,128)S(1)} %get-tuple-element.50), channel_id=1, source_target_pairs={{0,3},{1,2},{2,1},{3,0},{4,7},{5,6},{6,5},{7,4},{8,11},{9,10},{10,... | collective-permute-start | bytes 12296 | tf_op jit(solution)/shard_map/ppermute | solution.py:561
  8.0 2.1 %collective-permute-start.3 = (f32[8,128]{1,0:T(8,128)S(1)}, f32[8,128]{1,0:T(8,128)S(1)}, u32[]{:S(2)}, u32[]{:S(2)}) collective-permute-start(f32[8,128]{1,0:T(8,128)S(1)} %get-tuple-element.51), channel_id=1, source_target_pairs={{2,5},{3,4},{4,3},{5,2},{6,9},{7,8},{8,7},{9,6},{10,13},{11,12},{1... | collective-permute-start | bytes 12296 | tf_op jit(solution)/shard_map/ppermute | solution.py:562
  8.0 2.1 %copy-start = (f32[2,16,768]{2,1,0:T(8,128)S(1)}, f32[2,16,768]{2,1,0:T(8,128)}, u32[]{:S(2)}) copy-start(f32[2,16,768]{2,1,0:T(8,128)} %velocity.1) | copy-start | bytes 294916

commit v11 on v10

--- a/solution.py
+++ b/solution.py
@@ -36,8 +36,7 @@
 
 
 def first_pack_kernel(
-    bounds, misfit, visc, friction, ice, grounded, fields, levels, x_send,
-    levels_in, visc_in, friction_in, ice_in, grounded_in, sems,
+    misfit, visc, friction, ice, grounded, fields, x_send, visc_in, friction_in, ice_in, grounded_in, sems
 ):
     copies = [
         pltpu.make_async_copy(source, target, sems.at[n])
@@ -47,7 +46,6 @@
             (ice, ice_in),
             (friction, friction_in),
             (grounded, grounded_in),
-            (bounds, levels_in),
         ))
     ]
     for copy in copies:
@@ -59,11 +57,10 @@
     fields[3] = friction_in[...] * grounded_in[...].astype(F32)
     for n in range(4):
         x_send[8 * n : 8 * n + 8, :] = rim_rows(fields, n, low_half)[0]
-        levels[8 * n : 8 * n + 8, :] = jnp.full((8, LANES), levels_in[n])
     x_send[32:, :] = rim_tail(fields, low_half)[0]
 
 
-def second_pack_kernel(fields, levels, x_send, coefficients, z_send, side_send, x_corner, z_corner):
+def second_pack_kernel(fields, x_send, z_send, side_send, x_corner, z_corner):
     rows, cols = fields.shape[1:]
     left = lax.axis_index("gy") == 0
     position, last_position = lax.axis_index("gx"), lax.axis_size("gx") - 1
@@ -89,8 +86,11 @@
             row = jnp.sum(jnp.where(own_columns_of, columns, 0.0), axis=0, keepdims=True)
             packed = jnp.where(sublanes == q, row, packed)
         target[...] = packed
+
+
+def coefficient_kernel(bounds, coefficients):
     for sweep in range(2):
-        lower, upper = levels[16 * sweep : 16 * sweep + 8, :], levels[16 * sweep + 8 : 16 * sweep + 16, :]
+        lower, upper = jnp.full((8, LANES), bounds[2 * sweep]), jnp.full((8, LANES), bounds[2 * sweep + 1])
         middle = 0.5 * (upper + lower)
         half = 0.5 * (upper - lower)
         ratio = middle / half
@@ -519,37 +519,43 @@
     params = pltpu.CompilerParams(vmem_limit_bytes=32 * 1024 * 1024)
 
     held = pl.BlockSpec(memory_space=pltpu.HBM)
-    inputs = (bounds, misfit, viscosity, friction, ice, grounded)
-    fields, levels, x_send = pl.pallas_call(
+    inputs = (misfit, viscosity, friction, ice, grounded)
+    fields, x_send = pl.pallas_call(
         first_pack_kernel,
-        out_shape=(shaped((4, rows, cols), F32), shaped((32, LANES), F32), shaped((4 * RIM, cols), F32)),
-        in_specs=[held] * 6,
-        out_specs=[whole] * 3,
+        out_shape=(shaped((4, rows, cols), F32), shaped((4 * RIM, cols), F32)),
+        in_specs=[held] * 5,
+        out_specs=[whole] * 2,
         scratch_shapes=[
-            pltpu.SMEM((4,), F32),
             pltpu.VMEM((rows, cols), F32),
             pltpu.VMEM((rows, cols), F32),
             pltpu.VMEM((rows, cols), jnp.int32),
             pltpu.VMEM((rows, cols), jnp.int32),
-            pltpu.SemaphoreType.DMA((6,)),
+            pltpu.SemaphoreType.DMA((5,)),
         ],
         compiler_params=params,
         name="first_pack",
     )(*(pltpu.with_memory_space_constraint(x, pltpu.HBM) for x in inputs))
-    coefficients, z_send, side_send, x_corner, z_corner = pl.pallas_call(
+    z_send, side_send, x_corner, z_corner = pl.pallas_call(
         second_pack_kernel,
         out_shape=(
-            shaped((16 * (2 * DEG - 1), LANES), F32),
             shaped((4 * RIM, cols), F32),
             shaped((4 * rows, LANES), F32),
             shaped((8, LANES), F32),
             shaped((8, LANES), F32),
         ),
-        in_specs=[whole] * 3,
-        out_specs=[whole] * 5,
+        in_specs=[whole] * 2,
+        out_specs=[whole] * 4,
         compiler_params=params,
         name="second_pack",
-    )(fields, levels, x_send)
+    )(fields, x_send)
+    coefficients = pl.pallas_call(
+        coefficient_kernel,
+        out_shape=shaped((16 * (2 * DEG - 1), LANES), F32),
+        in_specs=[pl.BlockSpec(memory_space=pltpu.SMEM)],
+        out_specs=whole,
+        compiler_params=params,
+        name="coefficients",
+    )(bounds)
 
     x_pairs = [(i, i ^ 1) for i in range(gx_size)]
     z_pairs = [(2 * i + c, 2 * j + c) for i in range(1, gx_size - 1) for j in (i + 1 if i % 2 else i - 1,) for c in (0, 1)]

time: 24.8 us -> 24.8 us (level)
  waiting for transfers between devices: 1.15 us -> 0.55 us
  Pallas kernels: 4.37 us -> 4.92 us
    ppermute x1, waiting for transfers between devices: 1.14 us -> 0.54 us  [body(): lax.ppermute(x_corner, AXES, [(2 * i + c, 2 * j + 1 - c) for i, j in x_pa...]
    pallas_call x1 -> x2, Pallas kernels: 0.11 us -> 0.68 us  [the longest x1 0.57 us: body(): pl.pallas_call(coefficient_kernel, out_shape=shaped((16 * (2 * DEG - 1),...]
  transfers between devices with their start and end apart: 5 -> 5, of which waited for: 1 -> 1; matrix products, arithmetic and copies ran while one was open for 0% -> 0% of each run, Pallas kernels for 4% -> 6%
where the time goes in v11:
time: 24.8 us; the launch traced here: 24.6 us
  blocking collectives  12.2 us (49%)
  starting transfers between devices  6.22 us (25%)
  Pallas kernels  4.92 us (20%)
  between operations  0.71 us (3%)
  waiting for transfers between devices  0.55 us (2%)
    all_to_all x1, blocking collectives, body(): gathered = lax.all_to_all(sums, AXES, 0, 0, tiled=True)  12.2 us
    ppermute x1, starting transfers between devices, body(): from_x = lax.ppermute(x_send, 'gx', x_pairs)  3 us
    ppermute x1, starting transfers between devices, body(): lax.ppermute(x_corner, AXES, [(2 * i + c, 2 * j + 1 - c) for i, j in x_pa...  2.64 us
    pallas_call x1, Pallas kernels, body(): pl.pallas_call(leg_kernel, out_shape=(pltpu.VMEM((2, rows, cols), F32), p...  1.57 us
    pallas_call x1, Pallas kernels, body(): pl.pallas_call(first_pack_kernel, out_shape=(shaped((4, rows, cols), F32)...  0.99 us
    pallas_call x1, Pallas kernels, body(): pl.pallas_call(middle_kernel, out_shape=[owned] * 5 + [pltpu.VMEM((8, LAN...  0.9 us
    pallas_call x1, Pallas kernels, body(): pl.pallas_call(functools.partial(scale_kernel, nodes), out_shape=(pltpu.H...  0.79 us
    pallas_call x1, Pallas kernels, body(): pl.pallas_call(coefficient_kernel, out_shape=shaped((16 * (2 * DEG - 1),...  0.57 us
  transfers between devices with their start and end apart: 5, of which 1 were waited for; matrix products, arithmetic and copies ran while one was open for 0% of the time, Pallas kernels for 6%

profile of v11, /device:TPU:0, one launch (start us, length us, event | category | flops | bytes accessed | tf_op | source)
XLA Modules:
  0.0 24.6 jit_solution(7895500934122405738)
XLA Ops:
  0.6 1.0 %first_pack.1 = (f32[4,16,768]{2,1,0:T(8,128)S(1)}, f32[40,768]{1,0:T(8,128)S(1)}) custom-call(f32[2,16,768]{2,1,0:T(8,128)} %misfit.1, f32[16,768]{1,0:T(8,128)} %visc.1, f32[16,768]{1,0:T(8,128)} %friction.1, s32[16,768]{1,0:T(8,128)} %ice.1, s32[16,768]{1,0:T(8,128)} %grounded.1), custom_call_target="tpu_custom_call" | custom-call | tf_op jit(solution)/shard_map/first_pack/pallas_call | solution.py:523
  1.6 3.0 %collective-permute-start = (f32[40,768]{1,0:T(8,128)S(1)}, f32[40,768]{1,0:T(8,128)S(1)}, u32[]{:S(2)}, u32[]{:S(2)}) collective-permute-start(f32[40,768]{1,0:T(8,128)S(1)} %get-tuple-element.44.x_send), channel_id=1, source_target_pairs={{0,2},{2,0},{4,6},{6,4},{8,10},{10,8},{12,14},{14,12},{1,3},{3,1},... | collective-permute-start | bytes 368648 | tf_op jit(solution)/shard_map/ppermute | solution.py:564
  4.6 0.1 second_pack.1
  4.7 0.1 collective-permute-start.1
  4.8 0.5 %collective-permute-start.4 = (f32[64,128]{1,0:T(8,128)S(1)}, f32[64,128]{1,0:T(8,128)S(1)}, u32[]{:S(2)}, u32[]{:S(2)}) collective-permute-start(f32[64,128]{1,0:T(8,128)S(1)} %get-tuple-element.48), channel_id=1, source_target_pairs={{0,1},{1,0},{2,3},{3,2},{4,5},{5,4},{6,7},{7,6},{8,9},{9,8},{10,11... | collective-permute-start | bytes 98312 | tf_op jit(solution)/shard_map/ppermute | solution.py:566
  5.3 0.0 copy-start.1
  5.3 2.6 %collective-permute-start.2 = (f32[8,128]{1,0:T(8,128)S(1)}, f32[8,128]{1,0:T(8,128)S(1)}, u32[]{:S(2)}, u32[]{:S(2)}) collective-permute-start(f32[8,128]{1,0:T(8,128)S(1)} %get-tuple-element.46), channel_id=1, source_target_pairs={{0,3},{1,2},{2,1},{3,0},{4,7},{5,6},{6,5},{7,4},{8,11},{9,10},{10,... | collective-permute-start | bytes 12296 | tf_op jit(solution)/shard_map/ppermute | solution.py:567
  8.0 0.0 collective-permute-start.3
  8.0 0.0 copy-done.1
  8.0 0.6 %coefficients.1 = f32[112,128]{1,0:T(8,128)S(1)} custom-call(f32[4]{0:T(128)S(1)} %copy-done.1), custom_call_target="tpu_custom_call" | custom-call | tf_op jit(solution)/shard_map/coefficients/pallas_call | solution.py:551
  8.5 0.0 collective-permute-done.4.side
  8.6 0.0 copy-start
  8.6 0.9 %middle.1 = (f32[128,128]{1,0:T(8,128)S(1)}, f32[128,128]{1,0:T(8,128)S(1)}, f32[128,128]{1,0:T(8,128)S(1)}, f32[128,128]{1,0:T(8,128)S(1)}, f32[128,128]{1,0:T(...) custom-call(f32[112,128]{1,0:T(8,128)S(1)} %coefficients.1, ...), custom_call_target="tpu_custom_call" | custom-call | tf_op jit(solution)/shard_map/middle/pallas_call | solution.py:574
  9.5 0.5 %collective-permute-done.2.side_x = f32[8,128]{1,0:T(8,128)S(1)} collective-permute-done((f32[8,128]{1,0:T(8,128)S(1)}, f32[8,128]{1,0:T(8,128)S(1)}, u32[]{:S(2)}, u32[]{:S(2)}) %collective-permute-start.2) | collective-permute-done | bytes 4128 | tf_op jit(solution)/shard_map/ppermute | solution.py:567
  10.0 0.0 collective-permute-done.3.side_z
  10.0 0.0 collective-permute-done.from_x
  10.0 0.0 collective-permute-done.1.from_z
  10.0 0.0 copy-done
  10.0 1.6 %leg.1 = (f32[2,16,768]{2,1,0:T(8,128)S(1)}, f32[16,768]{1,0:T(8,128)S(1)}, f32[16,256]{1,0:T(8,128)S(1)}) custom-call(f32[112,128]{1,0:T(8,128)S(1)} %coefficients.1, f32[4,16,768]{2,1,0:T(8,128)S(1)} %get-tuple-element.43.fields, f32[2,16,768]{2,1,0:T(8,128)S(1)} %copy-done, f32[40,768]{1,0:T(8,128)S(1)} %collective-permute-done.from_x, ...), custom_call_target="tpu_custom_call" | custom-call | tf_op jit(solution)/shard_map/leg/pallas_call | solution.py:589
  11.6 12.2 %all_to_all.11 = f32[16,1,256]{2,1,0:T(1,128)S(1)} all-to-all(f32[16,1,256]{2,1,0:T(1,128)S(1)} %copy.10), channel_id=1, replica_groups=mesh['grp'=2,'gx'=8,'gy'=2] {'gx','gy'}, dimensions={0} | all-to-all | bytes 32768 | tf_op jit(solution)/shard_map/all_to_all | solution.py:603
  23.8 0.8 %scale.1 = (f32[16,768]{1,0:T(8,128)}, f32[1,1]{1,0:T(1,128)}, f32[2,16,768]{2,1,0:T(8,128)}) custom-call(f32[16,256]{1,0:T(8,128)S(1)} %bitcast.5, f32[16,768]{1,0:T(8,128)S(1)} %get-tuple-element.78.gradient, f32[2,16,768]{2,1,0:T(8,128)S(1)} %get-tuple-element.79.held_multiplier), custom_call_target="tpu_custom_call" | custom-call | tf_op jit(solution)/shard_map/scale/pallas_call | solution.py:604
  (2 shorter events, 0.0 us)
Async XLA Ops:
  1.6 8.4 %collective-permute-start = (f32[40,768]{1,0:T(8,128)S(1)}, f32[40,768]{1,0:T(8,128)S(1)}, u32[]{:S(2)}, u32[]{:S(2)}) collective-permute-start(f32[40,768]{1,0:T(8,128)S(1)} %get-tuple-element.44.x_send), channel_id=1, source_target_pairs={{0,2},{2,0},{4,6},{6,4},{8,10},{10,8},{12,14},{14,12},{1,3},{3,1},... | collective-permute-start | bytes 368648 | tf_op jit(solution)/shard_map/ppermute | solution.py:564
  4.7 5.3 %collective-permute-start.1 = (f32[40,768]{1,0:T(8,128)S(1)}, f32[40,768]{1,0:T(8,128)S(1)}, u32[]{:S(2)}, u32[]{:S(2)}) collective-permute-start(f32[40,768]{1,0:T(8,128)S(1)} %get-tuple-element.45), channel_id=1, source_target_pairs={{2,4},{3,5},{4,2},{5,3},{6,8},{7,9},{8,6},{9,7},{10,12},{11,13},{1... | collective-permute-start | bytes 368648 | tf_op jit(solution)/shard_map/ppermute | solution.py:565
  4.8 3.7 %collective-permute-start.4 = (f32[64,128]{1,0:T(8,128)S(1)}, f32[64,128]{1,0:T(8,128)S(1)}, u32[]{:S(2)}, u32[]{:S(2)}) collective-permute-start(f32[64,128]{1,0:T(8,128)S(1)} %get-tuple-element.48), channel_id=1, source_target_pairs={{0,1},{1,0},{2,3},{3,2},{4,5},{5,4},{6,7},{7,6},{8,9},{9,8},{10,11... | collective-permute-start | bytes 98312 | tf_op jit(solution)/shard_map/ppermute | solution.py:566
  5.3 2.7 %copy-start.1 = (f32[4]{0:T(128)S(1)}, f32[4]{0:T(128)}, u32[]{:S(2)}) copy-start(f32[4]{0:T(128)} %bounds.1) | copy-start | bytes 52
  5.3 4.7 %collective-permute-start.2 = (f32[8,128]{1,0:T(8,128)S(1)}, f32[8,128]{1,0:T(8,128)S(1)}, u32[]{:S(2)}, u32[]{:S(2)}) collective-permute-start(f32[8,128]{1,0:T(8,128)S(1)} %get-tuple-element.46), channel_id=1, source_target_pairs={{0,3},{1,2},{2,1},{3,0},{4,7},{5,6},{6,5},{7,4},{8,11},{9,10},{10,... | collective-permute-start | bytes 12296 | tf_op jit(solution)/shard_map/ppermute | solution.py:567
  8.0 2.0 %collective-permute-start.3 = (f32[8,128]{1,0:T(8,128)S(1)}, f32[8,128]{1,0:T(8,128)S(1)}, u32[]{:S(2)}, u32[]{:S(2)}) collective-permute-start(f32[8,128]{1,0:T(8,128)S(1)} %get-tuple-element.47), channel_id=1, source_target_pairs={{2,5},{3,4},{4,3},{5,2},{6,9},{7,8},{8,7},{9,6},{10,13},{11,12},{1... | collective-permute-start | bytes 12296 | tf_op jit(solution)/shard_map/ppermute | solution.py:568
  8.6 1.5 %copy-start = (f32[2,16,768]{2,1,0:T(8,128)S(1)}, f32[2,16,768]{2,1,0:T(8,128)}, u32[]{:S(2)}) copy-start(f32[2,16,768]{2,1,0:T(8,128)} %velocity.1) | copy-start | bytes 294916

commit v12 on v10

--- a/solution.py
+++ b/solution.py
@@ -53,14 +53,22 @@
     for copy in copies:
         copy.start()
     low_half = lax.axis_index("gx") % 2 == 0
-    for copy in copies:
-        copy.wait()
-    fields[2] = visc_in[...] * ice_in[...].astype(F32)
-    fields[3] = friction_in[...] * grounded_in[...].astype(F32)
     for n in range(4):
+        if n == 0:
+            copies[0].wait()
+        if n == 2:
+            copies[1].wait()
+            copies[2].wait()
+            fields[2] = visc_in[...] * ice_in[...].astype(F32)
+        if n == 3:
+            copies[3].wait()
+            copies[4].wait()
+            fields[3] = friction_in[...] * grounded_in[...].astype(F32)
         x_send[8 * n : 8 * n + 8, :] = rim_rows(fields, n, low_half)[0]
+    x_send[32:, :] = rim_tail(fields, low_half)[0]
+    copies[5].wait()
+    for n in range(4):
         levels[8 * n : 8 * n + 8, :] = jnp.full((8, LANES), levels_in[n])
-    x_send[32:, :] = rim_tail(fields, low_half)[0]
 
 
 def second_pack_kernel(fields, levels, x_send, coefficients, z_send, side_send, x_corner, z_corner):
@@ -359,6 +367,34 @@
     stiffness(visc, cell, 0, RIM, 1)
     stiffness(visc, cell, end - 1, total - 1, 1)
     begin(levels[0], followings[0], f, coefficients, [*range(RIM), *range(end, total)], 1)
+    even = lane_ids() % 2 == 0
+    coarse_rim = (RIM - DEG) // 2
+    half = rows // 4
+    count = half + 2 * coarse_rim
+
+    def plain():
+        return Rows((0, count, take(1)[0], 0))
+
+    def packed(make, ref, margin):
+        first, last = coarse_rim + margin, coarse_rim + 2 * half - margin
+        target = plain()
+        for j in range(count):
+            i, k = j, j + half
+            one = at(Rows((first, last, ref, margin)), i) if first <= i < last else make(i, "even")
+            two = at(Rows((first, last, ref, margin)), k) if first <= k < last else make(k, "odd")
+            put(target, j, jnp.where(even, one, two))
+        return target
+
+    c_visc = packed(lambda i, lanes: restrict(visc, i, lanes, 0.25), coarse_refs[0], 0)
+    c_beta = packed(lambda i, lanes: restrict(beta, i, lanes), coarse_refs[1], 0)
+    masks = [
+        jnp.where(even, above if j < coarse_rim else inside, below if j >= count - coarse_rim else inside)
+        for j in range(count)
+    ]
+    stiff, stiff_before = plain(), plain()
+    stiffness(c_visc, stiff, 0, count - 1, 2)
+    for row in range(count - 1):
+        put(stiff_before, row, to_right(at(stiff, row), 2))
     for step in range(DEG - 1):
         spans = ((step + 1, RIM + step + 1), (end - step - 1, total - step - 1))
         advance(levels, followings, f, beta, cell, coefficients, step, spans, mask_of)
@@ -385,45 +421,7 @@
             value = base + (to_right(base - other, 1) - to_right(other, 2))
         return mask_of(row) * value
 
-    even = lane_ids() % 2 == 0
-    coarse_rim = (RIM - DEG) // 2
-    half = rows // 4
-    count = half + 2 * coarse_rim
-
-    def plain():
-        return Rows((0, count, take(1)[0], 0))
-
-    def packed(make, ref, margin):
-        first, last = coarse_rim + margin, coarse_rim + 2 * half - margin
-        target = plain()
-        for j in range(count):
-            i, k = j, j + half
-            one = at(Rows((first, last, ref, margin)), i) if first <= i < last else make(i, "even")
-            two = at(Rows((first, last, ref, margin)), k) if first <= k < last else make(k, "odd")
-            put(target, j, jnp.where(even, one, two))
-        return target
-
-    c_visc, c_beta, *c_f = (
-        packed(make, ref, margin)
-        for make, ref, margin in zip(
-            (
-                lambda i, lanes: restrict(visc, i, lanes, 0.25),
-                lambda i, lanes: restrict(beta, i, lanes),
-                functools.partial(restrict_residual, 0),
-                functools.partial(restrict_residual, 1),
-            ),
-            coarse_refs,
-            (0, 0, DEG // 2, DEG // 2),
-        )
-    )
-    masks = [
-        jnp.where(even, above if j < coarse_rim else inside, below if j >= count - coarse_rim else inside)
-        for j in range(count)
-    ]
-    stiff, stiff_before = plain(), plain()
-    stiffness(c_visc, stiff, 0, count - 1, 2)
-    for row in range(count - 1):
-        put(stiff_before, row, to_right(at(stiff, row), 2))
+    c_f = [packed(functools.partial(restrict_residual, n), coarse_refs[n + 2], DEG // 2) for n in range(2)]
     table = 8 * (2 * DEG - 1)
 
     def gradients(here):

time: 24.8 us -> 24.8 us (level)
  no operation moved by 1% of the time
where the time goes in v12:
time: 24.8 us; the launch traced here: 24.6 us
  blocking collectives  12.2 us (49%)
  starting transfers between devices  6.22 us (25%)
  Pallas kernels  4.36 us (18%)
  waiting for transfers between devices  1.15 us (5%)
  between operations  0.69 us (3%)
    all_to_all x1, blocking collectives, body(): gathered = lax.all_to_all(sums, AXES, 0, 0, tiled=True)  12.2 us
    ppermute x1, starting transfers between devices, body(): from_x = lax.ppermute(x_send, 'gx', x_pairs)  3 us
    ppermute x1, starting transfers between devices, body(): lax.ppermute(x_corner, AXES, [(2 * i + c, 2 * j + 1 - c) for i, j in x_pa...  2.64 us
    pallas_call x1, Pallas kernels, body(): pl.pallas_call(leg_kernel, out_shape=(pltpu.VMEM((2, rows, cols), F32), p...  1.57 us
    ppermute x1, waiting for transfers between devices, body(): lax.ppermute(x_corner, AXES, [(2 * i + c, 2 * j + 1 - c) for i, j in x_pa...  1.14 us
    pallas_call x1, Pallas kernels, body(): pl.pallas_call(first_pack_kernel, out_shape=(shaped((4, rows, cols), F32)...  1 us
    pallas_call x1, Pallas kernels, body(): pl.pallas_call(middle_kernel, out_shape=[owned] * 5 + [pltpu.VMEM((8, LAN...  0.9 us
    pallas_call x1, Pallas kernels, body(): pl.pallas_call(functools.partial(scale_kernel, nodes), out_shape=(pltpu.H...  0.79 us
  transfers between devices with their start and end apart: 5, of which 1 were waited for; matrix products, arithmetic and copies ran while one was open for 0% of the time, Pallas kernels for 4%

profile of v12, /device:TPU:0, one launch (start us, length us, event | category | flops | bytes accessed | tf_op | source)
XLA Modules:
  0.0 24.6 jit_solution(9402341535675634019)
XLA Ops:
  0.6 1.0 %first_pack.1 = (f32[4,16,768]{2,1,0:T(8,128)S(1)}, f32[32,128]{1,0:T(8,128)S(1)}, f32[40,768]{1,0:T(8,128)S(1)}) custom-call(f32[4]{0:T(128)} %bounds.1, f32[2,16,768]{2,1,0:T(8,128)} %misfit.1, f32[16,768]{1,0:T(8,128)} %visc.1, f32[16,768]{1,0:T(8,128)} %friction.1, s32[16,768]{1,0:T(8,128)} %ice.1, s32[16,768]{1,0:T(8,128)} %grounded.1), custom_call_target="tpu_custom_call" | custom-call | tf_op jit(solution)/shard_map/first_pack/pallas_call | solution.py:521
  1.6 3.0 %collective-permute-start = (f32[40,768]{1,0:T(8,128)S(1)}, f32[40,768]{1,0:T(8,128)S(1)}, u32[]{:S(2)}, u32[]{:S(2)}) collective-permute-start(f32[40,768]{1,0:T(8,128)S(1)} %get-tuple-element.47.x_send), channel_id=1, source_target_pairs={{0,2},{2,0},{4,6},{6,4},{8,10},{10,8},{12,14},{14,12},{1,3},{3,1},... | collective-permute-start | bytes 368648 | tf_op jit(solution)/shard_map/ppermute | solution.py:556
  4.6 0.1 second_pack.1
  4.8 0.1 collective-permute-start.1
  4.8 0.5 %collective-permute-start.4 = (f32[64,128]{1,0:T(8,128)S(1)}, f32[64,128]{1,0:T(8,128)S(1)}, u32[]{:S(2)}, u32[]{:S(2)}) collective-permute-start(f32[64,128]{1,0:T(8,128)S(1)} %get-tuple-element.52), channel_id=1, source_target_pairs={{0,1},{1,0},{2,3},{3,2},{4,5},{5,4},{6,7},{7,6},{8,9},{9,8},{10,11... | collective-permute-start | bytes 98312 | tf_op jit(solution)/shard_map/ppermute | solution.py:558
  5.3 2.6 %collective-permute-start.2 = (f32[8,128]{1,0:T(8,128)S(1)}, f32[8,128]{1,0:T(8,128)S(1)}, u32[]{:S(2)}, u32[]{:S(2)}) collective-permute-start(f32[8,128]{1,0:T(8,128)S(1)} %get-tuple-element.50), channel_id=1, source_target_pairs={{0,3},{1,2},{2,1},{3,0},{4,7},{5,6},{6,5},{7,4},{8,11},{9,10},{10,... | collective-permute-start | bytes 12296 | tf_op jit(solution)/shard_map/ppermute | solution.py:559
  8.0 0.0 collective-permute-start.3
  8.0 0.0 collective-permute-done.4.side
  8.0 0.0 copy-start
  8.0 0.9 %middle.1 = (f32[128,128]{1,0:T(8,128)S(1)}, f32[128,128]{1,0:T(8,128)S(1)}, f32[128,128]{1,0:T(8,128)S(1)}, f32[128,128]{1,0:T(8,128)S(1)}, f32[128,128]{1,0:T(...) custom-call(f32[112,128]{1,0:T(8,128)S(1)} %get-tuple-element.48.coe, ...), custom_call_target="tpu_custom_call" | custom-call | tf_op jit(solution)/shard_map/middle/pallas_call | solution.py:566
  8.9 1.1 %collective-permute-done.2.side_x = f32[8,128]{1,0:T(8,128)S(1)} collective-permute-done((f32[8,128]{1,0:T(8,128)S(1)}, f32[8,128]{1,0:T(8,128)S(1)}, u32[]{:S(2)}, u32[]{:S(2)}) %collective-permute-start.2) | collective-permute-done | bytes 4128 | tf_op jit(solution)/shard_map/ppermute | solution.py:559
  10.0 0.0 collective-permute-done.3.side_z
  10.0 0.0 collective-permute-done.from_x
  10.0 0.0 collective-permute-done.1.from_z
  10.0 0.0 copy-done
  10.0 1.6 %leg.1 = (f32[2,16,768]{2,1,0:T(8,128)S(1)}, f32[16,768]{1,0:T(8,128)S(1)}, f32[16,256]{1,0:T(8,128)S(1)}) custom-call(f32[112,128]{1,0:T(8,128)S(1)} %get-tuple-element.48.coefficients, f32[4,16,768]{2,1,0:T(8,128)S(1)} %get-tuple-element.45.fields, f32[2,16,768]{2,1,0:T(8,128)S(1)} %copy-done, f32[40,768]{1,0:T(8,128)S(1)} %collective-permute-done.from_x, ...), custom_call_target="tpu_custom_call" | custom-call | tf_op jit(solution)/shard_map/leg/pallas_call | solution.py:581
  11.7 12.2 %all_to_all.11 = f32[16,1,256]{2,1,0:T(1,128)S(1)} all-to-all(f32[16,1,256]{2,1,0:T(1,128)S(1)} %copy.10), channel_id=1, replica_groups=mesh['grp'=2,'gx'=8,'gy'=2] {'gx','gy'}, dimensions={0} | all-to-all | bytes 32768 | tf_op jit(solution)/shard_map/all_to_all | solution.py:595
  23.9 0.8 %scale.1 = (f32[16,768]{1,0:T(8,128)}, f32[1,1]{1,0:T(1,128)}, f32[2,16,768]{2,1,0:T(8,128)}) custom-call(f32[16,256]{1,0:T(8,128)S(1)} %bitcast.5, f32[16,768]{1,0:T(8,128)S(1)} %get-tuple-element.82.gradient, f32[2,16,768]{2,1,0:T(8,128)S(1)} %get-tuple-element.83.held_multiplier), custom_call_target="tpu_custom_call" | custom-call | tf_op jit(solution)/shard_map/scale/pallas_call | solution.py:596
  (2 shorter events, 0.0 us)
Async XLA Ops:
  1.6 8.4 %collective-permute-start = (f32[40,768]{1,0:T(8,128)S(1)}, f32[40,768]{1,0:T(8,128)S(1)}, u32[]{:S(2)}, u32[]{:S(2)}) collective-permute-start(f32[40,768]{1,0:T(8,128)S(1)} %get-tuple-element.47.x_send), channel_id=1, source_target_pairs={{0,2},{2,0},{4,6},{6,4},{8,10},{10,8},{12,14},{14,12},{1,3},{3,1},... | collective-permute-start | bytes 368648 | tf_op jit(solution)/shard_map/ppermute | solution.py:556
  4.8 5.3 %collective-permute-start.1 = (f32[40,768]{1,0:T(8,128)S(1)}, f32[40,768]{1,0:T(8,128)S(1)}, u32[]{:S(2)}, u32[]{:S(2)}) collective-permute-start(f32[40,768]{1,0:T(8,128)S(1)} %get-tuple-element.49), channel_id=1, source_target_pairs={{2,4},{3,5},{4,2},{5,3},{6,8},{7,9},{8,6},{9,7},{10,12},{11,13},{1... | collective-permute-start | bytes 368648 | tf_op jit(solution)/shard_map/ppermute | solution.py:557
  4.8 3.1 %collective-permute-start.4 = (f32[64,128]{1,0:T(8,128)S(1)}, f32[64,128]{1,0:T(8,128)S(1)}, u32[]{:S(2)}, u32[]{:S(2)}) collective-permute-start(f32[64,128]{1,0:T(8,128)S(1)} %get-tuple-element.52), channel_id=1, source_target_pairs={{0,1},{1,0},{2,3},{3,2},{4,5},{5,4},{6,7},{7,6},{8,9},{9,8},{10,11... | collective-permute-start | bytes 98312 | tf_op jit(solution)/shard_map/ppermute | solution.py:558
  5.3 4.7 %collective-permute-start.2 = (f32[8,128]{1,0:T(8,128)S(1)}, f32[8,128]{1,0:T(8,128)S(1)}, u32[]{:S(2)}, u32[]{:S(2)}) collective-permute-start(f32[8,128]{1,0:T(8,128)S(1)} %get-tuple-element.50), channel_id=1, source_target_pairs={{0,3},{1,2},{2,1},{3,0},{4,7},{5,6},{6,5},{7,4},{8,11},{9,10},{10,... | collective-permute-start | bytes 12296 | tf_op jit(solution)/shard_map/ppermute | solution.py:559
  8.0 2.1 %collective-permute-start.3 = (f32[8,128]{1,0:T(8,128)S(1)}, f32[8,128]{1,0:T(8,128)S(1)}, u32[]{:S(2)}, u32[]{:S(2)}) collective-permute-start(f32[8,128]{1,0:T(8,128)S(1)} %get-tuple-element.51), channel_id=1, source_target_pairs={{2,5},{3,4},{4,3},{5,2},{6,9},{7,8},{8,7},{9,6},{10,13},{11,12},{1... | collective-permute-start | bytes 12296 | tf_op jit(solution)/shard_map/ppermute | solution.py:560
  8.0 2.1 %copy-start = (f32[2,16,768]{2,1,0:T(8,128)S(1)}, f32[2,16,768]{2,1,0:T(8,128)}, u32[]{:S(2)}) copy-start(f32[2,16,768]{2,1,0:T(8,128)} %velocity.1) | copy-start | bytes 294916
